TPU v7x, 32 devices: a whole 2x2x4 slice. The times are simulated.
32 devices in a mesh: grp: 4 (over y, x), cand: 8 (over z, core).
Axes of the slice: x: 2, y: 2, z: 4, core: 2. Of those that a mesh axis runs over, the one named last changes fastest.
Arguments:
- node_emb: bfloat16 [8, 512, 512], P('cand'), may hold values from -6 to 6
- rel_emb: float32 [900, 512], P('grp'), may hold values from -6 to 6
- w_in: bfloat16 [512, 512], replicated, may hold values from -0.25 to 0.25
- w_self: bfloat16 [512, 512], replicated, may hold values from -1 to 1
- rel_score: float32 [900, 512], replicated, may hold values from -7 to 7
- mirror_blocks: int32 [4, 8, 8, 1], P('grp', 'cand'), may hold values from 0 to 3
- adj_values: bfloat16 [4, 8, 192, 128, 128], P('grp', 'cand'), may hold values from -0.0390625 to 0.0390625
- adj_source: int32 [4, 8, 192], P('grp', 'cand'), may hold values from 0 to 7
- adj_target: int32 [4, 8, 192], P('grp', 'cand'), may hold values from 0 to 3
- adj_relation: int32 [4, 8, 192], P('grp', 'cand'), may hold values from 0 to 224
- live_blocks: int32 [4, 8], P('grp', 'cand'), may hold values from 48 to 192, as said below
- query_head: int32 [1024], replicated, may hold values from 0 to 4095
- query_rel: int32 [1024], replicated, may hold values from 0 to 899
- allowed: int32 [1024, 8], replicated, may hold values from 0 to 31, as said below
- true_tail: int32 [1024], replicated, may hold values from 0 to 4095, as said below
Outputs:
- h_out: bfloat16 [8, 512, 512], P('cand', 'grp')
- loss: float32 [1024], replicated
- grad_h: float32 [8, 512, 512], P('cand', 'grp')
- grad_rel: float32 [900, 512], P('grp')
- grad_w_in: float32 [512, 512], replicated
- grad_w_self: float32 [512, 512], replicated
Inputs may be any that keep to these rules, and one draw needn't show every extreme that they name: `live_blocks`: blocks from this count on are padding; on some device all 192 blocks are live. `allowed`: ids of blocks of 128 concepts; a query may name a block twice. `true_tail`: lies in one of the query's allowed blocks.
All inputs are finite; a program needn't handle non-finite values.
Results may differ from a plain program's by a relative error of at most 0.011.
Values may be sent and summed in bfloat16 or wider, within the bound.
No kernel may reach another device: no remote copies, remote signals or barrier semaphores. Data moves between devices by JAX's collectives and lax.ppermute only.
A program may use at most 128 MiB of HBM per device.

v0:
```python
import math

import jax
import jax.numpy as jnp
from jax import lax
from jax.sharding import PartitionSpec as P

NEG_FILL = -1e30
HIGH = lax.Precision.HIGHEST


def body(
    node_emb,
    rel_emb,
    w_in,
    w_self,
    rel_score,
    mirror_blocks,
    adj_values,
    adj_source,
    adj_target,
    adj_relation,
    live_blocks,
    query_head,
    query_rel,
    allowed,
    true_tail,
):
    cand_count = lax.axis_size("cand")
    grp_count = lax.axis_size("grp")
    grp_index = lax.axis_index("grp")
    cand_index = lax.axis_index("cand")
    nodes = node_emb[0]
    node_rows, feature_dim = nodes.shape
    block_rows = adj_values.shape[-1]
    tile_count = node_rows // block_rows
    share_rows = node_rows // grp_count
    wanted = mirror_blocks[0, 0]
    slot_count = wanted.shape[1]
    mirror_count = cand_count * slot_count
    requested = lax.all_to_all(wanted, "cand", split_axis=0, concat_axis=0, tiled=True)
    everything = lax.all_gather(node_emb, "cand", axis=0, tiled=True)
    everything = everything.reshape(cand_count * tile_count, block_rows, feature_dim)
    owners = jnp.arange(cand_count, dtype=jnp.int32)[:, None] * tile_count
    mirrors = jnp.take(everything, (owners + wanted).reshape(-1), axis=0)
    tile_values = adj_values[0, 0]
    block_count = tile_values.shape[0]
    stride = math.gcd(block_count, 16)
    turns = block_count // stride
    live_mask = (jnp.arange(block_count, dtype=jnp.int32) < live_blocks[0, 0]).astype(jnp.float32)
    packed = (
        tile_values.reshape(turns, stride, block_rows, block_rows),
        adj_source[0, 0].reshape(turns, stride),
        adj_target[0, 0].reshape(turns, stride),
        adj_relation[0, 0].reshape(turns, stride),
        live_mask.reshape(turns, stride),
    )

    def forward_turn(partial_value, inputs_now):
        values_now, source_now, target_now, relation_now, live_now = inputs_now
        composed = (
            jnp.take(mirrors, source_now, axis=0).astype(jnp.float32)
            - jnp.take(rel_emb, relation_now, axis=0)[:, None, :]
        ).astype(jnp.bfloat16)
        messages = jnp.einsum(
            "bij,bjd->bid", values_now, composed, preferred_element_type=jnp.float32
        )
        messages = messages * live_now[:, None, None]
        return (partial_value.at[target_now].add(messages), None)

    partial_value, ignored = lax.scan(
        forward_turn, jnp.zeros((tile_count, block_rows, feature_dim), jnp.float32), packed
    )
    aggregate = lax.psum_scatter(
        partial_value.reshape(node_rows, feature_dim), "grp", scatter_dimension=0, tiled=True
    )
    aggregate_bf = aggregate.astype(jnp.bfloat16)
    own_rows = lax.dynamic_slice_in_dim(nodes, grp_index * share_rows, share_rows, 0)
    pre_act = jnp.dot(aggregate_bf, w_in, preferred_element_type=jnp.float32) + jnp.dot(
        own_rows, w_self, preferred_element_type=jnp.float32
    )
    activated = jnp.tanh(pre_act)
    h_new = activated.astype(jnp.bfloat16)
    first_row = cand_index * node_rows + grp_index * share_rows
    row_ids = first_row + jnp.arange(share_rows, dtype=jnp.int32)
    head_pick = query_head[:, None] == row_ids[None, :]
    head_part = jnp.dot(head_pick.astype(jnp.bfloat16), h_new, preferred_element_type=jnp.float32)
    heads = lax.psum(head_part, ("grp", "cand"))
    queries = heads + jnp.take(rel_score, query_rel, axis=0)
    cand_rows = h_new.astype(jnp.float32)
    scale = feature_dim ** (-0.5)
    cross = jnp.dot(queries, cand_rows.T, precision=HIGH)
    scores = -scale * (
        jnp.sum(queries * queries, axis=1)[:, None]
        + jnp.sum(cand_rows * cand_rows, axis=1)[None, :]
        - 2.0 * cross
    )
    block_ids = first_row // block_rows + jnp.arange(share_rows // block_rows, dtype=jnp.int32)
    block_ok = jnp.any(allowed[:, :, None] == block_ids[None, None, :], axis=1)
    allowed_mask = jnp.repeat(block_ok, block_rows, axis=1)
    tail_pick = true_tail[:, None] == row_ids[None, :]
    truth_part = jnp.sum(jnp.where(tail_pick, scores, 0.0), axis=1)
    local_max = jnp.max(jnp.where(allowed_mask, scores, NEG_FILL), axis=1)
    row_max = lax.pmax(local_max, ("grp", "cand"))
    local_total = jnp.sum(
        jnp.exp(jnp.where(allowed_mask, scores - row_max[:, None], NEG_FILL)), axis=1
    )
    row_total, truth = lax.psum((local_total, truth_part), ("grp", "cand"))
    log_norm = row_max + jnp.log(row_total)
    loss = log_norm - truth
    prob = jnp.exp(jnp.where(allowed_mask, scores - log_norm[:, None], NEG_FILL))
    grad_score = (prob - tail_pick.astype(jnp.float32)) / query_head.shape[0]
    query_part = (
        2.0
        * scale
        * (
            jnp.dot(grad_score, cand_rows, precision=HIGH)
            - queries * jnp.sum(grad_score, axis=1)[:, None]
        )
    )
    query_grad = lax.psum(query_part, ("grp", "cand"))
    cand_grad = (
        2.0
        * scale
        * (
            jnp.dot(grad_score.T, queries, precision=HIGH)
            - cand_rows * jnp.sum(grad_score, axis=0)[:, None]
        )
    )
    row_grad = cand_grad + jnp.dot(head_pick.astype(jnp.float32).T, query_grad, precision=HIGH)
    pre_grad = (row_grad * (1.0 - activated * activated)).astype(jnp.bfloat16)
    grad_w_in, grad_w_self = lax.psum(
        (
            jnp.dot(aggregate_bf.T, pre_grad, preferred_element_type=jnp.float32),
            jnp.dot(own_rows.T, pre_grad, preferred_element_type=jnp.float32),
        ),
        ("grp", "cand"),
    )
    agg_grad = jnp.dot(pre_grad, w_in.T, preferred_element_type=jnp.float32).astype(jnp.bfloat16)
    agg_tiles = lax.all_gather(agg_grad, "grp", axis=0, tiled=True).reshape(
        tile_count, block_rows, feature_dim
    )

    def backward_turn(carry, inputs_now):
        mirror_grad, relation_grad = carry
        values_now, source_now, target_now, relation_now, live_now = inputs_now
        composed_grad = jnp.einsum(
            "bij,bid->bjd",
            values_now,
            jnp.take(agg_tiles, target_now, axis=0),
            preferred_element_type=jnp.float32,
        )
        composed_grad = composed_grad * live_now[:, None, None]
        mirror_grad = mirror_grad.at[source_now].add(composed_grad)
        relation_grad = relation_grad.at[relation_now].add(-jnp.sum(composed_grad, axis=1))
        return ((mirror_grad, relation_grad), None)

    start = (
        jnp.zeros((mirror_count, block_rows, feature_dim), jnp.float32),
        jnp.zeros(rel_emb.shape, jnp.float32),
    )
    (mirror_grad, relation_grad), ignored = lax.scan(backward_turn, start, packed)
    grad_rel = lax.psum(relation_grad, "cand")
    returned = lax.all_to_all(
        mirror_grad.reshape(cand_count, slot_count, block_rows, feature_dim).astype(jnp.bfloat16),
        "cand",
        split_axis=0,
        concat_axis=0,
        tiled=True,
    ).astype(jnp.float32)
    owned = (
        jnp.zeros((tile_count, block_rows, feature_dim), jnp.float32)
        .at[requested.reshape(-1)]
        .add(returned.reshape(mirror_count, block_rows, feature_dim))
    )
    node_grad = lax.psum_scatter(
        owned.reshape(node_rows, feature_dim).astype(jnp.bfloat16),
        "grp",
        scatter_dimension=0,
        tiled=True,
    ).astype(jnp.float32)
    node_grad = node_grad + jnp.dot(pre_grad, w_self.T, preferred_element_type=jnp.float32)
    return (h_new[None], loss, node_grad[None], grad_rel, grad_w_in, grad_w_self)


def solution(mesh):
    return jax.shard_map(
        body,
        mesh=mesh,
        in_specs=(
            P("cand", None, None),
            P("grp", None),
            P(),
            P(),
            P(),
            P("grp", "cand", None, None),
            P("grp", "cand", None, None, None),
            P("grp", "cand", None),
            P("grp", "cand", None),
            P("grp", "cand", None),
            P("grp", "cand"),
            P(),
            P(),
            P(),
            P(),
        ),
        out_specs=(P("cand", "grp", None), P(), P("cand", "grp", None), P("grp", None), P(), P()),
        check_vma=False,
    )
```

profile of v0, /device:TPU:8, one launch (start us, length us, event | category | flops | bytes accessed | tf_op | source)
XLA Modules:
  0.0 1119.7 jit_solution(7515817247613911504)
XLA Ops:
  14.8 41.7 %all-gather.2.cloned.1.call-done = bf16[8,512,512]{2,1,0:T(8,128)(2,1)} async-done(((bf16[1,512,512]{2,1,0:T(8,128)(2,1)}), bf16[8,512,512]{2,1,0:T(8,128)(2,1)}) %all-gather.2.cloned.1.call-update) | async-done | bytes 4194320 | tf_op jit(solution)/shard_map/all_gather | solution.py:42
  60.5 176.3 %while.22 = (s32[]{:T(128)}, f32[4,128,512]{2,1,0:T(8,128)S(1)}, s32[12,16]{1,0:T(8,128)S(1)}, bf16[12,16,128,128]{3,2,1,0:T(8,128)(2,1)}, s32[12,16]{1,0:T(8,12...) while((s32[]{:T(128)}, f32[4,128,512]{2,1,0:T(8,128)S(1)}, ...), condition=%wide.region_2.3_spmd, body=%wide.region_0.0_spmd.sunk | while | flops 274737504 | bytes 23766208 | solution.py:71
  98.4 6.1 scatter_fusion
  142.5 6.1 scatter_fusion
  171.9 6.1 scatter_fusion
  201.3 6.1 scatter_fusion
  216.0 6.1 scatter_fusion
  230.7 6.1 scatter_fusion
  237.9 28.0 %reduce-scatter.3.cloned.1.call-done = f32[128,512]{1,0:T(8,128)} async-done(((f32[512,512]{1,0:T(8,128)}), f32[128,512]{1,0:T(8,128)}) %reduce-scatter.3.cloned.1.call-update) | async-done | bytes 262160 | tf_op jit(solution)/shard_map/reduce_scatter | solution.py:74
  275.5 130.4 %all-reduce.6.cloned.1.call-done = f32[1024,512]{1,0:T(8,128)} async-done(((f32[1024,512]{1,0:T(8,128)}), f32[1024,512]{1,0:T(8,128)}) %all-reduce.6.cloned.1.call-update) | async-done | bytes 2097168 | tf_op jit(solution)/shard_map/psum | solution.py:88
  411.5 39.2 %pmax.7 = f32[1024]{0:T(1024)S(1)} all-reduce(f32[1024]{0:T(1024)S(1)} %get-tuple-element.185), channel_id=1, replica_groups=mesh['grp'=4,'cand'=8] {'grp','cand'}, use_global_device_ids=true, to_apply=%region_9.10 | all-reduce | flops 1024 | bytes 8192 | tf_op jit(solution)/shard_map/pmax | solution.py:104
  450.7 40.1 %psum.50 = f32[1024]{0:T(1024)S(1)} all-reduce(f32[1024]{0:T(1024)S(1)} %exponential_reduce_fusion), channel_id=1, replica_groups=mesh['grp'=4,'cand'=8] {'grp','cand'}, use_global_device_ids=true, to_apply=%region_11.12 | all-reduce | flops 1024 | bytes 8192 | tf_op jit(solution)/shard_map/psum | solution.py:108
  500.7 8.7 copy.26
  512.5 116.4 %all-reduce.8.cloned.1.call-done = f32[1024,512]{1,0:T(8,128)} async-done(((f32[1024,512]{1,0:T(8,128)}), f32[1024,512]{1,0:T(8,128)}) %all-reduce.8.cloned.1.call-update) | async-done | bytes 2097168 | tf_op jit(solution)/shard_map/psum | solution.py:121
  631.7 10.8 all_gather.7
  644.2 201.2 %while.23 = (s32[]{:T(128)}, f32[8,128,512]{2,1,0:T(8,128)}, f32[225,512]{1,0:T(8,128)S(1)}, s32[12,16]{1,0:T(8,128)S(1)}, bf16[12,16,128,128]{2,3,1,0:T(8,128)(...) while((s32[]{:T(128)}, f32[8,128,512]{2,1,0:T(8,128)}, ...), condition=%wide.region_21.22_spmd, body=%wide.region_17.21_spmd.sunk | while | flops 272639232 | bytes 24124384 | solution.py:162
  650.9 9.5 scatter_fusion.1
  667.8 9.3 scatter_fusion.1
  684.6 9.2 scatter_fusion.1
  701.4 9.1 scatter_fusion.1
  718.0 9.2 scatter_fusion.1
  734.8 9.3 scatter_fusion.1
  751.5 9.4 scatter_fusion.1
  768.5 9.2 scatter_fusion.1
  785.2 9.2 scatter_fusion.1
  801.9 9.2 scatter_fusion.1
  818.6 9.3 scatter_fusion.1
  835.4 9.2 scatter_fusion.1
  853.4 22.9 %all-to-all-done.1 = bf16[8,1,128,512]{3,2,1,0:T(8,128)(2,1)S(1)} async-done(((bf16[8,1,128,512]{3,2,1,0:T(8,128)(2,1)}), bf16[8,1,128,512]{3,2,1,0:T(8,128)(2,1)S(1)}, u32[]{:S(2)}, u32[]{:S(2)}) %all-to-all-start.1) | async-done | bytes 1048608 | tf_op jit(solution)/shard_map/all_to_all | solution.py:164
  886.4 41.8 %psum.51 = f32[1024]{0:T(1024)S(1)} all-reduce(f32[1024]{0:T(1024)S(1)} %get-tuple-element.133), channel_id=1, replica_groups=mesh['grp'=4,'cand'=8] {'grp','cand'}, use_global_device_ids=true, to_apply=%region_13.14 | all-reduce | flops 1024 | bytes 8192 | tf_op jit(solution)/shard_map/psum | solution.py:108
  930.6 36.0 %all-reduce.10.cloned.1.call-done = f32[225,512]{1,0:T(8,128)} async-done(((f32[225,512]{1,0:T(8,128)}), f32[225,512]{1,0:T(8,128)}) %all-reduce.10.cloned.1.call-update) | async-done | bytes 460816 | tf_op jit(solution)/shard_map/psum | solution.py:163
  966.6 141.0 %all-reduce.12.cloned.1.call-done = (f32[512,512]{1,0:T(8,128)}, f32[512,512]{1,0:T(8,128)}) async-done(((f32[512,512]{1,0:T(8,128)}, f32[512,512]{1,0:T(8,128)}), (f32[512,512]{1,0:T(8,128)}, f32[512,512]{1,0:T(8,128)})) %all-reduce.12.cloned.1.call-update) | async-done | bytes 2097168 | tf_op jit(solution)/shard_map/psum | solution.py:132
  (320 shorter events, 298.5 us)
Async XLA Ops:
  7.2 263.4 %copy-start = (f32[900,512]{1,0:T(8,128)S(1)}, f32[900,512]{1,0:T(8,128)}, u32[]{:S(2)}) copy-start(f32[900,512]{1,0:T(8,128)} %param.23) | copy-start | bytes 5529604
  7.2 49.2 %all-gather.2.cloned.1.call-start = ((), (), s32[]{:S(2)}) async-start(), calls=%async_computation.4 | async-start | bytes 4718592 | tf_op jit(solution)/shard_map/all_gather | solution.py:42
  7.9 258.0 %reduce-scatter.3.cloned.1.call-start = ((), (), s32[]{:S(2)}) async-start(), calls=%async_computation.5 | async-start | bytes 1310720 | tf_op jit(solution)/shard_map/reduce_scatter | solution.py:74
  59.2 1.3 copy-start.4
  236.9 1.0 copy-start.2
  236.9 30.4 %copy-start.7 = (bf16[512,512]{1,0:T(8,128)(2,1)S(1)}, bf16[512,512]{1,0:T(8,128)(2,1)}, u32[]{:S(2)}) copy-start(bf16[512,512]{1,0:T(8,128)(2,1)} %param.22) | copy-start | bytes 1572868
  236.9 31.7 %copy-start.13 = (s32[1024]{0:T(1024)S(1)}, s32[1024]{0:T(1024)}, u32[]{:S(2)}) copy-start(s32[1024]{0:T(1024)} %param.30) | copy-start | bytes 12292
  237.8 168.0 %all-reduce.6.cloned.1.call-start = ((), (), s32[]{:S(2)}) async-start(), calls=%async_computation.6 | async-start | bytes 4194304 | tf_op jit(solution)/shard_map/psum | solution.py:88
  268.5 240.9 %copy-start.5 = (bf16[128,512]{1,0:T(8,128)(2,1)}, bf16[128,512]{1,0:T(8,128)(2,1)S(1)}, u32[]{:S(2)}) copy-start(bf16[128,512]{1,0:T(8,128)(2,1)S(1)} %get-tuple-element.175) | copy-start | bytes 393220
  268.5 2.0 copy-start.14
  270.4 358.5 %all-reduce.8.cloned.1.call-start = ((), (), s32[]{:S(2)}) async-start(), calls=%async_computation.7 | async-start | bytes 4194304 | tf_op jit(solution)/shard_map/psum | solution.py:121
  270.5 4.9 copy-start.12
  408.7 1.4 copy-start.3
  408.7 82.1 %copy-start.11 = (s32[1024]{0:T(1024)S(1)}, s32[1024]{0:T(1024)}, u32[]{:S(2)}) copy-start(s32[1024]{0:T(1024)} %param.33) | copy-start | bytes 12292
  495.3 0.7 copy-start.15
  496.6 351.7 %all-to-all-start = ((s32[8,1,1]{2,1,0:T(1,128)}), s32[8,1,1]{2,1,0:T(1,128)S(1)}, u32[]{:S(2)}, u32[]{:S(2)}) async-start(s32[8,1,1]{2,1,0:T(1,128)} %copy.28), calls=%async_computation.1 | async-start | bytes 8192 | tf_op jit(solution)/shard_map/all_to_all | solution.py:41
  512.5 118.9 %copy-start.6 = (bf16[512,512]{1,0:T(8,128)(2,1)S(1)}, bf16[512,512]{1,0:T(8,128)(2,1)}, u32[]{:S(2)}) copy-start(bf16[512,512]{1,0:T(8,128)(2,1)} %param.21) | copy-start | bytes 1572868
  845.5 2.9 copy-start.8
  848.3 27.9 %all-to-all-start.1 = ((bf16[8,1,128,512]{3,2,1,0:T(8,128)(2,1)}), bf16[8,1,128,512]{3,2,1,0:T(8,128)(2,1)S(1)}, u32[]{:S(2)}, u32[]{:S(2)}) async-start(bf16[8,1,128,512]{3,2,1,0:T(8,128)(2,1)} %convert_bitcast_fusion), calls=%async_computation.2 | async-start | bytes 2097152 | tf_op jit(solution)/shard_map/all_to_all | solution.py:164
  853.1 75.6 %reduce-scatter.5.cloned.1.call-start = ((), (), s32[]{:S(2)}) async-start(), calls=%async_computation.8 | async-start | bytes 655360 | tf_op jit(solution)/shard_map/reduce_scatter | solution.py:176
  881.3 1.5 copy-start.10
  882.2 84.4 %all-reduce.10.cloned.1.call-start = ((), (), s32[]{:S(2)}) async-start(), calls=%async_computation.9 | async-start | bytes 950272 | tf_op jit(solution)/shard_map/psum | solution.py:163
  882.8 224.8 %all-reduce.12.cloned.1.call-start = ((), (), s32[]{:S(2)}) async-start(), calls=%async_computation.10 | async-start | bytes 4194304 | tf_op jit(solution)/shard_map/psum | solution.py:132
  1107.6 4.2 copy-start.9
  1107.6 5.2 copy-start.1
Sparse Core Ops, SparseCore 0:
  9.6 46.7 all-gather.1
  238.0 27.9 reduce-scatter.2
  272.1 133.6 all-reduce.5
  495.4 133.4 all-reduce.7
  882.3 26.2 reduce-scatter.4
  911.4 55.1 all-reduce.9
  973.7 133.9 all-reduce.11
where the time goes:
time: 1120 us
  waiting for transfers between devices  518 us (46%)
  other arithmetic  216 us (19%)
  blocking collectives  132 us (12%)
  matrix products  131 us (12%)
  local copies, waits for them, and re-layouts  97.7 us (9%)
  between operations  15.1 us (1%)
    psum x1, waiting for transfers between devices, body(): lax.psum((jnp.dot(aggregate_bf.T, pre_grad, preferred_element_type=jnp.fl...  141 us
    psum x1, waiting for transfers between devices, body(): heads = lax.psum(head_part, ('grp', 'cand'))  130 us
    psum x1, waiting for transfers between devices, body(): query_grad = lax.psum(query_part, ('grp', 'cand'))  116 us
    scatter-add x12, other arithmetic, backward_turn(): mirror_grad = mirror_grad.at[source_now].add(composed_grad)  111 us
    psum x2, blocking collectives, body(): row_total, truth = lax.psum((local_total, truth_part), ('grp', 'cand'))  81.8 us
    scatter-add x12, other arithmetic, forward_turn(): return (partial_value.at[target_now].add(messages), None)  73.3 us
    dot_general x12, matrix products, backward_turn(): jnp.einsum('bij,bid->bjd', values_now, jnp.take(agg_tiles, target_now, ax...  55 us
    dot_general x12, matrix products, forward_turn(): jnp.einsum('bij,bjd->bid', values_now, composed, preferred_element_type=j...  54.8 us
  transfers between devices with their start and end apart: 9, of which 7 were waited for; matrix products, arithmetic and copies ran while one was open for 21% of the time, Pallas kernels for 0%

commit v1 on v0

v1 whole, which is shorter than its diff:
```python
import functools

import jax
import jax.numpy as jnp
from jax import lax
from jax.experimental import pallas as pl
from jax.experimental.pallas import tpu as pltpu
from jax.sharding import PartitionSpec as P

NEG_FILL = -1e30
BF = jnp.bfloat16
F32 = jnp.float32
NT = (((1,), (1,)), ((), ()))
TN = (((0,), (0,)), ((), ()))
VMEM_BYTES = 60 * 1024 * 1024


def dot(a, b):
    return jnp.dot(a, b, preferred_element_type=F32)


def dot_nt(a, b, precision=None):
    return lax.dot_general(a, b, NT, precision=precision, preferred_element_type=F32)


def split(x):
    hi = x.astype(BF)
    return hi, (x - hi.astype(F32)).astype(BF)


def params(**kw):
    return pltpu.CompilerParams(vmem_limit_bytes=VMEM_BYTES, **kw)


def fixed(shape):
    return pl.BlockSpec(shape, lambda *a: (0,) * len(shape), pipeline_mode=pl.Buffered(1))


def fold_kernel(
    tiles, per, src, tgt, rel, live, a_ref, anh_ref, anl_ref, at_ref, w_ref, wth_ref, wtl_ref, acc, wacc
):
    step = pl.program_id(0)
    slots, block, rows = at_ref.shape

    @pl.when(step == 0)
    def _():
        acc[...] = jnp.zeros_like(acc)
        wacc[...] = jnp.zeros_like(wacc)

    ones = jnp.ones((8, block), BF)
    sums = dot_nt(ones, a_ref[...].reshape(per * block, block))
    for i in range(per):
        b = step * per + i

        @pl.when(b < live[0])
        def _():
            at = tgt[b] * slots + src[b]
            acc[at] = acc[at] + a_ref[i].astype(F32)
            row = pl.ds(rel[b], 1)
            wacc[tgt[b], row, :] = wacc[tgt[b], row, :] + sums[0:1, i * block : (i + 1) * block]

    @pl.when(step == pl.num_programs(0) - 1)
    def _():
        for t in range(tiles):
            at = slice(t * block, (t + 1) * block)
            for s in range(slots):
                part = acc[t * slots + s]
                hi, lo = split(part)
                anh_ref[at, s * block : (s + 1) * block] = hi
                anl_ref[at, s * block : (s + 1) * block] = lo
                at_ref[s, :, at] = part.T.astype(BF)
            w_ref[:, at] = wacc[t].astype(BF)
            hi, lo = split(wacc[t].T)
            wth_ref[at, :] = hi
            wtl_ref[at, :] = lo


def fold(adj, src, tgt, rel, live, slots, tiles, rel_rows):
    count, block, _ = adj.shape
    per = next(p for p in (16, 8, 4, 2, 1) if count % p == 0)
    rows = tiles * block
    shapes = [
        ((rows, slots * block), BF),
        ((rows, slots * block), BF),
        ((slots, block, rows), BF),
        ((rel_rows, rows), BF),
        ((rows, rel_rows), BF),
        ((rows, rel_rows), BF),
    ]
    return pl.pallas_call(
        functools.partial(fold_kernel, tiles, per),
        grid_spec=pltpu.PrefetchScalarGridSpec(
            num_scalar_prefetch=4,
            grid=(count // per,),
            in_specs=[pl.BlockSpec((per, block, block), lambda i, *a: (i, 0, 0))],
            out_specs=[fixed(s) for s, _ in shapes],
            scratch_shapes=[
                pltpu.VMEM((tiles * slots, block, block), F32),
                pltpu.VMEM((tiles, rel_rows, block), F32),
            ],
        ),
        out_shape=[jax.ShapeDtypeStruct(s, d) for s, d in shapes],
        compiler_params=params(),
        name="fold_adjacency",
    )(src, tgt, rel, live, adj)


def forward_kernel(slots, ids, *refs):
    anh_ref, anl_ref, wth_ref, wtl_ref, rel_ref, out_ref, outb_ref = refs[slots:]
    mirrors = jnp.concatenate([ref[0] for ref in refs[:slots]], axis=0)
    hi, lo = split(rel_ref[...])
    total = dot(anh_ref[...], mirrors) + dot(anl_ref[...], mirrors)
    total = total - (dot(wth_ref[...], hi) + dot(wth_ref[...], lo) + dot(wtl_ref[...], hi))
    out_ref[...] = total
    outb_ref[...] = total.astype(BF)


def forward(ids, nodes, anh, anl, wth, wtl, rel):
    slots = ids.shape[0]
    rows = anh.shape[0]
    _, block, width = nodes.shape
    rest = (anh, anl, wth, wtl, rel)
    return pl.pallas_call(
        functools.partial(forward_kernel, slots),
        grid_spec=pltpu.PrefetchScalarGridSpec(
            num_scalar_prefetch=1,
            grid=(1,),
            in_specs=[
                pl.BlockSpec((1, block, width), lambda i, ids, s=s: (ids[s], 0, 0))
                for s in range(slots)
            ]
            + [fixed(x.shape) for x in rest],
            out_specs=[fixed((rows, width)), fixed((rows, width))],
        ),
        out_shape=[
            jax.ShapeDtypeStruct((rows, width), F32),
            jax.ShapeDtypeStruct((rows, width), BF),
        ],
        compiler_params=params(),
        name="forward_partial",
    )(ids, *[nodes] * slots, *rest)


def activate_kernel(agg_ref, node_ref, win_ref, wself_ref, h_ref, *more):
    act = jnp.tanh(dot(agg_ref[...], win_ref[...]) + dot(node_ref[...], wself_ref[...]))
    h = act.astype(BF)
    h_ref[...] = h
    if more:
        d_ref, ht_ref = more
        d_ref[...] = (1.0 - act * act).astype(BF)
        ht_ref[...] = h.astype(F32).T.astype(BF)


def activate(agg, nodes, w_in, w_self, rows, flipped):
    total, width = agg.shape
    tall = pl.BlockSpec((rows, width), lambda i: (i, 0))
    return pl.pallas_call(
        activate_kernel,
        grid=(total // rows,),
        in_specs=[tall, tall, fixed(w_in.shape), fixed(w_self.shape)],
        out_specs=[tall] + [tall] * flipped + [pl.BlockSpec((width, rows), lambda i: (0, i))] * flipped,
        out_shape=[jax.ShapeDtypeStruct((total, width), BF)] * (1 + flipped)
        + [jax.ShapeDtypeStruct((width, total), BF)] * flipped,
        compiler_params=params(),
        name="activate",
    )(agg, nodes, w_in, w_self)


def score_kernel(block, total_q, flipped, h_ref, *refs):
    ht_ref = refs[0] if flipped else None
    q_ref, meta_ref, gs_ref, qg_ref, qb_ref, loss_ref, s_ref, hsq_ref = refs[flipped:]
    total, width = h_ref.shape
    qt = q_ref.shape[0]
    blocks = total // block
    scale = width ** (-0.5)

    def rows_of(b):
        return pl.ds(pl.multiple_of(b * block, block), block)

    @pl.when(pl.program_id(0) == 0)
    def _():
        def square(b, carry):
            x = h_ref[rows_of(b), :].astype(F32)
            norm = scale * jnp.sum(x * x, axis=1, keepdims=True)
            hsq_ref[rows_of(b), :] = jnp.broadcast_to(norm, (block, 128))
            return carry

        lax.fori_loop(0, blocks, square, 0)

    q = q_ref[...]
    qb_ref[...] = q.astype(BF)
    hi, lo = split(q * (2.0 * scale))
    qsq = scale * dot_nt(jnp.ones((8, width), F32), q * q, precision=lax.Precision.HIGHEST)[0:1]
    allowed = meta_ref[:-8, :]
    tail = meta_ref[meta_ref.shape[0] - 8 : meta_ref.shape[0] - 7, :]

    def first(b, top):
        hb = h_ref[rows_of(b), :]
        cross = dot_nt(hb, hi) + dot_nt(hb, lo)
        ok = jnp.max((allowed == b).astype(jnp.int32), axis=0, keepdims=True) > 0
        bias = jnp.where(ok, 0.0, NEG_FILL) - qsq
        hsq = jnp.concatenate([hsq_ref[rows_of(b), :]] * (qt // 128), axis=1)
        s = cross - hsq + bias
        s_ref[rows_of(b), :] = s
        return jnp.maximum(top, jnp.max(s.reshape(block // 8, 8, qt), axis=0))

    top = lax.fori_loop(0, blocks, first, jnp.full((8, qt), 2.0 * NEG_FILL, F32), unroll=4)
    top = jnp.max(top, axis=0, keepdims=True)
    row = lax.broadcasted_iota(jnp.int32, (block, qt), 0)

    def second(b, carry):
        norm, truth = carry
        s = s_ref[rows_of(b), :]
        e = jnp.exp(s - top)
        s_ref[rows_of(b), :] = e
        at_tail = jnp.where(row == tail - b * block, s, 0.0)
        norm = norm + jnp.sum(e.reshape(block // 8, 8, qt), axis=0)
        truth = truth + jnp.sum(at_tail.reshape(block // 8, 8, qt), axis=0)
        return norm, truth

    zero = jnp.zeros((8, qt), F32)
    norm, truth = lax.fori_loop(0, blocks, second, (zero, zero))
    norm = jnp.sum(norm, axis=0, keepdims=True)
    truth = jnp.sum(truth, axis=0, keepdims=True)
    loss_ref[...] = top + jnp.log(norm) - truth
    inverse = 1.0 / norm

    def third(b, carry):
        e = s_ref[rows_of(b), :]
        picked = jnp.where(row == tail - b * block, 1.0, 0.0)
        gs_ref[rows_of(b), :] = ((e * inverse - picked) * (1.0 / total_q)).astype(BF)
        return carry

    lax.fori_loop(0, blocks, third, 0)
    if flipped:
        pulled = dot(ht_ref[...], gs_ref[...]).T
    else:
        pulled = lax.dot_general(gs_ref[...], h_ref[...], TN, preferred_element_type=F32)
    rowsum = (norm * inverse - 1.0) * (1.0 / total_q)
    rowsum = jnp.broadcast_to(rowsum, (128, qt)).T[:, 0:1]
    qg_ref[...] = (2.0 * scale * (pulled - q * rowsum)).astype(BF)


def score(h, ht, q, meta, block, qt):
    flipped = len(ht)
    total, width = h.shape
    total_q = q.shape[0]
    return pl.pallas_call(
        functools.partial(score_kernel, block, total_q, flipped),
        grid=(total_q // qt,),
        in_specs=[
            fixed(h.shape),
            *[fixed(x.shape) for x in ht],
            pl.BlockSpec((qt, width), lambda i: (i, 0)),
            pl.BlockSpec((meta.shape[0], qt), lambda i: (0, i)),
        ],
        out_specs=[
            pl.BlockSpec((total, qt), lambda i: (0, i)),
            pl.BlockSpec((qt, width), lambda i: (i, 0)),
            pl.BlockSpec((qt, width), lambda i: (i, 0)),
            pl.BlockSpec((1, qt), lambda i: (0, i)),
        ],
        out_shape=[
            jax.ShapeDtypeStruct((total, total_q), BF),
            jax.ShapeDtypeStruct((total_q, width), BF),
            jax.ShapeDtypeStruct((total_q, width), BF),
            jax.ShapeDtypeStruct((1, total_q), F32),
        ],
        scratch_shapes=[pltpu.VMEM((total, qt), F32), pltpu.VMEM((total, 128), F32)],
        compiler_params=params(),
        name="score",
    )(h, *ht, q, meta)


def backward_kernel(
    tiles,
    slot_count,
    recompute,
    pos,
    gs_ref,
    qb_ref,
    qg_ref,
    head_ref,
    h_ref,
    d_ref,
    agg_ref,
    node_ref,
    win_ref,
    wself_ref,
    at_ref,
    w_ref,
    pre_ref,
    owned_ref,
    grel_ref,
    gwin_ref,
    gwself_ref,
):
    c = pl.program_id(0)
    count = pl.num_programs(0)
    rows, width = h_ref.shape
    total_q = qb_ref.shape[0]
    block = rows // tiles
    scale = width ** (-0.5)

    @pl.when(c == 0)
    def _():
        owned_ref[...] = jnp.zeros_like(owned_ref)
        grel_ref[...] = jnp.zeros_like(grel_ref)
        gwin_ref[...] = jnp.zeros_like(gwin_ref)
        gwself_ref[...] = jnp.zeros_like(gwself_ref)

    gs = gs_ref[...]
    colsum = dot(gs, jnp.ones((total_q, 128), BF))
    colsum = jnp.concatenate([colsum] * (width // 128), axis=1)
    row = lax.broadcasted_iota(jnp.int32, (rows, total_q), 0) + c * rows
    picked = jnp.where(row == head_ref[0:1, :], 1.0, 0.0).astype(BF)
    grad = 2.0 * scale * (dot(gs, qb_ref[...]) - h_ref[...].astype(F32) * colsum)
    grad = grad + dot(picked, qg_ref[...])
    if recompute:
        act = jnp.tanh(dot(agg_ref[...], win_ref[...]) + dot(node_ref[...], wself_ref[...]))
        slope = 1.0 - act * act
    else:
        slope = d_ref[...].astype(F32)
    pre = (grad * slope).astype(BF)

    @pl.when(c == pos[count])
    def _():
        pre_ref[...] = pre

    agg_grad = dot_nt(pre, win_ref[...]).astype(BF)
    for s in range(slot_count):
        back = dot(at_ref[0, s, 0:block, :], agg_grad)
        which = at_ref[0, s, block : block + 16, :].astype(F32)[0:1, :]
        for t in range(tiles):
            owned_ref[t] = owned_ref[t] + jnp.where(which == t, back, 0.0)
    grel_ref[...] = grel_ref[...] - dot(w_ref[0], agg_grad)
    gwin_ref[...] += lax.dot_general(agg_ref[...], pre, TN, preferred_element_type=F32)
    gwself_ref[...] += lax.dot_general(node_ref[...], pre, TN, preferred_element_type=F32)


def backward(pos, gs, qb, qg, head, h, d, agg, nodes, w_in, w_self, at, w, tiles, recompute):
    total, width = h.shape
    count, slot_count, at_rows, rows = at.shape
    rel_rows = w.shape[1]
    total_q = qb.shape[0]
    block = rows // tiles
    tall = pl.BlockSpec((rows, width), lambda i, pos: (i, 0))
    return pl.pallas_call(
        functools.partial(backward_kernel, tiles, slot_count, recompute),
        grid_spec=pltpu.PrefetchScalarGridSpec(
            num_scalar_prefetch=1,
            grid=(count,),
            in_specs=[
                pl.BlockSpec((rows, total_q), lambda i, pos: (i, 0)),
                fixed(qb.shape),
                fixed(qg.shape),
                fixed(head.shape),
                tall,
                tall,
                tall,
                tall,
                fixed(w_in.shape),
                fixed(w_self.shape),
                pl.BlockSpec((1, slot_count, at_rows, rows), lambda i, pos: (pos[i], 0, 0, 0)),
                pl.BlockSpec((1, rel_rows, rows), lambda i, pos: (i, 0, 0)),
            ],
            out_specs=[
                fixed((rows, width)),
                fixed((tiles, block, width)),
                fixed((rel_rows, width)),
                fixed((width, width)),
                fixed((width, width)),
            ],
        ),
        out_shape=[
            jax.ShapeDtypeStruct((rows, width), BF),
            jax.ShapeDtypeStruct((tiles, block, width), F32),
            jax.ShapeDtypeStruct((rel_rows, width), F32),
            jax.ShapeDtypeStruct((width, width), F32),
            jax.ShapeDtypeStruct((width, width), F32),
        ],
        compiler_params=params(),
        name="backward",
    )(pos, gs, qb, qg, head, h, d, agg, nodes, w_in, w_self, at, w)


def sum_over_grp(whole, whole_bf, grp_index, grp_count, share_rows):
    total = lax.dynamic_slice_in_dim(whole, grp_index * share_rows, share_rows, 0)
    for k in range(1, grp_count):
        part = lax.dynamic_slice_in_dim(whole_bf, (grp_index ^ k) * share_rows, share_rows, 0)
        got = lax.ppermute(part, "grp", [(i, i ^ k) for i in range(grp_count)])
        total = total + got.astype(F32)
    return total


def body(
    node_emb,
    rel_emb,
    w_in,
    w_self,
    rel_score,
    mirror_blocks,
    adj_values,
    adj_source,
    adj_target,
    adj_relation,
    live_blocks,
    query_head,
    query_rel,
    allowed,
    true_tail,
):
    cand_count = lax.axis_size("cand")
    grp_count = lax.axis_size("grp")
    grp_index = lax.axis_index("grp")
    cand_index = lax.axis_index("cand")
    nodes = node_emb[0]
    node_rows, width = nodes.shape
    block = adj_values.shape[-1]
    tiles = node_rows // block
    share_rows = node_rows // grp_count
    wanted = mirror_blocks[0, 0]
    slot_count = wanted.shape[1]
    slots = cand_count * slot_count
    total = cand_count * node_rows
    total_q = query_head.shape[0]
    rel_rows = -(-rel_emb.shape[0] // 128) * 128

    all_nodes = lax.all_gather(nodes, "cand", axis=0, tiled=True)
    anh, anl, at, w, wth, wtl = fold(
        adj_values[0, 0],
        adj_source[0, 0],
        adj_target[0, 0],
        adj_relation[0, 0],
        live_blocks[0],
        slots,
        tiles,
        rel_rows,
    )
    owners = jnp.arange(cand_count, dtype=jnp.int32)[:, None] * tiles
    rel_pad = jnp.pad(rel_emb, ((0, rel_rows - rel_emb.shape[0]), (0, 0)))
    partial, partial_bf = forward(
        (owners + wanted).reshape(-1),
        all_nodes.reshape(cand_count * tiles, block, width),
        anh,
        anl,
        wth,
        wtl,
        rel_pad,
    )
    own_agg = sum_over_grp(partial, partial_bf, grp_index, grp_count, share_rows).astype(BF)
    all_agg = lax.all_gather(own_agg, ("cand", "grp"), axis=0, tiled=True)
    rel_rows_q = jnp.take(rel_score, query_rel, axis=0)

    marks = jnp.broadcast_to(
        wanted.astype(BF).reshape(cand_count, slot_count, 1, 1),
        (cand_count, slot_count, 16, node_rows),
    )
    at = jnp.concatenate([at.reshape(cand_count, slot_count, block, node_rows), marks], axis=2)
    all_agg, at, w = lax.optimization_barrier((all_agg, at, w))
    pieces = [lax.dynamic_index_in_dim(at, cand_index, 0, keepdims=True)]
    for k in range(1, cand_count):
        piece = lax.dynamic_index_in_dim(at, (cand_index + k) % cand_count, 0, keepdims=True)
        shift = [(i, (i + k) % cand_count) for i in range(cand_count)]
        pieces.append(lax.ppermute(piece, "cand", shift))
    at_mine = jnp.concatenate(pieces, axis=0)
    pos = (cand_index - jnp.arange(cand_count, dtype=jnp.int32)) % cand_count
    pos = jnp.concatenate([pos, cand_index.astype(jnp.int32)[None]])
    w_all = lax.all_gather(w[None], "cand", axis=0, tiled=True)

    small = total <= 4096
    h, *more = activate(all_agg, all_nodes, w_in, w_self, node_rows, int(small))
    d, ht = (more[0], more[1:]) if small else (h, [])
    queries = jnp.take(h, query_head, axis=0).astype(F32) + rel_rows_q
    meta = jnp.concatenate(
        [
            allowed.T,
            jnp.broadcast_to(true_tail[None, :], (8, total_q)),
        ],
        axis=0,
    )
    qt = 256 if small else 128
    gs, qg, qb, loss = score(h, ht, queries, meta, block, qt)
    head = jnp.broadcast_to(query_head[None, :], (8, total_q))
    pre, owned, grel, gwin, gwself = backward(
        pos,
        gs,
        qb,
        qg,
        head,
        h,
        d,
        all_agg,
        all_nodes,
        w_in,
        w_self,
        at_mine,
        w_all,
        tiles,
        not small,
    )
    owned = owned.reshape(node_rows, width)
    node_grad = sum_over_grp(owned, owned.astype(BF), grp_index, grp_count, share_rows)
    first_row = cand_index * node_rows + grp_index * share_rows
    own_pre = lax.dynamic_slice_in_dim(pre, grp_index * share_rows, share_rows, 0)
    node_grad = node_grad + lax.dot_general(own_pre, w_self, NT, preferred_element_type=F32)
    h_own = lax.dynamic_slice_in_dim(h, first_row, share_rows, 0)
    return (
        h_own[None],
        loss[0],
        node_grad[None],
        grel[: rel_emb.shape[0]],
        gwin,
        gwself,
    )


def solution(mesh):
    return jax.shard_map(
        body,
        mesh=mesh,
        in_specs=(
            P("cand", None, None),
            P("grp", None),
            P(),
            P(),
            P(),
            P("grp", "cand", None, None),
            P("grp", "cand", None, None, None),
            P("grp", "cand", None),
            P("grp", "cand", None),
            P("grp", "cand", None),
            P("grp", "cand"),
            P(),
            P(),
            P(),
            P(),
        ),
        out_specs=(P("cand", "grp", None), P(), P("cand", "grp", None), P("grp", None), P(), P()),
        check_vma=False,
    )
```

time: 1120 us -> 285 us (0.25)
  waiting for transfers between devices: 518 us -> 108 us
  other arithmetic: 216 us -> 9.17 us
  blocking collectives: 132 us -> 0 us
  matrix products: 131 us -> 2.1 us
  Pallas kernels: 0 us -> 115 us
  local copies, waits for them, and re-layouts: 97.7 us -> 19 us
    psum x4 -> x0, waiting for transfers between devices: 424 us -> none  [the longest x1 141 us: body(): lax.psum((jnp.dot(aggregate_bf.T, pre_grad, preferred_element_type=jnp.fl...]
    scatter-add x37 -> x0, other arithmetic: 198 us -> none  [the longest x12 111 us: backward_turn(): mirror_grad = mirror_grad.at[source_now].add(composed_grad)]
    dot_general x35 -> x1, matrix products: 131 us -> 2.1 us  [body(): lax.dot_general(own_pre, w_self, NT, preferred_element_type=F32)]
    pallas_call x0 -> x5, Pallas kernels: none -> 115 us  [the longest x1 50.5 us: score(): pl.pallas_call(functools.partial(score_kernel, block, total_q, flipped),...]
    psum x2 -> x0, blocking collectives: 81.8 us -> none  [body(): row_total, truth = lax.psum((local_total, truth_part), ('grp', 'cand'))]
    gather x38 -> x2, local copies, waits for them, and re-layouts: 77.2 us -> 11.7 us  [the longest x1 6.73 us: body(): queries = jnp.take(h, query_head, axis=0).astype(F32) + rel_rows_q]
    all_gather x1 -> x3, waiting for transfers between devices: 41.7 us -> 92.6 us  [the longest x1 60.2 us: body(): all_agg = lax.all_gather(own_agg, ('cand', 'grp'), axis=0, tiled=True)]
    pmax x1 -> x0, blocking collectives: 39.2 us -> none  [body(): row_max = lax.pmax(local_max, ('grp', 'cand'))]
  transfers between devices with their start and end apart: 9 -> 16, of which waited for: 7 -> 7; matrix products, arithmetic and copies ran while one was open for 21% -> 8% of each run, Pallas kernels for 0% -> 27%
where the time goes in v1:
time: 285 us; the launch traced here: 283 us
  Pallas kernels  115 us (40%)
  waiting for transfers between devices  108 us (38%)
  local copies, waits for them, and re-layouts  19 us (7%)
  between operations  14.8 us (5%)
  starting transfers between devices  14.6 us (5%)
  other arithmetic  9.17 us (3%)
    all_gather x1, waiting for transfers between devices, body(): all_agg = lax.all_gather(own_agg, ('cand', 'grp'), axis=0, tiled=True)  60.2 us
    pallas_call x1, Pallas kernels, score(): pl.pallas_call(functools.partial(score_kernel, block, total_q, flipped),...  50.5 us
    pallas_call x1, Pallas kernels, backward(): pl.pallas_call(functools.partial(backward_kernel, tiles, slot_count, reco...  33.4 us
    all_gather x1, waiting for transfers between devices, body(): all_nodes = lax.all_gather(nodes, 'cand', axis=0, tiled=True)  32.4 us
    pallas_call x1, Pallas kernels, fold(): pl.pallas_call(functools.partial(fold_kernel, tiles, per), grid_spec=pltp...  13 us
    pallas_call x1, Pallas kernels, activate(): pl.pallas_call(activate_kernel, grid=(total // rows,), in_specs=[tall, ta...  12.3 us
    ppermute x6, waiting for transfers between devices, sum_over_grp(): got = lax.ppermute(part, 'grp', [(i, i ^ k) for i in range(grp_count)])  10.7 us
    ppermute x7, starting transfers between devices, body(): pieces.append(lax.ppermute(piece, 'cand', shift))  7.36 us
  transfers between devices with their start and end apart: 16, of which 7 were waited for; matrix products, arithmetic and copies ran while one was open for 8% of the time, Pallas kernels for 27%

profile of v1, /device:TPU:8, one launch (start us, length us, event | category | flops | bytes accessed | tf_op | source)
XLA Modules:
  0.0 282.9 jit_solution(5008476249987161439)
XLA Ops:
  8.6 1.9 pad.4.refs_12_
  10.5 13.0 %fold_adjacency.1 = (bf16[512,1024]{1,0:T(8,128)(2,1)}, bf16[512,1024]{1,0:T(8,128)(2,1)}, bf16[8,128,512]{2,1,0:T(8,128)(2,1)}, bf16[256,512]{1,0:T(8,128)(2,1)...) custom-call(s32[192]{0:T(256)} %bitcast.38, s32[192]{0:T(256)} %bitcast.39, s32[192]{0:T(256)} %bitcast.40, ...), custom_call_target="tpu_custom_call" | custom-call | tf_op jit(solution)/shard_map/fold_adjacency/pallas_call | solution.py:90
  24.1 32.4 %all-gather.8.cloned.1.call-done = bf16[1,4096,512]{2,1,0:T(8,128)(2,1)} async-done(((bf16[1,512,512]{2,1,0:T(8,128)(2,1)}), bf16[1,4096,512]{2,1,0:T(8,128)(2,1)}) %all-gather.8.cloned.1.call-update) | async-done | bytes 4194320 | tf_op jit(solution)/shard_map/all_gather | solution.py:429
  56.4 5.8 %forward_partial.1 = (f32[512,512]{1,0:T(8,128)}, bf16[512,512]{1,0:T(8,128)(2,1)}) custom-call(s32[8]{0:T(128)} %bitcast_add_fusion.ids, bf16[32,128,512]{2,1,0:T(8,128)(2,1)} %bitcast.23, bf16[32,128,512]{2,1,0:T(8,128)(2,1)} %bitcast.24, bf16[32,128,512]{2,1,0:T(8,128)(2,1)} %bitcast.25, bf16[32,128,512]{2,1,0:T(8,128)(2,1)} %bitcast.26, ...), custom_call_target="tpu_custom_call" | custom-call | tf_op jit(solution)/shard_map/forward_partial/pallas_call | solution.py:123
  62.2 1.1 constant_dynamic-slice_fusion.12
  63.3 1.5 collective-permute-start
  64.8 1.5 collective-permute-start.1
  66.8 2.5 collective-permute-done
  69.3 3.6 %collective-permute-done.1 = bf16[128,512]{1,0:T(8,128)(2,1)S(1)} collective-permute-done((bf16[128,512]{1,0:T(8,128)(2,1)S(1)}, bf16[128,512]{1,0:T(8,128)(2,1)S(1)}, u32[]{:S(2)}, u32[]{:S(2)}) %collective-permute-start.1) | collective-permute-done | bytes 131104 | tf_op jit(solution)/shard_map/ppermute | solution.py:391
  73.0 1.7 add_convert_fusion
  74.8 1.3 pad_maximum_fusion
  76.2 60.2 %all-gather.6.cloned.1.call-done.agg_ref = bf16[4096,512]{1,0:T(8,128)(2,1)} async-done(((bf16[128,512]{1,0:T(8,128)(2,1)}), bf16[4096,512]{1,0:T(8,128)(2,1)}) %all-gather.6.cloned.1.call-update) | async-done | bytes 4194320 | tf_op jit(solution)/shard_map/all_gather | solution.py:452
  136.6 4.9 %gather_fusion.1 = f32[1024,512]{1,0:T(8,128)} fusion(f32[900,512]{1,0:T(8,128)S(1)} %copy-done, s32[1024]{0:T(1024)S(1)} %get-tuple-element.69), kind=kCustom, calls=%fused_computation.1 | custom fusion | bytes 4198400 | tf_op jit(solution)/shard_map/jit(_take)/gather | solution.py:453
  142.8 0.8 constant_dynamic-slice_fusion.3
  143.9 0.8 collective-permute-start.4
  144.6 2.0 collective-permute-start.5
  146.6 1.6 collective-permute-start.6
  148.2 1.0 collective-permute-start.7
  149.2 12.3 %activate.1 = (bf16[4096,512]{1,0:T(8,128)(2,1)}, bf16[4096,512]{1,0:T(8,128)(2,1)}, bf16[512,4096]{1,0:T(8,128)(2,1)}) custom-call(bf16[4096,512]{1,0:T(8,128)(2,1)} %all-gather.6.cloned.1.call-done.agg_ref, bf16[4096,512]{1,0:T(8,128)(2,1)} %bitcast.31, bf16[512,512]{1,0:T(8,128)(2,1)} %win_ref.3, bf16[512,512]{1,0:T(8,128)(2,1)} %wself_ref.3), custom_call_target="tpu_custom_call" | custom-call | tf_op jit(solution)/shard_map/activate/pallas_call | solution.py:157
  161.5 6.7 %gather_fusion = bf16[1024,512]{1,0:T(8,128)(2,1)S(1)} fusion(bf16[4096,512]{1,0:T(8,128)(2,1)} %get-tuple-element.38.h_ref, s32[1024]{0:T(1024)S(1)} %get-tuple-element.68), kind=kCustom, calls=%fused_computation | custom fusion | bytes 2101248 | tf_op jit(solution)/shard_map/jit(_take)/gather | solution.py:474
  168.3 3.0 %select_add_fusion.refs_1_ = f32[1024,512]{1,0:T(8,128)} fusion(f32[1024,512]{1,0:T(8,128)} %gather_fusion.1, bf16[1024,512]{1,0:T(8,128)(2,1)S(1)} %gather_fusion, pred[1024]{0:T(1024)(128)(4,1)S(1)} %get-tuple-element.66, pred[1024]{0:T(1024)(128)(4,1)S(1)} %get-tuple-element.67), kind=kLoop, calls=%fused_computation.2 | loop fusion | flops 2097152 | bytes 5244928 | tf_op jit(solution)/shard_map/add | solution.py:474
  171.3 50.5 %score.1 = (bf16[4096,1024]{1,0:T(8,128)(2,1)}, bf16[1024,512]{1,0:T(8,128)(2,1)}, bf16[1024,512]{1,0:T(8,128)(2,1)}, f32[1,1024]{1,0:T(1,128)}) custom-call(bf16[4096,512]{1,0:T(8,128)(2,1)} %get-tuple-element.38.h_ref, bf16[512,4096]{1,0:T(8,128)(2,1)} %get-tuple-element.39.refs_0_, f32[1024,512]{1,0:T(8,128)} %select_add_fusion.refs_1_, ...), custom_call_target="tpu_custom_call" | custom-call | tf_op jit(solution)/shard_map/score/pallas_call | solution.py:248
  222.2 1.4 collective-permute-start.9
  223.7 4.3 %collective-permute-done.8 = bf16[1,1,144,512]{3,2,1,0:T(8,128)(2,1)S(1)} collective-permute-done((bf16[1,1,144,512]{3,2,1,0:T(8,128)(2,1)S(1)}, bf16[1,1,144,512]{3,2,1,0:T(8,128)(2,1)S(1)}, u32[]{:S(2)}, u32[]{:S(2)}) %collective-permute-start.8) | collective-permute-done | bytes 147488 | tf_op jit(solution)/shard_map/ppermute | solution.py:465
  229.1 33.4 %backward.1 = (bf16[512,512]{1,0:T(8,128)(2,1)}, f32[4,128,512]{2,1,0:T(8,128)}, f32[256,512]{1,0:T(8,128)}, f32[512,512]{1,0:T(8,128)}, f32[512,512]{1,0:T(8,128)}) custom-call(s32[9]{0:T(128)} %pad_add_fusion.1.pos, bf16[4096,1024]{1,0:T(8,128)(2,1)} %get-tuple-element.41.gs_ref, bf16[1024,512]{1,0:T(8,128)(2,1)} %get-tuple-element.42.qb_ref, ...), custom_call_target="tpu_custom_call" | custom-call | tf_op jit(solution)/shard_map/backward/pallas_call | solution.py:348
  262.4 1.3 bitcast_convert_fusion.1
  263.8 1.4 collective-permute-start.10
  265.9 1.4 collective-permute-start.12
  267.4 1.6 dynamic-slice_bitcast_fusion
  269.0 0.8 slice.3
  270.0 4.3 %collective-permute-done.11 = bf16[128,512]{1,0:T(8,128)(2,1)S(1)} collective-permute-done((bf16[128,512]{1,0:T(8,128)(2,1)S(1)}, bf16[128,512]{1,0:T(8,128)(2,1)S(1)}, u32[]{:S(2)}, u32[]{:S(2)}) %collective-permute-start.11) | collective-permute-done | bytes 131104 | tf_op jit(solution)/shard_map/ppermute | solution.py:391
  274.3 2.1 add_bitcast_fusion
  (60 shorter events, 6.0 us)
Async XLA Ops:
  7.2 129.4 %copy-start = (f32[900,512]{1,0:T(8,128)S(1)}, f32[900,512]{1,0:T(8,128)}, u32[]{:S(2)}) copy-start(f32[900,512]{1,0:T(8,128)} %param.19) | copy-start | bytes 5529604
  7.2 49.2 %all-gather.8.cloned.1.call-start = ((), (), s32[]{:S(2)}) async-start(), calls=%async_computation.1 | async-start | bytes 4718592 | tf_op jit(solution)/shard_map/all_gather | solution.py:429
  7.9 128.5 %all-gather.6.cloned.1.call-start = ((), (), s32[]{:S(2)}) async-start(), calls=%async_computation | async-start | bytes 4325376 | tf_op jit(solution)/shard_map/all_gather | solution.py:452
  10.5 13.0 %copy-start.10 = (s32[1,1,8,1]{2,3,1,0:T(1,128)S(1)}, s32[1,1,8,1]{2,3,1,0:T(1,128)}, u32[]{:S(2)}) copy-start(s32[1,1,8,1]{2,3,1,0:T(1,128)} %param.20) | copy-start | bytes 100
  63.3 6.1 %collective-permute-start = (bf16[128,512]{1,0:T(8,128)(2,1)S(1)}, bf16[128,512]{1,0:T(8,128)(2,1)S(1)}, u32[]{:S(2)}, u32[]{:S(2)}) collective-permute-start(bf16[128,512]{1,0:T(8,128)(2,1)S(1)} %get-tuple-element.63), channel_id=1, source_target_pairs={{0,8},{8,0},{16,24},{24,16},{1,9},{9,1},{17,25},{25,17},{2,10},{10... | collective-permute-start | bytes 393224 | tf_op jit(solution)/shard_map/ppermute | solution.py:391
  64.8 8.2 %collective-permute-start.1 = (bf16[128,512]{1,0:T(8,128)(2,1)S(1)}, bf16[128,512]{1,0:T(8,128)(2,1)S(1)}, u32[]{:S(2)}, u32[]{:S(2)}) collective-permute-start(bf16[128,512]{1,0:T(8,128)(2,1)S(1)} %get-tuple-element.65), channel_id=1, source_target_pairs={{0,16},{8,24},{16,0},{24,8},{1,17},{9,25},{17,1},{25,9},{2,18},{10... | collective-permute-start | bytes 393224 | tf_op jit(solution)/shard_map/ppermute | solution.py:391
  66.3 6.7 %collective-permute-start.2 = (bf16[128,512]{1,0:T(8,128)(2,1)S(1)}, bf16[128,512]{1,0:T(8,128)(2,1)S(1)}, u32[]{:S(2)}, u32[]{:S(2)}) collective-permute-start(bf16[128,512]{1,0:T(8,128)(2,1)S(1)} %get-tuple-element.64), channel_id=1, source_target_pairs={{0,24},{8,16},{16,8},{24,0},{1,25},{9,17},{17,9},{25,1},{2,26},{10... | collective-permute-start | bytes 393224 | tf_op jit(solution)/shard_map/ppermute | solution.py:391
  74.7 153.4 %all-gather.10.cloned.1.call-start = ((), (), s32[]{:S(2)}) async-start(), calls=%async_computation.2 | async-start | bytes 2359296 | tf_op jit(solution)/shard_map/all_gather | solution.py:469
  74.8 61.7 %copy-start.6 = (s32[1024]{0:T(1024)S(1)}, s32[1024]{0:T(1024)}, u32[]{:S(2)}) copy-start(s32[1024]{0:T(1024)} %param.26) | copy-start | bytes 12292
  74.8 61.7 %copy-start.8 = (s32[1024]{0:T(1024)S(1)}, s32[1024]{0:T(1024)}, u32[]{:S(2)}) copy-start(s32[1024]{0:T(1024)} %param.27) | copy-start | bytes 12292
  136.6 5.6 %copy-start.9 = (s32[1024]{0:T(1024)S(1)}, s32[1024]{0:T(1024)}, u32[]{:S(2)}) copy-start(s32[1024]{0:T(1024)} %param.29) | copy-start | bytes 12292
  136.6 5.6 %copy-start.7 = (s32[1024,8]{0,1:T(8,128)S(1)}, s32[1024,8]{0,1:T(8,128)}, u32[]{:S(2)}) copy-start(s32[1024,8]{0,1:T(8,128)} %param.28) | copy-start | bytes 98308
  143.6 78.2 %collective-permute-start.3 = (bf16[1,1,144,512]{3,2,1,0:T(8,128)(2,1)S(1)}, bf16[1,1,144,512]{3,2,1,0:T(8,128)(2,1)S(1)}, u32[]{:S(2)}, u32[]{:S(2)}) collective-permute-start(bf16[1,1,144,512]{3,2,1,0:T(8,128)(2,1)S(1)} %get-tuple-element.58), channel_id=1, source_target_pairs={{0,1},{1,2},{2,3},{3,4},{4,5},{5,6},{6,7},{7,0},{8,9},{9,10},{10,1... | collective-permute-start | bytes 442376 | tf_op jit(solution)/shard_map/ppermute | solution.py:465
  143.9 78.3 %collective-permute-start.4 = (bf16[1,1,144,512]{3,2,1,0:T(8,128)(2,1)S(1)}, bf16[1,1,144,512]{3,2,1,0:T(8,128)(2,1)S(1)}, u32[]{:S(2)}, u32[]{:S(2)}) collective-permute-start(bf16[1,1,144,512]{3,2,1,0:T(8,128)(2,1)S(1)} %get-tuple-element.57), channel_id=1, source_target_pairs={{0,2},{1,3},{2,4},{3,5},{4,6},{5,7},{6,0},{7,1},{8,10},{9,11},{10,... | collective-permute-start | bytes 442376 | tf_op jit(solution)/shard_map/ppermute | solution.py:465
  144.6 79.0 %collective-permute-start.5 = (bf16[1,1,144,512]{3,2,1,0:T(8,128)(2,1)S(1)}, bf16[1,1,144,512]{3,2,1,0:T(8,128)(2,1)S(1)}, u32[]{:S(2)}, u32[]{:S(2)}) collective-permute-start(bf16[1,1,144,512]{3,2,1,0:T(8,128)(2,1)S(1)} %get-tuple-element.56), channel_id=1, source_target_pairs={{0,3},{1,4},{2,5},{3,6},{4,7},{5,0},{6,1},{7,2},{8,11},{9,12},{10,... | collective-permute-start | bytes 442376 | tf_op jit(solution)/shard_map/ppermute | solution.py:465
  146.6 77.1 %collective-permute-start.6 = (bf16[1,1,144,512]{3,2,1,0:T(8,128)(2,1)S(1)}, bf16[1,1,144,512]{3,2,1,0:T(8,128)(2,1)S(1)}, u32[]{:S(2)}, u32[]{:S(2)}) collective-permute-start(bf16[1,1,144,512]{3,2,1,0:T(8,128)(2,1)S(1)} %get-tuple-element.55), channel_id=1, source_target_pairs={{0,4},{1,5},{2,6},{3,7},{4,0},{5,1},{6,2},{7,3},{8,12},{9,13},{10,... | collective-permute-start | bytes 442376 | tf_op jit(solution)/shard_map/ppermute | solution.py:465
  148.2 75.5 %collective-permute-start.7 = (bf16[1,1,144,512]{3,2,1,0:T(8,128)(2,1)S(1)}, bf16[1,1,144,512]{3,2,1,0:T(8,128)(2,1)S(1)}, u32[]{:S(2)}, u32[]{:S(2)}) collective-permute-start(bf16[1,1,144,512]{3,2,1,0:T(8,128)(2,1)S(1)} %get-tuple-element.54), channel_id=1, source_target_pairs={{0,5},{1,6},{2,7},{3,0},{4,1},{5,2},{6,3},{7,4},{8,13},{9,14},{10,... | collective-permute-start | bytes 442376 | tf_op jit(solution)/shard_map/ppermute | solution.py:465
  171.3 50.9 %copy-start.3 = (bf16[8,1,144,512]{3,2,1,0:T(8,128)(2,1)S(1)}, bf16[8,1,144,512]{3,2,1,0:T(8,128)(2,1)}, u32[]{:S(2)}) copy-start(bf16[8,1,144,512]{3,2,1,0:T(8,128)(2,1)} %get-tuple-element.59) | copy-start | bytes 3538948
  221.8 6.2 %collective-permute-start.8 = (bf16[1,1,144,512]{3,2,1,0:T(8,128)(2,1)S(1)}, bf16[1,1,144,512]{3,2,1,0:T(8,128)(2,1)S(1)}, u32[]{:S(2)}, u32[]{:S(2)}) collective-permute-start(bf16[1,1,144,512]{3,2,1,0:T(8,128)(2,1)S(1)} %get-tuple-element.53), channel_id=1, source_target_pairs={{0,6},{1,7},{2,0},{3,1},{4,2},{5,3},{6,4},{7,5},{8,14},{9,15},{10,... | collective-permute-start | bytes 442376 | tf_op jit(solution)/shard_map/ppermute | solution.py:465
  222.2 5.8 %collective-permute-start.9 = (bf16[1,1,144,512]{3,2,1,0:T(8,128)(2,1)S(1)}, bf16[1,1,144,512]{3,2,1,0:T(8,128)(2,1)S(1)}, u32[]{:S(2)}, u32[]{:S(2)}) collective-permute-start(bf16[1,1,144,512]{3,2,1,0:T(8,128)(2,1)S(1)} %get-tuple-element.52), channel_id=1, source_target_pairs={{0,7},{1,0},{2,1},{3,2},{4,3},{5,4},{6,5},{7,6},{8,15},{9,8},{10,9... | collective-permute-start | bytes 442376 | tf_op jit(solution)/shard_map/ppermute | solution.py:465
  228.0 1.0 copy-start.4
  262.4 6.5 %copy-start.5 = (f32[256,512]{1,0:T(8,128)S(1)}, f32[256,512]{1,0:T(8,128)}, u32[]{:S(2)}) copy-start(f32[256,512]{1,0:T(8,128)} %get-tuple-element.49) | copy-start | bytes 1572868
  263.8 10.5 %copy-start.2 = (bf16[512,512]{1,0:T(8,128)(2,1)S(1)}, bf16[512,512]{1,0:T(8,128)(2,1)}, u32[]{:S(2)}) copy-start(bf16[512,512]{1,0:T(8,128)(2,1)} %wself_ref.3) | copy-start | bytes 1572868
  263.8 6.1 %collective-permute-start.10 = (bf16[128,512]{1,0:T(8,128)(2,1)S(1)}, bf16[128,512]{1,0:T(8,128)(2,1)S(1)}, u32[]{:S(2)}, u32[]{:S(2)}) collective-permute-start(bf16[128,512]{1,0:T(8,128)(2,1)S(1)} %get-tuple-element.60), channel_id=1, source_target_pairs={{0,8},{8,0},{16,24},{24,16},{1,9},{9,1},{17,25},{25,17},{2,10},{10... | collective-permute-start | bytes 393224 | tf_op jit(solution)/shard_map/ppermute | solution.py:391
  265.2 9.1 %collective-permute-start.11 = (bf16[128,512]{1,0:T(8,128)(2,1)S(1)}, bf16[128,512]{1,0:T(8,128)(2,1)S(1)}, u32[]{:S(2)}, u32[]{:S(2)}) collective-permute-start(bf16[128,512]{1,0:T(8,128)(2,1)S(1)} %get-tuple-element.62), channel_id=1, source_target_pairs={{0,16},{8,24},{16,0},{24,8},{1,17},{9,25},{17,1},{25,9},{2,18},{10... | collective-permute-start | bytes 393224 | tf_op jit(solution)/shard_map/ppermute | solution.py:391
  265.9 8.3 %collective-permute-start.12 = (bf16[128,512]{1,0:T(8,128)(2,1)S(1)}, bf16[128,512]{1,0:T(8,128)(2,1)}, u32[]{:S(2)}, u32[]{:S(2)}) collective-permute-start(bf16[128,512]{1,0:T(8,128)(2,1)S(1)} %get-tuple-element.61), channel_id=1, source_target_pairs={{0,24},{8,16},{16,8},{24,0},{1,25},{9,17},{17,9},{25,1},{2,26},{10... | collective-permute-start | bytes 393224 | tf_op jit(solution)/shard_map/ppermute | solution.py:391
  269.0 7.4 %copy-start.1 = (f32[900,512]{1,0:T(8,128)S(1)}, f32[900,512]{1,0:T(8,128)}, u32[]{:S(2)}) copy-start(f32[900,512]{1,0:T(8,128)} %param.19) | copy-start | bytes 5529604
Sparse Core Ops, SparseCore 0:
  9.6 46.7 all-gather.7
  74.8 61.5 all-gather.5
  138.6 46.4 all-gather.9

commit v2 on v0

v2 whole, which is shorter than its diff:
```python
import functools

import jax
import jax.numpy as jnp
from jax import lax
from jax.experimental import pallas as pl
from jax.experimental.pallas import tpu as pltpu
from jax.sharding import PartitionSpec as P

NEG_FILL = -1e30
BF = jnp.bfloat16
F32 = jnp.float32
I32 = jnp.int32
MARK_ROWS = 16


def dot(a, b):
    return jnp.dot(a, b, preferred_element_type=F32)


def dot_nt(a, b):
    return lax.dot_general(a, b, (((1,), (1,)), ((), ())), preferred_element_type=F32)


def split(x):
    hi = x.astype(BF)
    return hi, (x - hi.astype(F32)).astype(BF)


def params(small, mebibytes):
    return pltpu.CompilerParams(vmem_limit_bytes=(mebibytes if small else 60) * 1024 * 1024)


def fixed(shape):
    return pl.BlockSpec(shape, lambda *a: (0,) * len(shape), pipeline_mode=pl.Buffered(1))


def shaped(*pairs):
    return [jax.ShapeDtypeStruct(s, d) for s, d in pairs]


def cost(micros):
    return pl.CostEstimate(flops=micros * 10**9, bytes_accessed=micros * 10**6, transcendentals=0)


def rows_at(index, size):
    return pl.ds(pl.multiple_of(index * size, size), size)


def fold_kernel(tiles, per, src, tgt, rel, live, want, core, a_ref, *refs):
    cat_ref, send_ref, acc, wacc, line, ids = refs
    step = pl.program_id(0)
    block = a_ref.shape[1]
    slots = want.shape[0]
    part_rows = block + MARK_ROWS
    rel_rows = (wacc.shape[0] - 8) // tiles
    count = line.shape[0]

    @pl.when(step == 0)
    def _():
        acc[...] = jnp.zeros_like(acc)
        wacc[...] = jnp.zeros_like(wacc)

    sums = dot_nt(jnp.ones((8, block), BF), a_ref[...].reshape(per * block, block))
    for i in range(per):
        b = step * per + i
        good = b < live[0]
        at = jnp.where(good, tgt[b] * slots + src[b], tiles * slots)
        acc[at] = acc[at] + a_ref[i].astype(F32)
        row = jnp.where(good, tgt[b] * rel_rows + rel[b], tiles * rel_rows)
        total = sums[0:1, i * block : (i + 1) * block]
        wacc[pl.ds(row, 1), :] = wacc[pl.ds(row, 1), :] + total
        line[pl.ds(b, 1), :] = jnp.where(good, total, 0.0)
        ids[pl.ds(b, 1), :] = jnp.zeros((1, block), F32) + (rel[b] * tiles + tgt[b]).astype(F32)

    @pl.when(step == pl.num_programs(0) - 1)
    def _():
        base = 2 * slots * block
        quarter = count // tiles
        for z in range(slots // 2):
            for t in range(tiles):
                at = slice(t * block, (t + 1) * block)
                those = slice(t * quarter, (t + 1) * quarter)
                tail = 2 * part_rows
                send_ref[z, tail : tail + quarter, at] = line[those, :].astype(BF)
                packed = ids[those, :].astype(I32)
                send_ref[z, tail + quarter : tail + 2 * quarter, at] = jnp.where(
                    lax.broadcasted_iota(I32, packed.shape, 1) < block // 2,
                    packed // tiles,
                    packed % tiles,
                ).astype(F32).astype(BF)
        for t in range(tiles):
            at = slice(t * block, (t + 1) * block)
            hi, lo = split(-wacc[t * rel_rows : (t + 1) * rel_rows, :].T)
            cat_ref[at, base : base + rel_rows] = hi
            cat_ref[at, base + rel_rows : base + 2 * rel_rows] = hi
            cat_ref[at, base + 2 * rel_rows :] = lo
            for s in range(slots):
                part = acc[t * slots + s]
                hi, lo = split(part)
                cat_ref[at, s * block : (s + 1) * block] = hi
                cat_ref[at, (slots + s) * block : (slots + s + 1) * block] = lo
                place = pl.multiple_of((s % 2 ^ core[0]) * part_rows, 16)
                send_ref[s // 2, pl.ds(place, block), at] = part.T.astype(BF)
                mark = jnp.zeros((MARK_ROWS, block), F32) + want[s].astype(F32)
                send_ref[s // 2, pl.ds(place + block, MARK_ROWS), at] = mark.astype(BF)


def fold(adj, src, tgt, rel, live, want, core, tiles, rel_rows):
    count, block, _ = adj.shape
    slots = want.shape[0]
    per = next(p for p in (48, 16, 8, 4, 2, 1) if count % p == 0)
    rows = tiles * block
    outs = [
        ((rows, 2 * slots * block + 3 * rel_rows), BF),
        ((slots // 2, 2 * (block + MARK_ROWS) + 2 * (count // tiles), rows), BF),
    ]
    return pl.pallas_call(
        functools.partial(fold_kernel, tiles, per),
        grid_spec=pltpu.PrefetchScalarGridSpec(
            num_scalar_prefetch=6,
            grid=(count // per,),
            in_specs=[pl.BlockSpec((per, block, block), lambda i, *a: (i, 0, 0))],
            out_specs=[fixed(s) for s, _ in outs],
            scratch_shapes=[
                pltpu.VMEM((tiles * slots + 1, block, block), F32),
                pltpu.VMEM((tiles * rel_rows + 8, block), F32),
                pltpu.VMEM((count, block), F32),
                pltpu.VMEM((count, block), F32),
            ],
        ),
        out_shape=shaped(*outs),
        compiler_params=params(slots <= 8, 60),
        cost_estimate=cost(8),
        name="fold_adjacency",
    )(src, tgt, rel, live, want, core, adj)


def stacked(shift, flip, cut, block):
    if shift == 0:
        return 0, None
    if flip < 3:
        return 1 + flip, (shift - 1) * block
    return (4, (shift - 1) * block) if shift < cut else (5, (shift - cut) * block)


def pick_kernel(planes, block, cut, plane, grp, mine, theirs, *refs):
    sources, (mine_ref, theirs_ref, sems) = refs[:-3], refs[-3:]
    flips = sources[0].shape[0] // block
    for wait in (False, True):
        for n, (ids, out_ref) in enumerate(((mine, mine_ref), (theirs, theirs_ref))):
            for s in range(planes):
                j = lax.rem(plane[0] - s + planes, planes)
                for a in range(1 if s == 0 or wait else flips):
                    which, row = stacked(s, a, cut, block)
                    if s == 0:
                        source = sources[0].at[rows_at(ids[j], block), :]
                    else:
                        source = sources[which].at[row : row + block, :]
                    target = out_ref.at[rows_at(j, block), :]
                    copy = pltpu.make_async_copy(source, target, sems.at[n, s])
                    if wait:
                        copy.wait()
                    elif s == 0:
                        copy.start()
                    else:

                        @pl.when((ids[j] ^ grp[0]) == a)
                        def _():
                            copy.start()


def pick(plane, grp, mine, theirs, sources, block):
    planes = mine.shape[0]
    out = ((planes * block, sources[0].shape[1]), BF)
    cut = 1 + sources[4].shape[0] // block
    anywhere = pl.BlockSpec(memory_space=pl.ANY)
    return pl.pallas_call(
        functools.partial(pick_kernel, planes, block, cut),
        grid_spec=pltpu.PrefetchScalarGridSpec(
            num_scalar_prefetch=4,
            grid=(1,),
            in_specs=[anywhere] * len(sources),
            out_specs=[fixed(out[0])] * 2,
            scratch_shapes=[pltpu.SemaphoreType.DMA((2, planes))],
        ),
        out_shape=shaped(out, out),
        compiler_params=params(planes <= 4, 6),
        name="pick_mirrors",
    )(plane, grp, mine, theirs, *sources)


def forward_kernel(block, rel_count, core, mine_ref, theirs_ref, cat_ref, rel_ref, out_ref, outb_ref, right):
    depth = 2 * mine_ref.shape[0]
    rel_rows = rel_ref.shape[0]
    inside = lax.broadcasted_iota(I32, rel_ref.shape, 0) < rel_count
    for j in range(mine_ref.shape[0] // block):
        at = slice(j * block, (j + 1) * block)
        for base in (0, depth // block):
            right[rows_at(base + 2 * j + core[0], block), :] = mine_ref[at, :]
            right[rows_at(base + 2 * j + 1 - core[0], block), :] = theirs_ref[at, :]
    hi, lo = split(jnp.where(inside, rel_ref[...], 0.0))
    for i, part in enumerate((hi, lo, hi)):
        right[2 * depth + i * rel_rows : 2 * depth + (i + 1) * rel_rows, :] = part
    total = dot(cat_ref[...], right[...])
    out_ref[...] = total
    outb_ref[...] = total.astype(BF)


def forward(core, mine, theirs, cat, rel, block):
    rows, depth = cat.shape
    width = mine.shape[1]
    rel_rows = (depth - 4 * mine.shape[0]) // 3
    args = (mine, theirs, cat, rel)
    return pl.pallas_call(
        functools.partial(forward_kernel, block, rel.shape[0]),
        grid_spec=pltpu.PrefetchScalarGridSpec(
            num_scalar_prefetch=1,
            grid=(1,),
            in_specs=[fixed(x.shape) for x in args[:3]] + [fixed((rel_rows, width))],
            out_specs=[fixed((rows, width)), fixed((rows, width))],
            scratch_shapes=[pltpu.VMEM((depth, width), BF)],
        ),
        out_shape=shaped(((rows, width), F32), ((rows, width), BF)),
        compiler_params=params(mine.shape[0] <= 512, 16),
        name="forward_partial",
    )(core, *args)


def activate_kernel(planes, flips, cut, plane, grp, win_ref, wself_ref, *refs):
    agg_pieces = refs[: planes * flips]
    sources = refs[planes * flips : planes * flips + 6]
    outs = refs[planes * flips + 6 : planes * flips + 10]
    *held, sems = refs[planes * flips + 10 :]
    agg_ref, node_ref, h_ref, d_ref = held
    rows = sources[0].shape[0]
    block = rows // flips
    for s in range(planes):
        j = lax.rem(plane[0] - s + planes, planes)
        for a in range(flips):
            at = rows_at(j * flips + (grp[0] ^ a), block)
            agg_ref[at, :] = agg_pieces[s * flips + a][...]
            if s > 0:
                which, row = stacked(s, a, cut, block)
                node_ref[at, :] = sources[which][row : row + block, :]
        if s == 0:
            node_ref[rows_at(j, rows), :] = sources[0][...]

    def embed(j, carry):
        at = rows_at(j, rows)
        act = jnp.tanh(dot(agg_ref[at, :], win_ref[...]) + dot(node_ref[at, :], wself_ref[...]))
        h_ref[at, :] = act.astype(BF)
        d_ref[at, :] = (1.0 - act * act).astype(BF)
        for n in range(4):
            pltpu.make_async_copy(held[n].at[at, :], outs[n].at[at, :], sems.at[n, j]).start()
        return carry

    def finish(j, carry):
        at = rows_at(j, rows)
        for n in range(4):
            pltpu.make_async_copy(held[n].at[at, :], outs[n].at[at, :], sems.at[n, j]).wait()
        return carry

    lax.fori_loop(0, planes, embed, 0)
    lax.fori_loop(0, planes, finish, 0)


def activate(plane, grp, agg_pieces, sources, w_in, w_self):
    rows, width = sources[0].shape
    block = agg_pieces[0].shape[0]
    flips = rows // block
    cut = 1 + sources[4].shape[0] // block
    planes = len(agg_pieces) // flips
    out = ((planes * rows, width), BF)
    args = (w_in, w_self, *agg_pieces, *sources)
    return pl.pallas_call(
        functools.partial(activate_kernel, planes, flips, cut),
        grid_spec=pltpu.PrefetchScalarGridSpec(
            num_scalar_prefetch=2,
            grid=(1,),
            in_specs=[fixed(x.shape) for x in args],
            out_specs=[pl.BlockSpec(memory_space=pl.ANY)] * 4,
            scratch_shapes=[pltpu.VMEM(*out)] * 4 + [pltpu.SemaphoreType.DMA((4, planes))],
        ),
        out_shape=shaped(*[out] * 4),
        compiler_params=params(planes <= 4, 60),
        name="activate",
    )(plane, grp, *args)


def row_gradient(gs, h, start, qb_ref, qg_ref, meta_ref):
    step, width = h.shape
    count = qb_ref.shape[0]
    colsum = dot(gs, jnp.ones((count, 128), BF))
    colsum = jnp.concatenate([colsum] * (width // 128), axis=1)
    row = lax.broadcasted_iota(I32, (step, count), 0)
    picked = jnp.where(row == meta_ref[8:9, :] - start, 1.0, 0.0).astype(BF)
    grad = dot(gs, qb_ref[...]) - h.astype(F32) * colsum
    return 2.0 * width ** (-0.5) * grad + dot(picked, qg_ref[...])


def score_kernel(block, step, total_q, own_ref, other_ref, rel_ref, bias_ref, meta_ref, *refs):
    gs_ref, qg_ref, qb_ref, loss_ref = refs[:4]
    s_ref, ht_ref = refs[-2:]
    half, width = own_ref.shape
    qt = rel_ref.shape[0]
    scale = width ** (-0.5)
    blocks = step // block
    halves = ((0, own_ref), (half, other_ref))
    tail = meta_ref[0:1, :]
    head = jnp.broadcast_to(meta_ref[8:9, :].astype(F32), (128, qt)).T
    head = jnp.concatenate([head] * (step // 128), axis=1).astype(I32)

    q = rel_ref[...]
    for base, ref in halves:

        def pick(b, q):
            column = lax.broadcasted_iota(I32, (qt, step), 1)
            picked = jnp.where(column == head - (base + b * step), 1.0, 0.0).astype(BF)
            return q + dot(picked, ref[rows_at(b, step), :])

        q = lax.fori_loop(0, half // step, pick, q)
    qb_ref[...] = q.astype(BF)
    flipped = q.T
    hi, lo = split(flipped * (2.0 * scale))
    qsq = scale * jnp.sum(flipped * flipped, axis=0, keepdims=True)

    top = jnp.full((8, qt), 2.0 * NEG_FILL, F32)
    for base, ref in halves:

        def first(b, top):
            hb = ref[rows_at(b, step), :]
            cross = dot(hb, hi) + dot(hb, lo)
            x = hb.astype(F32)
            hsq = scale * jnp.sum(x * x, axis=1, keepdims=True)
            ht_ref[:, pl.ds(pl.multiple_of(base + b * step, step), step)] = x.T.astype(BF)
            for u in range(blocks):
                at = slice(u * block, (u + 1) * block)
                bias = bias_ref[pl.ds(base // block + b * blocks + u, 1), :] - qsq
                s = cross[at] - hsq[at] + bias
                s_ref[pl.ds(pl.multiple_of(base + b * step + u * block, block), block), :] = s
                top = jnp.maximum(top, jnp.max(s.reshape(block // 8, 8, qt), axis=0))
            return top

        top = lax.fori_loop(0, half // step, first, top, unroll=2)
    top = jnp.max(top, axis=0, keepdims=True)
    row = lax.broadcasted_iota(I32, (block, qt), 0)

    def second(b, carry):
        norm, truth = carry
        s = s_ref[rows_at(b, block), :]
        e = jnp.exp(s - top)
        s_ref[rows_at(b, block), :] = e
        at_tail = jnp.where(row == tail - b * block, s, 0.0)
        norm = norm + jnp.sum(e.reshape(block // 8, 8, qt), axis=0)
        truth = truth + jnp.sum(at_tail.reshape(block // 8, 8, qt), axis=0)
        return norm, truth

    zero = jnp.zeros((8, qt), F32)
    norm, truth = lax.fori_loop(0, 2 * half // block, second, (zero, zero))
    norm = jnp.sum(norm, axis=0, keepdims=True)
    truth = jnp.sum(truth, axis=0, keepdims=True)
    loss_ref[...] = top + jnp.log(norm) - truth
    inverse = 1.0 / norm
    share = inverse * (1.0 / total_q)

    def third(b, carry):
        picked = jnp.where(row == tail - b * block, 1.0 / total_q, 0.0)
        gs_ref[rows_at(b, block), :] = (s_ref[rows_at(b, block), :] * share - picked).astype(BF)
        return carry

    lax.fori_loop(0, 2 * half // block, third, 0)
    pulled = dot(ht_ref[...], gs_ref[...])
    rowsum = (norm * inverse - 1.0) * (1.0 / total_q)
    qg_ref[...] = (2.0 * scale * (pulled - flipped * rowsum)).T.astype(BF)
    for grad_ref in refs[4:-2]:

        def push(b, carry):
            at = pl.ds(pl.multiple_of(half + b * step, step), step)
            grad = row_gradient(
                gs_ref[at, :], other_ref[rows_at(b, step), :], half + b * step, qb_ref, qg_ref, meta_ref
            )
            grad_ref[rows_at(b, step), :] = grad.astype(BF)
            return carry

        lax.fori_loop(0, half // step, push, 0)


def score(own, other, rel, bias, meta, block, total_q):
    half, width = own.shape
    total = 2 * half
    count = rel.shape[0]
    whole = total * count <= 4096 * 512
    qt = count if whole else 128
    once = dict(pipeline_mode=pl.Buffered(1)) if whole else {}
    wide = pl.BlockSpec((qt, width), lambda i: (i, 0), **once)
    return pl.pallas_call(
        functools.partial(score_kernel, block, min(512, half), total_q),
        grid=(count // qt,),
        in_specs=[
            fixed(own.shape),
            fixed(other.shape),
            wide,
            pl.BlockSpec((bias.shape[0], qt), lambda i: (0, i), **once),
            pl.BlockSpec((meta.shape[0], qt), lambda i: (0, i), **once),
        ],
        out_specs=[
            pl.BlockSpec((total, qt), lambda i: (0, i), **once),
            wide,
            wide,
            pl.BlockSpec((1, qt), lambda i: (0, i), **once),
        ]
        + [fixed(other.shape)] * whole,
        out_shape=shaped(
            ((total, count), BF),
            ((count, width), BF),
            ((count, width), BF),
            ((1, count), F32),
            *[(other.shape, BF)] * whole,
        ),
        scratch_shapes=[pltpu.VMEM((total, qt), F32), pltpu.VMEM((width, total), BF)],
        compiler_params=params(whole, 28),
        cost_estimate=cost(60),
        name="score",
    )(own, other, rel, bias, meta)


def rows_kernel(base, gs_ref, qb_ref, qg_ref, meta_ref, h_ref, out_ref):
    start = base + pl.program_id(0) * h_ref.shape[0]
    grad = row_gradient(gs_ref[...], h_ref[...], start, qb_ref, qg_ref, meta_ref)
    out_ref[...] = grad.astype(BF)


def rows(base, gs, qb, qg, meta, h, name):
    half, width = h.shape
    count = qb.shape[0]
    step = min(512, half)
    tall = pl.BlockSpec((step, width), lambda i: (i, 0))
    return pl.pallas_call(
        functools.partial(rows_kernel, base),
        grid=(half // step,),
        in_specs=[
            pl.BlockSpec((step, count), lambda i: (i + base // step, 0)),
            fixed(qb.shape),
            fixed(qg.shape),
            fixed(meta.shape),
            tall,
        ],
        out_specs=tall,
        out_shape=jax.ShapeDtypeStruct((half, width), BF),
        compiler_params=params(half <= 2048, 10),
        cost_estimate=cost(0),
        name=name,
    )(gs, qb, qg, meta, h)


def backward_kernel(tiles, block, planes, plane, own_ref, other_ref, d_ref, win_ref, send_ref, *refs):
    got = refs[: planes - 1]
    pre_ref, agg_grad_ref, mine_ref, theirs_ref, owned, box, sems = refs[planes - 1 :]
    j = pl.program_id(0)
    part_rows = block + MARK_ROWS
    used = 2 * part_rows

    @pl.when(j == 0)
    def _():
        owned[...] = jnp.zeros_like(owned)
        for s in range(planes):
            at = lax.rem(plane[0] - s + planes, planes)
            source = send_ref.at[plane[0]] if s == 0 else got[s - 1]
            pltpu.make_async_copy(source.at[0:used, :], box.at[at], sems.at[at]).start()

    pltpu.make_async_copy(send_ref.at[0, 0:used, :], box.at[j], sems.at[j]).wait()
    grad = own_ref[...].astype(F32) + other_ref[...].astype(F32)
    pre = (grad * d_ref[...].astype(F32)).astype(BF)
    pre_ref[...] = pre
    agg_grad = dot_nt(pre, win_ref[...]).astype(BF)
    agg_grad_ref[...] = agg_grad
    back = dot(box[j], agg_grad)
    for s in range(2):
        part = back[s * part_rows : s * part_rows + block]
        which = box[j, s * part_rows + block : (s + 1) * part_rows, :].astype(F32)[0:1, 0:1]
        for t in range(tiles):
            owned[s * tiles + t] = owned[s * tiles + t] + jnp.where(which == t, part, 0.0)

    @pl.when(j == pl.num_programs(0) - 1)
    def _():
        for t in range(tiles):
            mine_ref[t * block : (t + 1) * block, :] = owned[t]
            theirs_ref[t * block : (t + 1) * block, :] = owned[tiles + t].astype(BF)


def backward(plane, own, other, d, w_in, send, got, tiles, block):
    half, width = own.shape
    planes, _, node_rows = send.shape
    tall = pl.BlockSpec((node_rows, width), lambda i, plane: (i, 0))
    anywhere = pl.BlockSpec(memory_space=pl.ANY)
    return pl.pallas_call(
        functools.partial(backward_kernel, tiles, block, planes),
        grid_spec=pltpu.PrefetchScalarGridSpec(
            num_scalar_prefetch=1,
            grid=(planes,),
            in_specs=[tall] * 3 + [fixed(w_in.shape)] + [anywhere] * planes,
            out_specs=[tall, tall] + [fixed((node_rows, width))] * 2,
            scratch_shapes=[
                pltpu.VMEM((2 * tiles, block, width), F32),
                pltpu.VMEM((planes, 2 * (block + MARK_ROWS), node_rows), BF),
                pltpu.SemaphoreType.DMA((planes,)),
            ],
        ),
        out_shape=shaped(
            ((half, width), BF),
            ((half, width), BF),
            ((node_rows, width), F32),
            ((node_rows, width), BF),
        ),
        compiler_params=params(planes <= 4, 16),
        cost_estimate=cost(6),
        name="backward_rows",
    )(plane, own, other, d, w_in, send, *got)


def sums_kernel(skip, planes, plane, pre_ref, agg_ref, node_ref, agg_grad_ref, send_ref, *refs):
    got = refs[: planes - 1]
    out_ref, gw, grel, box, sems = refs[planes - 1 :]
    j = pl.program_id(0)
    node_rows, width = pre_ref.shape
    used = box.shape[1]

    @pl.when(j == 0)
    def _():
        gw[...] = jnp.zeros_like(gw)
        grel[...] = jnp.zeros_like(grel)
        for s in range(planes):
            at = lax.rem(plane[0] - s + planes, planes)
            source = send_ref.at[plane[0]] if s == 0 else got[s - 1]
            pltpu.make_async_copy(source.at[skip : skip + used, :], box.at[at], sems.at[at]).start()

    pltpu.make_async_copy(send_ref.at[0, skip : skip + used, :], box.at[j], sems.at[j]).wait()
    quarter = used // 2
    tiles = node_rows // 128
    cut = [slice(t * 128, (t + 1) * 128) for t in range(tiles)]
    line = jnp.concatenate([box[j, 0:quarter, at] for at in cut], axis=0)
    ids = jnp.concatenate([box[j, quarter:, at] for at in cut], axis=0).astype(F32)
    spread = jnp.concatenate(
        [jnp.where(ids[:, 64:65] == t, line.astype(F32), 0.0) for t in range(tiles)], axis=1
    ).astype(BF)
    pulled = dot(spread, agg_grad_ref[...])
    hi, lo = split(pulled)
    flat = jnp.broadcast_to(ids[:, 0:1], (tiles * quarter, 128)).T[0:1, :]
    relation = lax.broadcasted_iota(I32, (grel.shape[0], tiles * quarter), 0).astype(F32)
    chosen = jnp.where(relation == flat, 1.0, 0.0).astype(BF)
    grel[...] = grel[...] - (dot(chosen, hi) + dot(chosen, lo))
    flipped = pre_ref[...].astype(F32).T.astype(BF)
    gw[0] = gw[0] + dot(flipped, agg_ref[...])
    gw[1] = gw[1] + dot(flipped, node_ref[...])

    @pl.when(j == pl.num_programs(0) - 1)
    def _():
        out_ref[0:width, :] = gw[0].T.astype(BF)
        out_ref[width : 2 * width, :] = gw[1].T.astype(BF)
        out_ref[2 * width :, :] = grel[...].astype(BF)


def sums_of_half(plane, pre, agg, nodes, agg_grad, send, got, skip, rel_rows):
    width = pre.shape[1]
    planes, send_rows, node_rows = send.shape
    tall = pl.BlockSpec((node_rows, width), lambda i, plane: (i, 0))
    anywhere = pl.BlockSpec(memory_space=pl.ANY)
    out = ((2 * width + rel_rows, width), BF)
    return pl.pallas_call(
        functools.partial(sums_kernel, skip, planes),
        grid_spec=pltpu.PrefetchScalarGridSpec(
            num_scalar_prefetch=1,
            grid=(planes,),
            in_specs=[tall] * 4 + [anywhere] * planes,
            out_specs=fixed(out[0]),
            scratch_shapes=[
                pltpu.VMEM((2, width, width), F32),
                pltpu.VMEM((rel_rows, width), F32),
                pltpu.VMEM((planes, send_rows - skip, node_rows), BF),
                pltpu.SemaphoreType.DMA((planes,)),
            ],
        ),
        out_shape=shaped(out)[0],
        compiler_params=params(planes <= 4, 16),
        cost_estimate=cost(8),
        name="sums_of_half",
    )(plane, pre, agg, nodes, agg_grad, send, *got)


def shift_planes(x, by, cand_count):
    return lax.ppermute(x, "cand", [(i, (i + 2 * by) % cand_count) for i in range(cand_count)])


def swap_core(x, cand_count):
    return lax.ppermute(x, "cand", [(i, i ^ 1) for i in range(cand_count)])


def swap_grp(x, flip, grp_count):
    return lax.ppermute(x, "grp", [(i, i ^ flip) for i in range(grp_count)])


def total_kernel(a_ref, b_ref, gwin_ref, gwself_ref, grel_ref):
    start = 0
    for ref in (gwin_ref, gwself_ref, grel_ref):
        at = slice(start, start + ref.shape[0])
        ref[...] = a_ref[at, :].astype(F32) + b_ref[at, :].astype(F32)
        start += ref.shape[0]


def total_sums(a, b, rel_count):
    width = a.shape[1]
    outs = [((n, width), F32) for n in (width, width, rel_count)]
    return pl.pallas_call(
        total_kernel,
        in_specs=[pl.BlockSpec(memory_space=pltpu.VMEM)] * 2,
        out_specs=[pl.BlockSpec(memory_space=pltpu.VMEM)] * 3,
        out_shape=shaped(*outs),
        compiler_params=params(True, 12),
        name="total_sums",
    )(a, b)


def gather_planes(x, cand_count):
    return [x] + [shift_planes(x, s, cand_count) for s in range(1, cand_count // 2)]


def gather_stacks(planes, grp_count):
    block = planes[0].shape[0]
    here = jnp.concatenate(planes)
    one, two = swap_grp(here, 1, grp_count), swap_grp(here, 2, grp_count)
    cut = len(planes) // 2 * block
    return [
        here,
        one,
        two,
        swap_grp(one[:cut], 2, grp_count),
        swap_grp(two[cut:], 1, grp_count),
    ]


def gather_pieces(planes, first, cand_count, grp_count):
    pieces = []
    for s in range(first, cand_count // 2):
        found = [planes[s]]
        for flip in range(1, grp_count):
            low, high = flip & -flip, flip - (flip & -flip)
            if high == 0:
                found.append(swap_grp(planes[s], flip, grp_count))
            elif s % 2:
                found.append(swap_grp(found[low], high, grp_count))
            else:
                found.append(swap_grp(found[high], low, grp_count))
        pieces += found
    return pieces


def sum_over_grp(whole, whole_bf, grp_index, grp_count, share_rows):
    total = lax.dynamic_slice_in_dim(whole, grp_index * share_rows, share_rows, 0)
    for flip in range(1, grp_count):
        part = lax.dynamic_slice_in_dim(whole_bf, (grp_index ^ flip) * share_rows, share_rows, 0)
        total = total + swap_grp(part, flip, grp_count).astype(F32)
    return total


def body(
    node_emb,
    rel_emb,
    w_in,
    w_self,
    rel_score,
    mirror_blocks,
    adj_values,
    adj_source,
    adj_target,
    adj_relation,
    live_blocks,
    query_head,
    query_rel,
    allowed,
    true_tail,
):
    cand_count = lax.axis_size("cand")
    grp_count = lax.axis_size("grp")
    grp_index = lax.axis_index("grp").astype(I32)
    cand_index = lax.axis_index("cand").astype(I32)
    nodes = node_emb[0]
    node_rows, width = nodes.shape
    block = adj_values.shape[-1]
    tiles = node_rows // block
    share_rows = node_rows // grp_count
    plane_count = cand_count // 2
    plane, core = cand_index // 2, cand_index % 2
    half = plane_count * node_rows
    want = mirror_blocks.reshape(-1)
    total_q = query_head.shape[0]
    half_q = total_q // 2
    rel_rows = -(-rel_emb.shape[0] // 128) * 128

    own_share = lax.dynamic_slice_in_dim(nodes, grp_index * share_rows, share_rows, 0)
    their_want = swap_core(want, cand_count)
    nodes_at = gather_stacks(gather_planes(own_share, cand_count)[1:], grp_count)
    hold, nodes_at[0] = lax.optimization_barrier((core[None], nodes_at[0]))
    cat, send = fold(
        adj_values[0, 0],
        adj_source[0, 0],
        adj_target[0, 0],
        adj_relation[0, 0],
        live_blocks[0],
        want,
        hold,
        tiles,
        rel_rows,
    )
    mine = jnp.take(want.reshape(plane_count, 2), core, axis=1)
    theirs = jnp.take(their_want.reshape(plane_count, 2), core, axis=1)
    *nodes_at, cat, send = lax.optimization_barrier((nodes, *nodes_at, cat, send))
    mine, theirs = pick(plane[None], grp_index[None], mine, theirs, nodes_at, block)
    theirs = swap_core(theirs, cand_count)
    partial, partial_bf = forward(core[None], mine, theirs, cat, rel_emb, block)
    own_agg = sum_over_grp(partial, partial_bf, grp_index, grp_count, share_rows).astype(BF)
    agg_planes = gather_planes(own_agg, cand_count)
    agg_pieces = gather_pieces(agg_planes, 0, cand_count, grp_count)

    def own_half(x):
        return lax.dynamic_slice_in_dim(x, core * half_q, half_q, 0)

    def order(ids):
        cand = ids // node_rows
        return ((cand % 2) ^ core) * half + (cand // 2) * node_rows + ids % node_rows

    rel_q = jnp.take(rel_score, own_half(query_rel), axis=0)
    allowed_at = order(own_half(allowed) * block) // block
    block_ids = jnp.arange(2 * half // block, dtype=I32)
    hit = jnp.any(allowed_at.T[:, None, :] == block_ids[None, :, None], axis=0)
    bias = jnp.where(hit, 0.0, NEG_FILL).astype(F32)
    meta = jnp.concatenate(
        [
            jnp.broadcast_to(order(own_half(true_tail))[None], (8, half_q)),
            jnp.broadcast_to(order(own_half(query_head))[None], (8, half_q)),
        ]
    )
    agg_pieces, rel_q, bias, meta = lax.optimization_barrier((agg_pieces, rel_q, bias, meta))
    half_agg, half_nodes, half_h, half_d = activate(
        plane[None], grp_index[None], agg_pieces, nodes_at, w_in, w_self
    )

    other_h = swap_core(half_h, cand_count)
    send, half_h = lax.optimization_barrier((send, half_h))
    got = [
        shift_planes(
            lax.dynamic_index_in_dim(send, (plane + s) % plane_count, 0, keepdims=False),
            s,
            cand_count,
        )
        for s in range(1, plane_count)
    ]
    gs, qg, qb, loss, *out_grad = score(half_h, other_h, rel_q, bias, meta, block, total_q)
    gs, *more = lax.optimization_barrier((gs, *out_grad, *got))
    out_grad, got = more[: len(out_grad)], more[len(out_grad) :]
    other_loss = swap_core(loss, cand_count)
    loss = jnp.where(
        core == 0,
        jnp.concatenate([loss[0], other_loss[0]]),
        jnp.concatenate([other_loss[0], loss[0]]),
    )
    out_grad = out_grad[0] if out_grad else rows(half, gs, qb, qg, meta, other_h, "rows_other")
    in_grad = swap_core(out_grad, cand_count)
    own_grad = rows(0, gs, qb, qg, meta, half_h, "rows_own")
    pre, agg_grad, mine, theirs = backward(
        plane[None], own_grad, in_grad, half_d, w_in, send, got, tiles, block
    )
    mine = mine + swap_core(theirs, cand_count).astype(F32)
    mine, pre, agg_grad = lax.optimization_barrier((mine, pre, agg_grad))
    node_grad = sum_over_grp(mine, mine.astype(BF), grp_index, grp_count, share_rows)
    sums = sums_of_half(
        plane[None],
        pre,
        half_agg,
        half_nodes,
        agg_grad,
        send,
        got,
        2 * (block + MARK_ROWS),
        rel_rows,
    )
    gwin, gwself, grel = total_sums(sums, swap_core(sums, cand_count), rel_emb.shape[0])
    first_row = plane * node_rows + grp_index * share_rows
    own_pre = lax.dynamic_slice_in_dim(pre, first_row, share_rows, 0)
    node_grad = node_grad + dot_nt(own_pre, w_self)
    h_own = lax.dynamic_slice_in_dim(half_h, first_row, share_rows, 0)
    return (
        h_own[None],
        loss,
        node_grad[None],
        grel,
        gwin,
        gwself,
    )


def solution(mesh):
    return jax.shard_map(
        body,
        mesh=mesh,
        in_specs=(
            P("cand", None, None),
            P("grp", None),
            P(),
            P(),
            P(),
            P("grp", "cand", None, None),
            P("grp", "cand", None, None, None),
            P("grp", "cand", None),
            P("grp", "cand", None),
            P("grp", "cand", None),
            P("grp", "cand"),
            P(),
            P(),
            P(),
            P(),
        ),
        out_specs=(P("cand", "grp", None), P(), P("cand", "grp", None), P("grp", None), P(), P()),
        check_vma=False,
    )
```

time: 1120 us -> 171 us (0.15)
  waiting for transfers between devices: 518 us -> 46.6 us
  other arithmetic: 216 us -> 5.23 us
  blocking collectives: 132 us -> 0 us
  matrix products: 131 us -> 2.04 us
  local copies, waits for them, and re-layouts: 97.7 us -> 13.7 us
  Pallas kernels: 0 us -> 58.1 us
  starting transfers between devices: 9.14 us -> 42 us
  between operations: 15.1 us -> 1.86 us
    psum x4 -> x0, waiting for transfers between devices: 424 us -> none  [the longest x1 141 us: body(): lax.psum((jnp.dot(aggregate_bf.T, pre_grad, preferred_element_type=jnp.fl...]
    scatter-add x37 -> x0, other arithmetic: 198 us -> none  [the longest x12 111 us: backward_turn(): mirror_grad = mirror_grad.at[source_now].add(composed_grad)]
    dot_general x35 -> x1, matrix products: 131 us -> 2.04 us  [dot_nt(): lax.dot_general(a, b, (((1,), (1,)), ((), ())), preferred_element_type=F32)]
    psum x2 -> x0, blocking collectives: 81.8 us -> none  [body(): row_total, truth = lax.psum((local_total, truth_part), ('grp', 'cand'))]
    gather x38 -> x1, local copies, waits for them, and re-layouts: 77.2 us -> 2.33 us  [body(): rel_q = jnp.take(rel_score, own_half(query_rel), axis=0)]
    pallas_call x0 -> x9, Pallas kernels: none -> 58.1 us  [the longest x1 21.5 us: score(): pl.pallas_call(functools.partial(score_kernel, block, min(512, half), tot...]
    ppermute x0 -> x38, waiting for transfers between devices: none -> 46.6 us  [the longest x9 25.9 us: shift_planes(): lax.ppermute(x, 'cand', [(i, (i + 2 * by) % cand_count) for i in range(ca...]
    ppermute x0 -> x38, starting transfers between devices: none -> 42 us  [the longest x22 26.8 us: swap_grp(): return lax.ppermute(x, 'grp', [(i, i ^ flip) for i in range(grp_count)])]
  transfers between devices with their start and end apart: 9 -> 38, of which waited for: 7 -> 18; matrix products, arithmetic and copies ran while one was open for 21% -> 8% of each run, Pallas kernels for 0% -> 20%
where the time goes in v2:
time: 171 us; the launch traced here: 169 us
  Pallas kernels  58.1 us (34%)
  waiting for transfers between devices  46.6 us (27%)
  starting transfers between devices  42 us (25%)
  local copies, waits for them, and re-layouts  13.7 us (8%)
  other arithmetic  5.23 us (3%)
  matrix products  2.04 us (1%)
  between operations  1.86 us (1%)
    ppermute x22, starting transfers between devices, swap_grp(): return lax.ppermute(x, 'grp', [(i, i ^ flip) for i in range(grp_count)])  26.8 us
    ppermute x9, waiting for transfers between devices, shift_planes(): lax.ppermute(x, 'cand', [(i, (i + 2 * by) % cand_count) for i in range(ca...  25.9 us
    pallas_call x1, Pallas kernels, score(): pl.pallas_call(functools.partial(score_kernel, block, min(512, half), tot...  21.5 us
    ppermute x22, waiting for transfers between devices, swap_grp(): return lax.ppermute(x, 'grp', [(i, i ^ flip) for i in range(grp_count)])  18.2 us
    ppermute x9, starting transfers between devices, shift_planes(): lax.ppermute(x, 'cand', [(i, (i + 2 * by) % cand_count) for i in range(ca...  14.3 us
    pallas_call x1, Pallas kernels, fold(): pl.pallas_call(functools.partial(fold_kernel, tiles, per), grid_spec=pltp...  8.85 us
    pallas_call x1, Pallas kernels, activate(): pl.pallas_call(functools.partial(activate_kernel, planes, flips, cut), gr...  6.99 us
    pallas_call x1, Pallas kernels, sums_of_half(): pl.pallas_call(functools.partial(sums_kernel, skip, planes), grid_spec=pl...  5.76 us
  transfers between devices with their start and end apart: 38, of which 18 were waited for; matrix products, arithmetic and copies ran while one was open for 8% of the time, Pallas kernels for 20%

profile of v2, /device:TPU:8, one launch (start us, length us, event | category | flops | bytes accessed | tf_op | source)
XLA Modules:
  0.0 169.5 jit_solution(8435680454764345009)
XLA Ops:
  1.7 1.6 collective-permute-start
  4.4 1.9 %collective-permute-start.2 = (bf16[128,512]{1,0:T(8,128)(2,1)S(1)}, bf16[128,512]{1,0:T(8,128)(2,1)S(1)}, u32[]{:S(2)}, u32[]{:S(2)}) collective-permute-start(bf16[128,512]{1,0:T(8,128)(2,1)S(1)} %dynamic-slice_bitcast_fusion.4), channel_id=1, source_target_pairs={{0,6},{1,7},{2,0},{3,1},{4,2},{5,3},{6,4},{7,5},{8,14},{9,15},{10,... | collective-permute-start | bytes 393224 | tf_op jit(solution)/shard_map/ppermute | solution.py:592
  6.4 6.5 %collective-permute-done = bf16[128,512]{1,0:T(8,128)(2,1)S(1)} collective-permute-done((bf16[128,512]{1,0:T(8,128)(2,1)S(1)}, bf16[128,512]{1,0:T(8,128)(2,1)S(1)}, u32[]{:S(2)}, u32[]{:S(2)}) %collective-permute-start) | collective-permute-done | bytes 131104 | tf_op jit(solution)/shard_map/ppermute | solution.py:592
  12.9 1.6 collective-permute-done.1
  14.5 1.7 %collective-permute-done.2 = bf16[128,512]{1,0:T(8,128)(2,1)S(1)} collective-permute-done((bf16[128,512]{1,0:T(8,128)(2,1)S(1)}, bf16[128,512]{1,0:T(8,128)(2,1)S(1)}, u32[]{:S(2)}, u32[]{:S(2)}) %collective-permute-start.2) | collective-permute-done | bytes 131104 | tf_op jit(solution)/shard_map/ppermute | solution.py:592
  16.3 1.6 collective-permute-start.3
  22.4 5.0 %collective-permute-done.3.refs_2_.refs_18_ = bf16[384,512]{1,0:T(8,128)(2,1)S(1)} collective-permute-done((bf16[384,512]{1,0:T(8,128)(2,1)S(1)}, bf16[384,512]{1,0:T(8,128)(2,1)S(1)}, u32[]{:S(2)}, u32[]{:S(2)}) %collective-permute-start.3) | collective-permute-done | bytes 393248 | tf_op jit(solution)/shard_map/ppermute | solution.py:600
  31.9 8.9 %fold_adjacency.1 = (bf16[512,2816]{1,0:T(8,128)(2,1)}, bf16[4,384,512]{2,1,0:T(8,128)(2,1)}) custom-call(s32[192]{0:T(256)} %bitcast.34, s32[192]{0:T(256)} %bitcast.35, s32[192]{0:T(256)} %bitcast.36, s32[1]{0:T(128)} %bitcast.28.live, s32[8]{0:T(128)} %bitcast.38, s32[1]{0:T(128)} %bitcast.1.core, bf16[192,128,128]{2,1,0:T(8,128)(2,1)} %bitcast.33), custom_call_target="tpu_custom_call" | custom-call | flops 8000000000 | bytes 8000000 | tf_op jit(solution)/shard_map/fold_adjacency/pallas_call | solution.py:118
  40.8 3.0 %pick_mirrors.1 = (bf16[512,512]{1,0:T(8,128)(2,1)S(1)}, bf16[512,512]{1,0:T(8,128)(2,1)}) custom-call(s32[1]{0:T(128)} %bitcast.9.plane, s32[1]{0:T(128)} %bitcast.10.grp, s32[4]{0:T(128)S(1)} %fusion.31.mine, s32[4]{0:T(128)S(1)} %fusion.33.theirs, bf16[512,512]{1,0:T(8,128)(2,1)S(1)} %bitcast.30, ...), custom_call_target="tpu_custom_call" | custom-call | tf_op jit(solution)/shard_map/pick_mirrors/pallas_call | solution.py:178
  44.8 2.3 %gather_fusion = f32[512,512]{1,0:T(8,128)} fusion(f32[900,512]{1,0:T(8,128)S(1)} %copy-done, s32[1024]{0:T(1024)S(1)} %pad_clamp_fusion), kind=kCustom, calls=%fused_computation | custom fusion | bytes 2099200 | tf_op jit(solution)/shard_map/jit(_take)/gather | solution.py:732
  47.1 1.8 %copy-done.1 = bf16[512,2816]{1,0:T(8,128)(2,1)S(1)} copy-done((bf16[512,2816]{1,0:T(8,128)(2,1)S(1)}, bf16[512,2816]{1,0:T(8,128)(2,1)}, u32[]{:S(2)}) %copy-start.1) | copy-done | bytes 2883608
  50.0 1.8 %forward_partial.1 = (f32[512,512]{1,0:T(8,128)S(1)}, bf16[512,512]{1,0:T(8,128)(2,1)S(1)}) custom-call(s32[1]{0:T(128)} %bitcast.1.core, bf16[512,512]{1,0:T(8,128)(2,1)S(1)} %copy-done.10, bf16[512,512]{1,0:T(8,128)(2,1)S(1)} %collective-permute-done.8.theirs_ref, bf16[512,2816]{1,0:T(8,128)(2,1)S(1)} %copy-done.1, f32[225,512]{1,0:T(8,128)S(1)} %copy-done.13), custom_call_target="tpu_custom_call" | custom-call | tf_op jit(solution)/shard_map/forward_partial/pallas_call | solution.py:215
  55.5 3.6 %collective-permute-done.11 = bf16[128,512]{1,0:T(8,128)(2,1)S(1)} collective-permute-done((bf16[128,512]{1,0:T(8,128)(2,1)S(1)}, bf16[128,512]{1,0:T(8,128)(2,1)S(1)}, u32[]{:S(2)}, u32[]{:S(2)}) %collective-permute-start.11) | collective-permute-done | bytes 131104 | tf_op jit(solution)/shard_map/ppermute | solution.py:600
  59.1 1.7 collective-permute-done.10
  63.9 1.6 collective-permute-start.23
  65.6 3.7 %collective-permute-done.15.refs_4_ = bf16[128,512]{1,0:T(8,128)(2,1)S(1)} collective-permute-done((bf16[128,512]{1,0:T(8,128)(2,1)S(1)}, bf16[128,512]{1,0:T(8,128)(2,1)S(1)}, u32[]{:S(2)}, u32[]{:S(2)}) %collective-permute-start.15) | collective-permute-done | bytes 131104 | tf_op jit(solution)/shard_map/ppermute | solution.py:592
  84.6 1.9 %collective-permute-done.18.refs_7_ = bf16[128,512]{1,0:T(8,128)(2,1)S(1)} collective-permute-done((bf16[128,512]{1,0:T(8,128)(2,1)S(1)}, bf16[128,512]{1,0:T(8,128)(2,1)S(1)}, u32[]{:S(2)}, u32[]{:S(2)}) %collective-permute-start.18) | collective-permute-done | bytes 131104 | tf_op jit(solution)/shard_map/ppermute | solution.py:600
  88.0 7.0 %activate.1 = (bf16[2048,512]{1,0:T(8,128)(2,1)}, bf16[2048,512]{1,0:T(8,128)(2,1)}, bf16[2048,512]{1,0:T(8,128)(2,1)}, bf16[2048,512]{1,0:T(8,128)(2,1)}) custom-call(s32[1]{0:T(128)} %bitcast.9.plane, s32[1]{0:T(128)} %bitcast.10.grp, bf16[512,512]{1,0:T(8,128)(2,1)} %win_ref.3, bf16[512,512]{1,0:T(8,128)(2,1)} %wself_ref.1, bf16[128,512]{1,0:T(8,128)(2,1)} %copy-done.20, ...), custom_call_target="tpu_custom_call" | custom-call | tf_op jit(solution)/shard_map/activate/pallas_call | solution.py:276
  96.6 5.5 %collective-permute-start.29 = (bf16[384,512]{1,0:T(8,128)(2,1)S(1)}, bf16[384,512]{1,0:T(8,128)(2,1)S(1)}, u32[]{:S(2)}, u32[]{:S(2)}) collective-permute-start(bf16[384,512]{1,0:T(8,128)(2,1)S(1)} %get-tuple-element.144), channel_id=1, source_target_pairs={{0,2},{1,3},{2,4},{3,5},{4,6},{5,7},{6,0},{7,1},{8,10},{9,11},{10,... | collective-permute-start | bytes 1179656 | tf_op jit(solution)/shard_map/ppermute | solution.py:592
  102.1 1.5 collective-permute-start.31
  103.7 21.5 %score.1 = (bf16[4096,512]{1,0:T(8,128)(2,1)S(1)}, bf16[512,512]{1,0:T(8,128)(2,1)S(1)}, bf16[512,512]{1,0:T(8,128)(2,1)S(1)}, f32[1,512]{1,0:T(1,128)S(1)}, bf16[2048,512]{1,0:T(8,128)(2,1)S(1)}) custom-call(bf16[2048,512]{1,0:T(8,128)(2,1)S(1)} %copy-done.4, bf16[2048,512]{1,0:T(8,128)(2,1)} %collective-permute-done.27.other_ref, ...), custom_call_target="tpu_custom_call" | custom-call | flops 60000002048 | bytes 60000000 | tf_op jit(solution)/shard_map/score/pallas_call | solution.py:397
  125.2 3.2 %collective-permute-done.29.refs_0_ = bf16[384,512]{1,0:T(8,128)(2,1)S(1)} collective-permute-done((bf16[384,512]{1,0:T(8,128)(2,1)S(1)}, bf16[384,512]{1,0:T(8,128)(2,1)S(1)}, u32[]{:S(2)}, u32[]{:S(2)}) %collective-permute-start.29) | collective-permute-done | bytes 393248 | tf_op jit(solution)/shard_map/ppermute | solution.py:592
  128.4 8.0 %collective-permute-done.30.refs_1_ = bf16[384,512]{1,0:T(8,128)(2,1)S(1)} collective-permute-done((bf16[384,512]{1,0:T(8,128)(2,1)S(1)}, bf16[384,512]{1,0:T(8,128)(2,1)S(1)}, u32[]{:S(2)}, u32[]{:S(2)}) %collective-permute-start.30) | collective-permute-done | bytes 393248 | tf_op jit(solution)/shard_map/ppermute | solution.py:592
  136.4 3.5 %rows_own.1.own_ref = bf16[2048,512]{1,0:T(8,128)(2,1)S(1)} custom-call(bf16[4096,512]{1,0:T(8,128)(2,1)S(1)} %get-tuple-element.109.gs_ref, bf16[512,512]{1,0:T(8,128)(2,1)S(1)} %get-tuple-element.110.qb_ref, bf16[512,512]{1,0:T(8,128)(2,1)S(1)} %get-tuple-element.111.qg_ref, s32[16,512]{1,0:T(8,128)S(1)} %pad_add_fusion.meta_ref, ...), custom_call_target="tpu_custom_call" | custom-call | tf_op jit(solution)/shard_map/rows_own/pallas_call | solution.py:439
  140.6 3.8 %backward_rows.1 = (bf16[2048,512]{1,0:T(8,128)(2,1)S(1)}, bf16[2048,512]{1,0:T(8,128)(2,1)S(1)}, f32[512,512]{1,0:T(8,128)S(1)}, bf16[512,512]{1,0:T(8,128)(2,1)S(1)}) custom-call(s32[1]{0:T(128)} %bitcast.9.plane, bf16[2048,512]{1,0:T(8,128)(2,1)S(1)} %rows_own.1.own_ref, bf16[2048,512]{1,0:T(8,128)(2,1)S(1)} %collective-permute-done.32.other_ref, ...), custom_call_target="tpu_custom_call" | custom-call | flops 6000000000 | bytes 6000000 | tf_op jit(solution)/shard_map/backward_rows/pallas_call | solution.py:497
  144.6 1.8 %collective-permute-done.33 = bf16[512,512]{1,0:T(8,128)(2,1)S(1)} collective-permute-done((bf16[512,512]{1,0:T(8,128)(2,1)S(1)}, bf16[512,512]{1,0:T(8,128)(2,1)S(1)}, u32[]{:S(2)}, u32[]{:S(2)}) %collective-permute-start.33) | collective-permute-done | bytes 524320 | tf_op jit(solution)/shard_map/ppermute | solution.py:596
  147.5 5.8 %sums_of_half.1.a_ref = bf16[1280,512]{1,0:T(8,128)(2,1)S(1)} custom-call(s32[1]{0:T(128)} %bitcast.9.plane, bf16[2048,512]{1,0:T(8,128)(2,1)S(1)} %get-tuple-element.122.pre_ref, bf16[2048,512]{1,0:T(8,128)(2,1)S(1)} %copy-done.15, bf16[2048,512]{1,0:T(8,128)(2,1)S(1)} %copy-done.16, bf16[2048,512]{1,0:T(8,128)(2,1)S(1)} %get-tuple-element.125.agg_grad_ref, ...), custom_call_target="tpu_custom_call" | custom-call | flops 8000000000 | bytes 8000000 | tf_op jit(solution)/shard_map/sums_of_half/pallas_call | solution.py:570
  158.8 1.6 dynamic-slice_bitcast_fusion.3
  160.9 1.6 collective-permute-done.36
  162.6 2.0 %collective-permute-done.35 = bf16[128,512]{1,0:T(8,128)(2,1)S(1)} collective-permute-done((bf16[128,512]{1,0:T(8,128)(2,1)S(1)}, bf16[128,512]{1,0:T(8,128)(2,1)S(1)}, u32[]{:S(2)}, u32[]{:S(2)}) %collective-permute-start.35) | collective-permute-done | bytes 131104 | tf_op jit(solution)/shard_map/ppermute | solution.py:600
  164.6 2.0 %add_bitcast_fusion = f32[1,128,512]{2,1,0:T(8,128)} fusion(bf16[128,512]{1,0:T(8,128)(2,1)S(1)} %collective-permute-done.36, bf16[128,512]{1,0:T(8,128)(2,1)S(1)} %collective-permute-done.35, bf16[128,512]{1,0:T(8,128)(2,1)S(1)} %collective-permute-done.34, f32[512,512]{1,0:T(8,128)} %convert_add_fusion, s32[]{:T(128)S(6)} %select_n.140, ...), kind=kOutput, calls=%fused_computation.8 | convolution fusion | flops 67567616 | bytes 1572872 | tf_op jit(solution)/shard_map/dot_general | solution.py:22
  166.6 2.9 %total_sums.1 = (f32[512,512]{1,0:T(8,128)}, f32[512,512]{1,0:T(8,128)}, f32[225,512]{1,0:T(8,128)}) custom-call(bf16[1280,512]{1,0:T(8,128)(2,1)S(1)} %sums_of_half.1.a_ref, bf16[1280,512]{1,0:T(8,128)(2,1)} %collective-permute-done.37.b_ref), custom_call_target="tpu_custom_call" | custom-call | tf_op jit(solution)/shard_map/total_sums/pallas_call | solution.py:614
  (163 shorter events, 45.8 us)
Async XLA Ops:
  1.7 11.1 %collective-permute-start = (bf16[128,512]{1,0:T(8,128)(2,1)S(1)}, bf16[128,512]{1,0:T(8,128)(2,1)S(1)}, u32[]{:S(2)}, u32[]{:S(2)}) collective-permute-start(bf16[128,512]{1,0:T(8,128)(2,1)S(1)} %dynamic-slice_bitcast_fusion.4), channel_id=1, source_target_pairs={{0,2},{1,3},{2,4},{3,5},{4,6},{5,7},{6,0},{7,1},{8,10},{9,11},{10,... | collective-permute-start | bytes 393224 | tf_op jit(solution)/shard_map/ppermute | solution.py:592
  3.3 11.2 %collective-permute-start.1 = (bf16[128,512]{1,0:T(8,128)(2,1)S(1)}, bf16[128,512]{1,0:T(8,128)(2,1)S(1)}, u32[]{:S(2)}, u32[]{:S(2)}) collective-permute-start(bf16[128,512]{1,0:T(8,128)(2,1)S(1)} %dynamic-slice_bitcast_fusion.4), channel_id=1, source_target_pairs={{0,4},{1,5},{2,6},{3,7},{4,0},{5,1},{6,2},{7,3},{8,12},{9,13},{10,... | collective-permute-start | bytes 393224 | tf_op jit(solution)/shard_map/ppermute | solution.py:592
  4.4 11.8 %collective-permute-start.2 = (bf16[128,512]{1,0:T(8,128)(2,1)S(1)}, bf16[128,512]{1,0:T(8,128)(2,1)S(1)}, u32[]{:S(2)}, u32[]{:S(2)}) collective-permute-start(bf16[128,512]{1,0:T(8,128)(2,1)S(1)} %dynamic-slice_bitcast_fusion.4), channel_id=1, source_target_pairs={{0,6},{1,7},{2,0},{3,1},{4,2},{5,3},{6,4},{7,5},{8,14},{9,15},{10,... | collective-permute-start | bytes 393224 | tf_op jit(solution)/shard_map/ppermute | solution.py:592
  16.3 11.1 %collective-permute-start.3 = (bf16[384,512]{1,0:T(8,128)(2,1)S(1)}, bf16[384,512]{1,0:T(8,128)(2,1)S(1)}, u32[]{:S(2)}, u32[]{:S(2)}) collective-permute-start(bf16[384,512]{1,0:T(8,128)(2,1)S(1)} %constant_dynamic-update-slice_fusion.refs_1_.refs_17_), channel_id=1, source_target_pairs={{0,8},{8,0},{16,24},{24,16},{1,9},{9,1},{17,25},{25,17},{2,10},{10... | collective-permute-start | bytes 1179656 | tf_op jit(solution)/shard_map/ppermute | solution.py:600
  17.9 11.8 %collective-permute-start.4 = (bf16[384,512]{1,0:T(8,128)(2,1)S(1)}, bf16[384,512]{1,0:T(8,128)(2,1)S(1)}, u32[]{:S(2)}, u32[]{:S(2)}) collective-permute-start(bf16[384,512]{1,0:T(8,128)(2,1)S(1)} %constant_dynamic-update-slice_fusion.refs_1_.refs_17_), channel_id=1, source_target_pairs={{0,16},{8,24},{16,0},{24,8},{1,17},{9,25},{17,1},{25,9},{2,18},{10... | collective-permute-start | bytes 1179656 | tf_op jit(solution)/shard_map/ppermute | solution.py:600
  28.1 12.6 %collective-permute-start.5 = (bf16[128,512]{1,0:T(8,128)(2,1)}, bf16[128,512]{1,0:T(8,128)(2,1)S(1)}, u32[]{:S(2)}, u32[]{:S(2)}) collective-permute-start(bf16[128,512]{1,0:T(8,128)(2,1)} %slice.17), channel_id=1, source_target_pairs={{0,16},{8,24},{16,0},{24,8},{1,17},{9,25},{17,1},{25,9},{2,18},{10... | collective-permute-start | bytes 393224 | tf_op jit(solution)/shard_map/ppermute | solution.py:600
  30.4 10.4 %collective-permute-start.6 = (bf16[256,512]{1,0:T(8,128)(2,1)}, bf16[256,512]{1,0:T(8,128)(2,1)S(1)}, u32[]{:S(2)}, u32[]{:S(2)}) collective-permute-start(bf16[256,512]{1,0:T(8,128)(2,1)} %slice.18), channel_id=1, source_target_pairs={{0,8},{8,0},{16,24},{24,16},{1,9},{9,1},{17,25},{25,17},{2,10},{10... | collective-permute-start | bytes 786440 | tf_op jit(solution)/shard_map/ppermute | solution.py:600
  51.8 7.3 %collective-permute-start.11 = (bf16[128,512]{1,0:T(8,128)(2,1)S(1)}, bf16[128,512]{1,0:T(8,128)(2,1)S(1)}, u32[]{:S(2)}, u32[]{:S(2)}) collective-permute-start(bf16[128,512]{1,0:T(8,128)(2,1)S(1)} %get-tuple-element.149), channel_id=1, source_target_pairs={{0,24},{8,16},{16,8},{24,0},{1,25},{9,17},{17,9},{25,1},{2,26},{10... | collective-permute-start | bytes 393224 | tf_op jit(solution)/shard_map/ppermute | solution.py:600
  52.4 8.4 %collective-permute-start.10 = (bf16[128,512]{1,0:T(8,128)(2,1)S(1)}, bf16[128,512]{1,0:T(8,128)(2,1)S(1)}, u32[]{:S(2)}, u32[]{:S(2)}) collective-permute-start(bf16[128,512]{1,0:T(8,128)(2,1)S(1)} %get-tuple-element.150), channel_id=1, source_target_pairs={{0,16},{8,24},{16,0},{24,8},{1,17},{9,25},{17,1},{25,9},{2,18},{10... | collective-permute-start | bytes 393224 | tf_op jit(solution)/shard_map/ppermute | solution.py:600
  53.9 6.9 %collective-permute-start.9 = (bf16[128,512]{1,0:T(8,128)(2,1)S(1)}, bf16[128,512]{1,0:T(8,128)(2,1)S(1)}, u32[]{:S(2)}, u32[]{:S(2)}) collective-permute-start(bf16[128,512]{1,0:T(8,128)(2,1)S(1)} %get-tuple-element.148), channel_id=1, source_target_pairs={{0,8},{8,0},{16,24},{24,16},{1,9},{9,1},{17,25},{25,17},{2,10},{10... | collective-permute-start | bytes 393224 | tf_op jit(solution)/shard_map/ppermute | solution.py:600
  60.9 9.8 %collective-permute-start.12 = (bf16[128,512]{1,0:T(8,128)(2,1)S(1)}, bf16[128,512]{1,0:T(8,128)(2,1)S(1)}, u32[]{:S(2)}, u32[]{:S(2)}) collective-permute-start(bf16[128,512]{1,0:T(8,128)(2,1)S(1)} %add_convert_fusion.refs_0_), channel_id=1, source_target_pairs={{0,8},{8,0},{16,24},{24,16},{1,9},{9,1},{17,25},{25,17},{2,10},{10... | collective-permute-start | bytes 393224 | tf_op jit(solution)/shard_map/ppermute | solution.py:600
  62.2 9.3 %collective-permute-start.13 = (bf16[128,512]{1,0:T(8,128)(2,1)S(1)}, bf16[128,512]{1,0:T(8,128)(2,1)S(1)}, u32[]{:S(2)}, u32[]{:S(2)}) collective-permute-start(bf16[128,512]{1,0:T(8,128)(2,1)S(1)} %add_convert_fusion.refs_0_), channel_id=1, source_target_pairs={{0,16},{8,24},{16,0},{24,8},{1,17},{9,25},{17,1},{25,9},{2,18},{10... | collective-permute-start | bytes 393224 | tf_op jit(solution)/shard_map/ppermute | solution.py:600
  62.8 6.4 %collective-permute-start.15 = (bf16[128,512]{1,0:T(8,128)(2,1)S(1)}, bf16[128,512]{1,0:T(8,128)(2,1)S(1)}, u32[]{:S(2)}, u32[]{:S(2)}) collective-permute-start(bf16[128,512]{1,0:T(8,128)(2,1)S(1)} %add_convert_fusion.refs_0_), channel_id=1, source_target_pairs={{0,2},{1,3},{2,4},{3,5},{4,6},{5,7},{6,0},{7,1},{8,10},{9,11},{10,... | collective-permute-start | bytes 393224 | tf_op jit(solution)/shard_map/ppermute | solution.py:592
  62.8 11.0 %collective-permute-start.19 = (bf16[128,512]{1,0:T(8,128)(2,1)S(1)}, bf16[128,512]{1,0:T(8,128)(2,1)S(1)}, u32[]{:S(2)}, u32[]{:S(2)}) collective-permute-start(bf16[128,512]{1,0:T(8,128)(2,1)S(1)} %add_convert_fusion.refs_0_), channel_id=1, source_target_pairs={{0,4},{1,5},{2,6},{3,7},{4,0},{5,1},{6,2},{7,3},{8,12},{9,13},{10,... | collective-permute-start | bytes 393224 | tf_op jit(solution)/shard_map/ppermute | solution.py:592
  63.9 11.5 %collective-permute-start.23 = (bf16[128,512]{1,0:T(8,128)(2,1)S(1)}, bf16[128,512]{1,0:T(8,128)(2,1)S(1)}, u32[]{:S(2)}, u32[]{:S(2)}) collective-permute-start(bf16[128,512]{1,0:T(8,128)(2,1)S(1)} %add_convert_fusion.refs_0_), channel_id=1, source_target_pairs={{0,6},{1,7},{2,0},{3,1},{4,2},{5,3},{6,4},{7,5},{8,14},{9,15},{10,... | collective-permute-start | bytes 393224 | tf_op jit(solution)/shard_map/ppermute | solution.py:592
  69.2 8.4 %collective-permute-start.16 = (bf16[128,512]{1,0:T(8,128)(2,1)S(1)}, bf16[128,512]{1,0:T(8,128)(2,1)S(1)}, u32[]{:S(2)}, u32[]{:S(2)}) collective-permute-start(bf16[128,512]{1,0:T(8,128)(2,1)S(1)} %collective-permute-done.15.refs_4_), channel_id=1, source_target_pairs={{0,8},{8,0},{16,24},{24,16},{1,9},{9,1},{17,25},{25,17},{2,10},{10... | collective-permute-start | bytes 393224 | tf_op jit(solution)/shard_map/ppermute | solution.py:600
  70.8 8.0 %collective-permute-start.17 = (bf16[128,512]{1,0:T(8,128)(2,1)S(1)}, bf16[128,512]{1,0:T(8,128)(2,1)S(1)}, u32[]{:S(2)}, u32[]{:S(2)}) collective-permute-start(bf16[128,512]{1,0:T(8,128)(2,1)S(1)} %collective-permute-done.15.refs_4_), channel_id=1, source_target_pairs={{0,16},{8,24},{16,0},{24,8},{1,17},{9,25},{17,1},{25,9},{2,18},{10... | collective-permute-start | bytes 393224 | tf_op jit(solution)/shard_map/ppermute | solution.py:600
  75.4 6.4 %collective-permute-start.24 = (bf16[128,512]{1,0:T(8,128)(2,1)S(1)}, bf16[128,512]{1,0:T(8,128)(2,1)S(1)}, u32[]{:S(2)}, u32[]{:S(2)}) collective-permute-start(bf16[128,512]{1,0:T(8,128)(2,1)S(1)} %collective-permute-done.23.refs_12_), channel_id=1, source_target_pairs={{0,8},{8,0},{16,24},{24,16},{1,9},{9,1},{17,25},{25,17},{2,10},{10... | collective-permute-start | bytes 393224 | tf_op jit(solution)/shard_map/ppermute | solution.py:600
  76.8 7.8 %collective-permute-start.20 = (bf16[128,512]{1,0:T(8,128)(2,1)S(1)}, bf16[128,512]{1,0:T(8,128)(2,1)S(1)}, u32[]{:S(2)}, u32[]{:S(2)}) collective-permute-start(bf16[128,512]{1,0:T(8,128)(2,1)S(1)} %collective-permute-done.19.refs_8_), channel_id=1, source_target_pairs={{0,8},{8,0},{16,24},{24,16},{1,9},{9,1},{17,25},{25,17},{2,10},{10... | collective-permute-start | bytes 393224 | tf_op jit(solution)/shard_map/ppermute | solution.py:600
  77.7 6.9 %collective-permute-start.25 = (bf16[128,512]{1,0:T(8,128)(2,1)S(1)}, bf16[128,512]{1,0:T(8,128)(2,1)S(1)}, u32[]{:S(2)}, u32[]{:S(2)}) collective-permute-start(bf16[128,512]{1,0:T(8,128)(2,1)S(1)} %collective-permute-done.23.refs_12_), channel_id=1, source_target_pairs={{0,16},{8,24},{16,0},{24,8},{1,17},{9,25},{17,1},{25,9},{2,18},{10... | collective-permute-start | bytes 393224 | tf_op jit(solution)/shard_map/ppermute | solution.py:600
  78.8 7.6 %collective-permute-start.18 = (bf16[128,512]{1,0:T(8,128)(2,1)S(1)}, bf16[128,512]{1,0:T(8,128)(2,1)S(1)}, u32[]{:S(2)}, u32[]{:S(2)}) collective-permute-start(bf16[128,512]{1,0:T(8,128)(2,1)S(1)} %collective-permute-done.16.refs_5_), channel_id=1, source_target_pairs={{0,16},{8,24},{16,0},{24,8},{1,17},{9,25},{17,1},{25,9},{2,18},{10... | collective-permute-start | bytes 393224 | tf_op jit(solution)/shard_map/ppermute | solution.py:600
  79.7 6.7 %collective-permute-start.22 = (bf16[128,512]{1,0:T(8,128)(2,1)S(1)}, bf16[128,512]{1,0:T(8,128)(2,1)S(1)}, u32[]{:S(2)}, u32[]{:S(2)}) collective-permute-start(bf16[128,512]{1,0:T(8,128)(2,1)S(1)} %collective-permute-done.21.refs_10_), channel_id=1, source_target_pairs={{0,8},{8,0},{16,24},{24,16},{1,9},{9,1},{17,25},{25,17},{2,10},{10... | collective-permute-start | bytes 393224 | tf_op jit(solution)/shard_map/ppermute | solution.py:600
  81.7 6.2 %collective-permute-start.26 = (bf16[128,512]{1,0:T(8,128)(2,1)S(1)}, bf16[128,512]{1,0:T(8,128)(2,1)}, u32[]{:S(2)}, u32[]{:S(2)}) collective-permute-start(bf16[128,512]{1,0:T(8,128)(2,1)S(1)} %collective-permute-done.24.refs_13_), channel_id=1, source_target_pairs={{0,16},{8,24},{16,0},{24,8},{1,17},{9,25},{17,1},{25,9},{2,18},{10... | collective-permute-start | bytes 393224 | tf_op jit(solution)/shard_map/ppermute | solution.py:600
  95.0 8.7 %collective-permute-start.27 = (bf16[2048,512]{1,0:T(8,128)(2,1)}, bf16[2048,512]{1,0:T(8,128)(2,1)}, u32[]{:S(2)}, u32[]{:S(2)}) collective-permute-start(bf16[2048,512]{1,0:T(8,128)(2,1)} %get-tuple-element.101.own_ref.h_ref), channel_id=1, source_target_pairs={{0,1},{1,0},{2,3},{3,2},{4,5},{5,4},{6,7},{7,6},{8,9},{9,8},{10,11... | collective-permute-start | bytes 6291464 | tf_op jit(solution)/shard_map/ppermute | solution.py:596
  96.6 31.8 %collective-permute-start.29 = (bf16[384,512]{1,0:T(8,128)(2,1)S(1)}, bf16[384,512]{1,0:T(8,128)(2,1)S(1)}, u32[]{:S(2)}, u32[]{:S(2)}) collective-permute-start(bf16[384,512]{1,0:T(8,128)(2,1)S(1)} %get-tuple-element.144), channel_id=1, source_target_pairs={{0,2},{1,3},{2,4},{3,5},{4,6},{5,7},{6,0},{7,1},{8,10},{9,11},{10,... | collective-permute-start | bytes 1179656 | tf_op jit(solution)/shard_map/ppermute | solution.py:592
  102.1 34.3 %collective-permute-start.30 = (bf16[384,512]{1,0:T(8,128)(2,1)S(1)}, bf16[384,512]{1,0:T(8,128)(2,1)S(1)}, u32[]{:S(2)}, u32[]{:S(2)}) collective-permute-start(bf16[384,512]{1,0:T(8,128)(2,1)S(1)} %get-tuple-element.143), channel_id=1, source_target_pairs={{0,4},{1,5},{2,6},{3,7},{4,0},{5,1},{6,2},{7,3},{8,12},{9,13},{10,... | collective-permute-start | bytes 1179656 | tf_op jit(solution)/shard_map/ppermute | solution.py:592
  102.1 34.3 %collective-permute-start.31 = (bf16[384,512]{1,0:T(8,128)(2,1)S(1)}, bf16[384,512]{1,0:T(8,128)(2,1)S(1)}, u32[]{:S(2)}, u32[]{:S(2)}) collective-permute-start(bf16[384,512]{1,0:T(8,128)(2,1)S(1)} %get-tuple-element.142), channel_id=1, source_target_pairs={{0,6},{1,7},{2,0},{3,1},{4,2},{5,3},{6,4},{7,5},{8,14},{9,15},{10,... | collective-permute-start | bytes 1179656 | tf_op jit(solution)/shard_map/ppermute | solution.py:592
  153.3 13.3 %collective-permute-start.37 = (bf16[1280,512]{1,0:T(8,128)(2,1)S(1)}, bf16[1280,512]{1,0:T(8,128)(2,1)}, u32[]{:S(2)}, u32[]{:S(2)}) collective-permute-start(bf16[1280,512]{1,0:T(8,128)(2,1)S(1)} %sums_of_half.1.a_ref), channel_id=1, source_target_pairs={{0,1},{1,0},{2,3},{3,2},{4,5},{5,4},{6,7},{7,6},{8,9},{9,8},{10,11... | collective-permute-start | bytes 3932168 | tf_op jit(solution)/shard_map/ppermute | solution.py:596
  153.5 6.8 %collective-permute-start.28 = (f32[1,512]{1,0:T(1,128)S(1)}, f32[1,512]{1,0:T(1,128)S(1)}, u32[]{:S(2)}, u32[]{:S(2)}) collective-permute-start(f32[1,512]{1,0:T(1,128)S(1)} %get-tuple-element.105), channel_id=1, source_target_pairs={{0,1},{1,0},{2,3},{3,2},{4,5},{5,4},{6,7},{7,6},{8,9},{9,8},{10,11... | collective-permute-start | bytes 6152 | tf_op jit(solution)/shard_map/ppermute | solution.py:596
  155.2 7.3 %collective-permute-start.36 = (bf16[128,512]{1,0:T(8,128)(2,1)S(1)}, bf16[128,512]{1,0:T(8,128)(2,1)S(1)}, u32[]{:S(2)}, u32[]{:S(2)}) collective-permute-start(bf16[128,512]{1,0:T(8,128)(2,1)S(1)} %get-tuple-element.146), channel_id=1, source_target_pairs={{0,24},{8,16},{16,8},{24,0},{1,25},{9,17},{17,9},{25,1},{2,26},{10... | collective-permute-start | bytes 393224 | tf_op jit(solution)/shard_map/ppermute | solution.py:600
  156.6 7.9 %collective-permute-start.35 = (bf16[128,512]{1,0:T(8,128)(2,1)S(1)}, bf16[128,512]{1,0:T(8,128)(2,1)S(1)}, u32[]{:S(2)}, u32[]{:S(2)}) collective-permute-start(bf16[128,512]{1,0:T(8,128)(2,1)S(1)} %get-tuple-element.147), channel_id=1, source_target_pairs={{0,16},{8,24},{16,0},{24,8},{1,17},{9,25},{17,1},{25,9},{2,18},{10... | collective-permute-start | bytes 393224 | tf_op jit(solution)/shard_map/ppermute | solution.py:600
  158.0 6.6 %collective-permute-start.34 = (bf16[128,512]{1,0:T(8,128)(2,1)S(1)}, bf16[128,512]{1,0:T(8,128)(2,1)S(1)}, u32[]{:S(2)}, u32[]{:S(2)}) collective-permute-start(bf16[128,512]{1,0:T(8,128)(2,1)S(1)} %get-tuple-element.145), channel_id=1, source_target_pairs={{0,8},{8,0},{16,24},{24,16},{1,9},{9,1},{17,25},{25,17},{2,10},{10... | collective-permute-start | bytes 393224 | tf_op jit(solution)/shard_map/ppermute | solution.py:600
  (45 other events, 431.7 us)

commit v3 on v2

--- a/solution.py
+++ b/solution.py
@@ -11,7 +11,7 @@
 BF = jnp.bfloat16
 F32 = jnp.float32
 I32 = jnp.int32
-MARK_ROWS = 16
+INFO_ROWS = 16
 
 
 def dot(a, b):
@@ -47,12 +47,11 @@
     return pl.ds(pl.multiple_of(index * size, size), size)
 
 
-def fold_kernel(tiles, per, src, tgt, rel, live, want, core, a_ref, *refs):
-    cat_ref, send_ref, acc, wacc, line, ids = refs
+def fold_kernel(tiles, per, src, tgt, rel, live, want, core, a_ref, info_ref, *refs):
+    cat_ref, send_ref, acc, wacc, line = refs
     step = pl.program_id(0)
     block = a_ref.shape[1]
     slots = want.shape[0]
-    part_rows = block + MARK_ROWS
     rel_rows = (wacc.shape[0] - 8) // tiles
     count = line.shape[0]
 
@@ -71,24 +70,21 @@
         total = sums[0:1, i * block : (i + 1) * block]
         wacc[pl.ds(row, 1), :] = wacc[pl.ds(row, 1), :] + total
         line[pl.ds(b, 1), :] = jnp.where(good, total, 0.0)
-        ids[pl.ds(b, 1), :] = jnp.zeros((1, block), F32) + (rel[b] * tiles + tgt[b]).astype(F32)
 
     @pl.when(step == pl.num_programs(0) - 1)
     def _():
         base = 2 * slots * block
         quarter = count // tiles
+        tail = 2 * block + INFO_ROWS
+        row = lax.broadcasted_iota(I32, info_ref.shape, 0)
         for z in range(slots // 2):
+            info = info_ref[...]
+            for n in range(2):
+                info = jnp.where(row == 2 + n, want[2 * z + (n ^ core[0])].astype(F32), info)
+            send_ref[z, 2 * block : tail, :] = info.astype(BF)
             for t in range(tiles):
-                at = slice(t * block, (t + 1) * block)
-                those = slice(t * quarter, (t + 1) * quarter)
-                tail = 2 * part_rows
-                send_ref[z, tail : tail + quarter, at] = line[those, :].astype(BF)
-                packed = ids[those, :].astype(I32)
-                send_ref[z, tail + quarter : tail + 2 * quarter, at] = jnp.where(
-                    lax.broadcasted_iota(I32, packed.shape, 1) < block // 2,
-                    packed // tiles,
-                    packed % tiles,
-                ).astype(F32).astype(BF)
+                those = line[t * quarter : (t + 1) * quarter, :]
+                send_ref[z, tail:, t * block : (t + 1) * block] = those.astype(BF)
         for t in range(tiles):
             at = slice(t * block, (t + 1) * block)
             hi, lo = split(-wacc[t * rel_rows : (t + 1) * rel_rows, :].T)
@@ -100,10 +96,7 @@
                 hi, lo = split(part)
                 cat_ref[at, s * block : (s + 1) * block] = hi
                 cat_ref[at, (slots + s) * block : (slots + s + 1) * block] = lo
-                place = pl.multiple_of((s % 2 ^ core[0]) * part_rows, 16)
-                send_ref[s // 2, pl.ds(place, block), at] = part.T.astype(BF)
-                mark = jnp.zeros((MARK_ROWS, block), F32) + want[s].astype(F32)
-                send_ref[s // 2, pl.ds(place + block, MARK_ROWS), at] = mark.astype(BF)
+                send_ref[s // 2, rows_at(s % 2 ^ core[0], block), at] = part.T.astype(BF)
 
 
 def fold(adj, src, tgt, rel, live, want, core, tiles, rel_rows):
@@ -111,29 +104,32 @@
     slots = want.shape[0]
     per = next(p for p in (48, 16, 8, 4, 2, 1) if count % p == 0)
     rows = tiles * block
+    info = jnp.pad(jnp.stack([rel, tgt]).astype(F32), ((0, INFO_ROWS - 2), (0, rows - count)))
     outs = [
         ((rows, 2 * slots * block + 3 * rel_rows), BF),
-        ((slots // 2, 2 * (block + MARK_ROWS) + 2 * (count // tiles), rows), BF),
+        ((slots // 2, 2 * block + INFO_ROWS + count // tiles, rows), BF),
     ]
     return pl.pallas_call(
         functools.partial(fold_kernel, tiles, per),
         grid_spec=pltpu.PrefetchScalarGridSpec(
             num_scalar_prefetch=6,
             grid=(count // per,),
-            in_specs=[pl.BlockSpec((per, block, block), lambda i, *a: (i, 0, 0))],
+            in_specs=[
+                pl.BlockSpec((per, block, block), lambda i, *a: (i, 0, 0)),
+                fixed((INFO_ROWS, rows)),
+            ],
             out_specs=[fixed(s) for s, _ in outs],
             scratch_shapes=[
                 pltpu.VMEM((tiles * slots + 1, block, block), F32),
                 pltpu.VMEM((tiles * rel_rows + 8, block), F32),
                 pltpu.VMEM((count, block), F32),
-                pltpu.VMEM((count, block), F32),
             ],
         ),
         out_shape=shaped(*outs),
         compiler_params=params(slots <= 8, 60),
         cost_estimate=cost(8),
         name="fold_adjacency",
-    )(src, tgt, rel, live, want, core, adj)
+    )(src, tgt, rel, live, want, core, adj, info)
 
 
 def stacked(shift, flip, cut, block):
@@ -144,17 +140,18 @@
     return (4, (shift - 1) * block) if shift < cut else (5, (shift - cut) * block)
 
 
-def pick_kernel(planes, block, cut, plane, grp, mine, theirs, *refs):
+def pick_kernel(planes, block, cut, plane, grp, core, mine, theirs, *refs):
     sources, (mine_ref, theirs_ref, sems) = refs[:-3], refs[-3:]
     flips = sources[0].shape[0] // block
     for wait in (False, True):
         for n, (ids, out_ref) in enumerate(((mine, mine_ref), (theirs, theirs_ref))):
             for s in range(planes):
                 j = lax.rem(plane[0] - s + planes, planes)
+                tile = ids[2 * j + core[0]]
                 for a in range(1 if s == 0 or wait else flips):
                     which, row = stacked(s, a, cut, block)
                     if s == 0:
-                        source = sources[0].at[rows_at(ids[j], block), :]
+                        source = sources[0].at[rows_at(tile, block), :]
                     else:
                         source = sources[which].at[row : row + block, :]
                     target = out_ref.at[rows_at(j, block), :]
@@ -165,20 +162,20 @@
                         copy.start()
                     else:
 
-                        @pl.when((ids[j] ^ grp[0]) == a)
+                        @pl.when((tile ^ grp[0]) == a)
                         def _():
                             copy.start()
 
 
-def pick(plane, grp, mine, theirs, sources, block):
-    planes = mine.shape[0]
+def pick(plane, grp, core, mine, theirs, sources, block):
+    planes = mine.shape[0] // 2
     out = ((planes * block, sources[0].shape[1]), BF)
     cut = 1 + sources[4].shape[0] // block
     anywhere = pl.BlockSpec(memory_space=pl.ANY)
     return pl.pallas_call(
         functools.partial(pick_kernel, planes, block, cut),
         grid_spec=pltpu.PrefetchScalarGridSpec(
-            num_scalar_prefetch=4,
+            num_scalar_prefetch=5,
             grid=(1,),
             in_specs=[anywhere] * len(sources),
             out_specs=[fixed(out[0])] * 2,
@@ -187,44 +184,97 @@
         out_shape=shaped(out, out),
         compiler_params=params(planes <= 4, 6),
         name="pick_mirrors",
-    )(plane, grp, mine, theirs, *sources)
-
-
-def forward_kernel(block, rel_count, core, mine_ref, theirs_ref, cat_ref, rel_ref, out_ref, outb_ref, right):
+    )(plane, grp, core, mine, theirs, *sources)
+
+
+def forward_kernel(block, core, grp, mine_ref, theirs_ref, cat_ref, rel_ref, *refs):
+    *share_refs, right, total = refs
     depth = 2 * mine_ref.shape[0]
-    rel_rows = rel_ref.shape[0]
-    inside = lax.broadcasted_iota(I32, rel_ref.shape, 0) < rel_count
+    rel_count = rel_ref.shape[0]
+    rel_rows = (right.shape[0] - 2 * depth) // 3
     for j in range(mine_ref.shape[0] // block):
         at = slice(j * block, (j + 1) * block)
         for base in (0, depth // block):
             right[rows_at(base + 2 * j + core[0], block), :] = mine_ref[at, :]
             right[rows_at(base + 2 * j + 1 - core[0], block), :] = theirs_ref[at, :]
-    hi, lo = split(jnp.where(inside, rel_ref[...], 0.0))
+    hi, lo = split(rel_ref[...])
     for i, part in enumerate((hi, lo, hi)):
-        right[2 * depth + i * rel_rows : 2 * depth + (i + 1) * rel_rows, :] = part
-    total = dot(cat_ref[...], right[...])
-    out_ref[...] = total
-    outb_ref[...] = total.astype(BF)
-
-
-def forward(core, mine, theirs, cat, rel, block):
-    rows, depth = cat.shape
-    width = mine.shape[1]
-    rel_rows = (depth - 4 * mine.shape[0]) // 3
-    args = (mine, theirs, cat, rel)
-    return pl.pallas_call(
-        functools.partial(forward_kernel, block, rel.shape[0]),
+        base = 2 * depth + i * rel_rows
+        edge = rel_count // 16 * 16
+        right[base + edge : base + rel_rows, :] = jnp.zeros((rel_rows - edge, right.shape[1]), BF)
+        right[base : base + rel_count, :] = part
+    total[...] = dot(cat_ref[...], right[...])
+    put_shares(total, grp[0], share_refs)
+
+
+def put_shares(total, grp, refs):
+    for flip, ref in enumerate(refs):
+        ref[...] = total[rows_at(grp ^ flip, ref.shape[0]), :].astype(ref.dtype)
+
+
+def share_shapes(rows, width, flips):
+    return [((rows // flips, width), BF if flip else F32) for flip in range(flips)]
+
+
+def merge_kernel(grp, mine_ref, theirs_ref, *refs):
+    *share_refs, total = refs
+    total[...] = mine_ref[...] + theirs_ref[...].astype(F32)
+    put_shares(total, grp[0], share_refs)
+
+
+def merge(grp, mine, theirs, flips):
+    outs = share_shapes(*mine.shape, flips)
+    return pl.pallas_call(
+        merge_kernel,
         grid_spec=pltpu.PrefetchScalarGridSpec(
             num_scalar_prefetch=1,
             grid=(1,),
-            in_specs=[fixed(x.shape) for x in args[:3]] + [fixed((rel_rows, width))],
-            out_specs=[fixed((rows, width)), fixed((rows, width))],
-            scratch_shapes=[pltpu.VMEM((depth, width), BF)],
-        ),
-        out_shape=shaped(((rows, width), F32), ((rows, width), BF)),
+            in_specs=[fixed(mine.shape), fixed(theirs.shape)],
+            out_specs=[fixed(x) for x, _ in outs],
+            scratch_shapes=[pltpu.VMEM(mine.shape, F32)],
+        ),
+        out_shape=shaped(*outs),
+        compiler_params=params(True, 8),
+        name="merge_cores",
+    )(grp, mine, theirs)
+
+
+def join_kernel(*refs):
+    total = refs[0][...]
+    for ref in refs[1:-1]:
+        total = total + ref[...].astype(F32)
+    refs[-1][...] = total.astype(refs[-1].dtype)
+
+
+def join(parts, dtype):
+    return pl.pallas_call(
+        join_kernel,
+        in_specs=[pl.BlockSpec(memory_space=pltpu.VMEM)] * len(parts),
+        out_specs=pl.BlockSpec(memory_space=pltpu.VMEM),
+        out_shape=jax.ShapeDtypeStruct(parts[0].shape, dtype),
+        compiler_params=params(True, 4),
+        name="join_group",
+    )(*parts)
+
+
+def forward(core, grp, mine, theirs, cat, rel, block, flips):
+    rows, depth = cat.shape
+    width = mine.shape[1]
+    args = (mine, theirs, cat, rel)
+    outs = share_shapes(rows, width, flips)
+    return pl.pallas_call(
+        functools.partial(forward_kernel, block),
+        grid_spec=pltpu.PrefetchScalarGridSpec(
+            num_scalar_prefetch=2,
+            grid=(1,),
+            in_specs=[fixed(x.shape) for x in args],
+            out_specs=[fixed(x) for x, _ in outs],
+            scratch_shapes=[pltpu.VMEM((depth, width), BF), pltpu.VMEM((rows, width), F32)],
+        ),
+        out_shape=shaped(*outs),
         compiler_params=params(mine.shape[0] <= 512, 16),
         name="forward_partial",
-    )(core, *args)
+    )(core, grp, *args)
 
 
 def activate_kernel(planes, flips, cut, plane, grp, win_ref, wself_ref, *refs):
@@ -454,12 +504,12 @@
     )(gs, qb, qg, meta, h)
 
 
-def backward_kernel(tiles, block, planes, plane, own_ref, other_ref, d_ref, win_ref, send_ref, *refs):
+def backward_kernel(tiles, block, planes, plane, grp, own_ref, other_ref, d_ref, *refs):
+    win_ref, wself_ref, send_ref, *refs = refs
     got = refs[: planes - 1]
-    pre_ref, agg_grad_ref, mine_ref, theirs_ref, owned, box, sems = refs[planes - 1 :]
+    pre_ref, agg_grad_ref, mine_ref, theirs_ref, self_ref, owned, box, sems = refs[planes - 1 :]
     j = pl.program_id(0)
-    part_rows = block + MARK_ROWS
-    used = 2 * part_rows
+    used = 2 * block + INFO_ROWS
 
     @pl.when(j == 0)
     def _():
@@ -473,12 +523,18 @@
     grad = own_ref[...].astype(F32) + other_ref[...].astype(F32)
     pre = (grad * d_ref[...].astype(F32)).astype(BF)
     pre_ref[...] = pre
+
+    @pl.when(j == plane[0])
+    def _():
+        self_ref[...] = dot_nt(pre_ref[rows_at(grp[0], block), :], wself_ref[...])
+
     agg_grad = dot_nt(pre, win_ref[...]).astype(BF)
     agg_grad_ref[...] = agg_grad
-    back = dot(box[j], agg_grad)
+    back = dot(box[j, 0 : 2 * block, :], agg_grad)
+    info = box[j, 2 * block :, :].astype(F32)
     for s in range(2):
-        part = back[s * part_rows : s * part_rows + block]
-        which = box[j, s * part_rows + block : (s + 1) * part_rows, :].astype(F32)[0:1, 0:1]
+        part = back[s * block : (s + 1) * block]
+        which = info[2 + s : 3 + s, 0:1]
         for t in range(tiles):
             owned[s * tiles + t] = owned[s * tiles + t] + jnp.where(which == t, part, 0.0)
 
@@ -489,21 +545,21 @@
             theirs_ref[t * block : (t + 1) * block, :] = owned[tiles + t].astype(BF)
 
 
-def backward(plane, own, other, d, w_in, send, got, tiles, block):
+def backward(plane, grp, own, other, d, w_in, w_self, send, got, tiles, block):
     half, width = own.shape
     planes, _, node_rows = send.shape
-    tall = pl.BlockSpec((node_rows, width), lambda i, plane: (i, 0))
+    tall = pl.BlockSpec((node_rows, width), lambda i, *a: (i, 0))
     anywhere = pl.BlockSpec(memory_space=pl.ANY)
     return pl.pallas_call(
         functools.partial(backward_kernel, tiles, block, planes),
         grid_spec=pltpu.PrefetchScalarGridSpec(
-            num_scalar_prefetch=1,
+            num_scalar_prefetch=2,
             grid=(planes,),
-            in_specs=[tall] * 3 + [fixed(w_in.shape)] + [anywhere] * planes,
-            out_specs=[tall, tall] + [fixed((node_rows, width))] * 2,
+            in_specs=[tall] * 3 + [fixed(w_in.shape)] * 2 + [anywhere] * planes,
+            out_specs=[tall, tall] + [fixed((node_rows, width))] * 2 + [fixed((block, width))],
             scratch_shapes=[
                 pltpu.VMEM((2 * tiles, block, width), F32),
-                pltpu.VMEM((planes, 2 * (block + MARK_ROWS), node_rows), BF),
+                pltpu.VMEM((planes, 2 * block + INFO_ROWS, node_rows), BF),
                 pltpu.SemaphoreType.DMA((planes,)),
             ],
         ),
@@ -512,11 +568,12 @@
             ((half, width), BF),
             ((node_rows, width), F32),
             ((node_rows, width), BF),
+            ((block, width), F32),
         ),
         compiler_params=params(planes <= 4, 16),
         cost_estimate=cost(6),
         name="backward_rows",
-    )(plane, own, other, d, w_in, send, *got)
+    )(plane, grp, own, other, d, w_in, w_self, send, *got)
 
 
 def sums_kernel(skip, planes, plane, pre_ref, agg_ref, node_ref, agg_grad_ref, send_ref, *refs):
@@ -536,19 +593,17 @@
             pltpu.make_async_copy(source.at[skip : skip + used, :], box.at[at], sems.at[at]).start()
 
     pltpu.make_async_copy(send_ref.at[0, skip : skip + used, :], box.at[j], sems.at[j]).wait()
-    quarter = used // 2
+    quarter = used - INFO_ROWS
     tiles = node_rows // 128
+    count = tiles * quarter
     cut = [slice(t * 128, (t + 1) * 128) for t in range(tiles)]
-    line = jnp.concatenate([box[j, 0:quarter, at] for at in cut], axis=0)
-    ids = jnp.concatenate([box[j, quarter:, at] for at in cut], axis=0).astype(F32)
-    spread = jnp.concatenate(
-        [jnp.where(ids[:, 64:65] == t, line.astype(F32), 0.0) for t in range(tiles)], axis=1
-    ).astype(BF)
-    pulled = dot(spread, agg_grad_ref[...])
-    hi, lo = split(pulled)
-    flat = jnp.broadcast_to(ids[:, 0:1], (tiles * quarter, 128)).T[0:1, :]
-    relation = lax.broadcasted_iota(I32, (grel.shape[0], tiles * quarter), 0).astype(F32)
-    chosen = jnp.where(relation == flat, 1.0, 0.0).astype(BF)
+    line = jnp.concatenate([box[j, INFO_ROWS:, at] for at in cut], axis=0).astype(F32)
+    info = box[j, 0:INFO_ROWS, :].astype(F32)
+    target = jnp.broadcast_to(info[1:2, 0:count], (128, count)).T[:, 0:1]
+    spread = [jnp.where(target == t, line, 0.0) for t in range(tiles)]
+    hi, lo = split(dot(jnp.concatenate(spread, axis=1).astype(BF), agg_grad_ref[...]))
+    relation = lax.broadcasted_iota(I32, (grel.shape[0], count), 0).astype(F32)
+    chosen = jnp.where(relation == info[0:1, 0:count], 1.0, 0.0).astype(BF)
     grel[...] = grel[...] - (dot(chosen, hi) + dot(chosen, lo))
     flipped = pre_ref[...].astype(F32).T.astype(BF)
     gw[0] = gw[0] + dot(flipped, agg_ref[...])
@@ -583,7 +638,7 @@
         ),
         out_shape=shaped(out)[0],
         compiler_params=params(planes <= 4, 16),
-        cost_estimate=cost(8),
+        cost_estimate=cost(20),
         name="sums_of_half",
     )(plane, pre, agg, nodes, agg_grad, send, *got)
 
@@ -625,11 +680,9 @@
     return [x] + [shift_planes(x, s, cand_count) for s in range(1, cand_count // 2)]
 
 
-def gather_stacks(planes, grp_count):
-    block = planes[0].shape[0]
-    here = jnp.concatenate(planes)
+def gather_stacks(here, block, grp_count):
     one, two = swap_grp(here, 1, grp_count), swap_grp(here, 2, grp_count)
-    cut = len(planes) // 2 * block
+    cut = here.shape[0] // block // 2 * block
     return [
         here,
         one,
@@ -655,12 +708,8 @@
     return pieces
 
 
-def sum_over_grp(whole, whole_bf, grp_index, grp_count, share_rows):
-    total = lax.dynamic_slice_in_dim(whole, grp_index * share_rows, share_rows, 0)
-    for flip in range(1, grp_count):
-        part = lax.dynamic_slice_in_dim(whole_bf, (grp_index ^ flip) * share_rows, share_rows, 0)
-        total = total + swap_grp(part, flip, grp_count).astype(F32)
-    return total
+def swap_shares(parts, grp_count):
+    return [swap_grp(part, flip + 1, grp_count) for flip, part in enumerate(parts)]
 
 
 def body(
@@ -699,8 +748,7 @@
 
     own_share = lax.dynamic_slice_in_dim(nodes, grp_index * share_rows, share_rows, 0)
     their_want = swap_core(want, cand_count)
-    nodes_at = gather_stacks(gather_planes(own_share, cand_count)[1:], grp_count)
-    hold, nodes_at[0] = lax.optimization_barrier((core[None], nodes_at[0]))
+    stack = jnp.concatenate(gather_planes(own_share, cand_count)[1:])
     cat, send = fold(
         adj_values[0, 0],
         adj_source[0, 0],
@@ -708,17 +756,21 @@
         adj_relation[0, 0],
         live_blocks[0],
         want,
-        hold,
+        core[None],
         tiles,
         rel_rows,
     )
-    mine = jnp.take(want.reshape(plane_count, 2), core, axis=1)
-    theirs = jnp.take(their_want.reshape(plane_count, 2), core, axis=1)
-    *nodes_at, cat, send = lax.optimization_barrier((nodes, *nodes_at, cat, send))
-    mine, theirs = pick(plane[None], grp_index[None], mine, theirs, nodes_at, block)
+    stack, cat, send = lax.optimization_barrier((stack, cat, send))
+    nodes_at = [nodes, *gather_stacks(stack, share_rows, grp_count)]
+
+    mine, theirs = pick(
+        plane[None], grp_index[None], core[None], want, their_want, nodes_at, block
+    )
     theirs = swap_core(theirs, cand_count)
-    partial, partial_bf = forward(core[None], mine, theirs, cat, rel_emb, block)
-    own_agg = sum_over_grp(partial, partial_bf, grp_index, grp_count, share_rows).astype(BF)
+    own, *parts = forward(
+        core[None], grp_index[None], mine, theirs, cat, rel_emb, block, grp_count
+    )
+    own_agg = join([own, *swap_shares(parts, grp_count)], BF)
     agg_planes = gather_planes(own_agg, cand_count)
     agg_pieces = gather_pieces(agg_planes, 0, cand_count, grp_count)
 
@@ -746,15 +798,16 @@
     )
 
     other_h = swap_core(half_h, cand_count)
-    send, half_h = lax.optimization_barrier((send, half_h))
-    got = [
-        shift_planes(
-            lax.dynamic_index_in_dim(send, (plane + s) % plane_count, 0, keepdims=False),
-            s,
-            cand_count,
-        )
-        for s in range(1, plane_count)
-    ]
+
+    def send_to_plane(x, by):
+        part = lax.dynamic_index_in_dim(x, (plane + by) % plane_count, 0, keepdims=False)
+        return shift_planes(part, by, cand_count)
+
+    send_after = lax.optimization_barrier((send, half_h))[0]
+    got = [send_to_plane(send_after, by) for by in range(1, plane_count)]
+    first_row = plane * node_rows + grp_index * share_rows
+    h_own = lax.dynamic_slice_in_dim(half_h, first_row, share_rows, 0)
+    other_h, h_own = lax.optimization_barrier((other_h, h_own))
     gs, qg, qb, loss, *out_grad = score(half_h, other_h, rel_q, bias, meta, block, total_q)
     gs, *more = lax.optimization_barrier((gs, *out_grad, *got))
     out_grad, got = more[: len(out_grad)], more[len(out_grad) :]
@@ -767,12 +820,19 @@
     out_grad = out_grad[0] if out_grad else rows(half, gs, qb, qg, meta, other_h, "rows_other")
     in_grad = swap_core(out_grad, cand_count)
     own_grad = rows(0, gs, qb, qg, meta, half_h, "rows_own")
-    pre, agg_grad, mine, theirs = backward(
-        plane[None], own_grad, in_grad, half_d, w_in, send, got, tiles, block
-    )
-    mine = mine + swap_core(theirs, cand_count).astype(F32)
-    mine, pre, agg_grad = lax.optimization_barrier((mine, pre, agg_grad))
-    node_grad = sum_over_grp(mine, mine.astype(BF), grp_index, grp_count, share_rows)
+    pre, agg_grad, mine, theirs, self_grad = backward(
+        plane[None],
+        grp_index[None],
+        own_grad,
+        in_grad,
+        half_d,
+        w_in,
+        w_self,
+        send,
+        got,
+        tiles,
+        block,
+    )
     sums = sums_of_half(
         plane[None],
         pre,
@@ -781,14 +841,13 @@
         agg_grad,
         send,
         got,
-        2 * (block + MARK_ROWS),
+        2 * block,
         rel_rows,
     )
     gwin, gwself, grel = total_sums(sums, swap_core(sums, cand_count), rel_emb.shape[0])
-    first_row = plane * node_rows + grp_index * share_rows
-    own_pre = lax.dynamic_slice_in_dim(pre, first_row, share_rows, 0)
-    node_grad = node_grad + dot_nt(own_pre, w_self)
-    h_own = lax.dynamic_slice_in_dim(half_h, first_row, share_rows, 0)
+    own, *parts = merge(grp_index[None], mine, swap_core(theirs, cand_count), grp_count)
+    own, gwin, gwself, grel = lax.optimization_barrier((own, gwin, gwself, grel))
+    node_grad = join([own, self_grad, *swap_shares(parts, grp_count)], F32)
     return (
         h_own[None],
         loss,

time: 171 us -> 164 us (0.959)
  waiting for transfers between devices: 46.6 us -> 34.8 us
  Pallas kernels: 58.1 us -> 63.3 us
  starting transfers between devices: 42 us -> 44.2 us
  matrix products: 2.04 us -> 0 us
    ppermute x9, waiting for transfers between devices: 25.9 us -> 6.98 us  [shift_planes(): lax.ppermute(x, 'cand', [(i, (i + 2 * by) % cand_count) for i in range(ca...]
    ppermute x7, waiting for transfers between devices: 2.48 us -> 6.67 us  [swap_core(): return lax.ppermute(x, 'cand', [(i, i ^ 1) for i in range(cand_count)])]
    pallas_call x1 -> x4, Pallas kernels: 1.79 us -> 5.68 us  [the longest x1 2.99 us: forward(): pl.pallas_call(functools.partial(forward_kernel, block), grid_spec=pltpu....]
    ppermute x22, starting transfers between devices: 26.8 us -> 29.8 us  [swap_grp(): return lax.ppermute(x, 'grp', [(i, i ^ flip) for i in range(grp_count)])]
    ppermute x22, waiting for transfers between devices: 18.2 us -> 21.1 us  [swap_grp(): return lax.ppermute(x, 'grp', [(i, i ^ flip) for i in range(grp_count)])]
    dot_general x1 -> x0, matrix products: 2.04 us -> none  [dot_nt(): lax.dot_general(a, b, (((1,), (1,)), ((), ())), preferred_element_type=F32)]
    unnamed x81 -> x76, local copies, waits for them, and re-layouts: 5.54 us -> 5.13 us
  transfers between devices with their start and end apart: 38 -> 38, of which waited for: 18 -> 17; matrix products, arithmetic and copies ran while one was open for 8% -> 7% of each run, Pallas kernels for 20% -> 23%
where the time goes in v3:
time: 164 us; the launch traced here: 162 us
  Pallas kernels  63.3 us (39%)
  starting transfers between devices  44.2 us (27%)
  waiting for transfers between devices  34.8 us (21%)
  local copies, waits for them, and re-layouts  13.8 us (8%)
  other arithmetic  4.33 us (3%)
  between operations  1.84 us (1%)
    ppermute x22, starting transfers between devices, swap_grp(): return lax.ppermute(x, 'grp', [(i, i ^ flip) for i in range(grp_count)])  29.8 us
    pallas_call x1, Pallas kernels, score(): pl.pallas_call(functools.partial(score_kernel, block, min(512, half), tot...  21.5 us
    ppermute x22, waiting for transfers between devices, swap_grp(): return lax.ppermute(x, 'grp', [(i, i ^ flip) for i in range(grp_count)])  21.1 us
    ppermute x9, starting transfers between devices, shift_planes(): lax.ppermute(x, 'cand', [(i, (i + 2 * by) % cand_count) for i in range(ca...  13.7 us
    pallas_call x1, Pallas kernels, fold(): pl.pallas_call(functools.partial(fold_kernel, tiles, per), grid_spec=pltp...  8.4 us
    ppermute x9, waiting for transfers between devices, shift_planes(): lax.ppermute(x, 'cand', [(i, (i + 2 * by) % cand_count) for i in range(ca...  6.98 us
    pallas_call x1, Pallas kernels, activate(): pl.pallas_call(functools.partial(activate_kernel, planes, flips, cut), gr...  6.91 us
    ppermute x7, waiting for transfers between devices, swap_core(): return lax.ppermute(x, 'cand', [(i, i ^ 1) for i in range(cand_count)])  6.67 us
  transfers between devices with their start and end apart: 38, of which 17 were waited for; matrix products, arithmetic and copies ran while one was open for 7% of the time, Pallas kernels for 23%

profile of v3, /device:TPU:8, one launch (start us, length us, event | category | flops | bytes accessed | tf_op | source)
XLA Modules:
  0.0 162.2 jit_solution(61472258833165825)
XLA Ops:
  1.8 3.0 %collective-permute-start.2 = (bf16[128,512]{1,0:T(8,128)(2,1)S(1)}, bf16[128,512]{1,0:T(8,128)(2,1)S(1)}, u32[]{:S(2)}, u32[]{:S(2)}) collective-permute-start(bf16[128,512]{1,0:T(8,128)(2,1)S(1)} %dynamic-slice_bitcast_fusion.3), channel_id=1, source_target_pairs={{0,4},{1,5},{2,6},{3,7},{4,0},{5,1},{6,2},{7,3},{8,12},{9,13},{10,... | collective-permute-start | bytes 393224 | tf_op jit(solution)/shard_map/ppermute | solution.py:647
  4.8 2.5 %collective-permute-start.1 = (bf16[128,512]{1,0:T(8,128)(2,1)S(1)}, bf16[128,512]{1,0:T(8,128)(2,1)S(1)}, u32[]{:S(2)}, u32[]{:S(2)}) collective-permute-start(bf16[128,512]{1,0:T(8,128)(2,1)S(1)} %dynamic-slice_bitcast_fusion.3), channel_id=1, source_target_pairs={{0,2},{1,3},{2,4},{3,5},{4,6},{5,7},{6,0},{7,1},{8,10},{9,11},{10,... | collective-permute-start | bytes 393224 | tf_op jit(solution)/shard_map/ppermute | solution.py:647
  9.3 8.4 %fold_adjacency.1 = (bf16[512,2816]{1,0:T(8,128)(2,1)}, bf16[4,320,512]{2,1,0:T(8,128)(2,1)}) custom-call(s32[192]{0:T(256)} %bitcast.36, s32[192]{0:T(256)} %bitcast.32, s32[192]{0:T(256)} %bitcast.34, s32[1]{0:T(128)} %bitcast.26.live, s32[8]{0:T(128)} %bitcast.3.want.mine, s32[1]{0:T(128)} %bitcast.2.core, bf16[192,128,128]{2,1,0:T(8,128)(2,1)} %bitcast.35, ...), custom_call_target="tpu_custom_call" | custom-call | flops 8000000000 | bytes 8000000 | tf_op jit(solution)/shard_map/fold_adjacency/pallas_call | solution.py:112
  17.7 1.6 collective-permute-start.5
  20.8 7.0 %collective-permute-done.5.refs_3_.refs_19_ = bf16[384,512]{1,0:T(8,128)(2,1)S(1)} collective-permute-done((bf16[384,512]{1,0:T(8,128)(2,1)S(1)}, bf16[384,512]{1,0:T(8,128)(2,1)S(1)}, u32[]{:S(2)}, u32[]{:S(2)}) %collective-permute-start.5) | collective-permute-done | bytes 393248 | tf_op jit(solution)/shard_map/ppermute | solution.py:655
  33.5 2.5 %collective-permute-done.6.refs_4_.refs_20_ = bf16[128,512]{1,0:T(8,128)(2,1)} collective-permute-done((bf16[128,512]{1,0:T(8,128)(2,1)}, bf16[128,512]{1,0:T(8,128)(2,1)}, u32[]{:S(2)}, u32[]{:S(2)}) %collective-permute-start.6) | collective-permute-done | bytes 131104 | tf_op jit(solution)/shard_map/ppermute | solution.py:655
  36.1 3.4 %pick_mirrors.1 = (bf16[512,512]{1,0:T(8,128)(2,1)S(1)}, bf16[512,512]{1,0:T(8,128)(2,1)}) custom-call(s32[1]{0:T(128)} %bitcast.plane, s32[1]{0:T(128)} %bitcast.1.grp, s32[1]{0:T(128)} %bitcast.2.core, s32[8]{0:T(128)} %bitcast.3.want.mine, s32[8]{0:T(128)} %collective-permute-done.theirs, bf16[512,512]{1,0:T(8,128)(2,1)S(1)} %bitcast.28, ...), custom_call_target="tpu_custom_call" | custom-call | tf_op jit(solution)/shard_map/pick_mirrors/pallas_call | solution.py:175
  42.2 2.6 %gather_fusion = f32[512,512]{1,0:T(8,128)} fusion(f32[900,512]{1,0:T(8,128)S(1)} %copy-done, s32[1024]{0:T(1024)} %pad_clamp_fusion), kind=kCustom, calls=%fused_computation | custom fusion | bytes 2099200 | tf_op jit(solution)/shard_map/jit(_take)/gather | solution.py:784
  44.9 1.8 %copy-done.2 = bf16[512,2816]{1,0:T(8,128)(2,1)S(1)} copy-done((bf16[512,2816]{1,0:T(8,128)(2,1)S(1)}, bf16[512,2816]{1,0:T(8,128)(2,1)}, u32[]{:S(2)}) %copy-start.2) | copy-done | bytes 2883608
  47.7 3.0 %forward_partial.1 = (f32[128,512]{1,0:T(8,128)S(1)}, bf16[128,512]{1,0:T(8,128)(2,1)S(1)}, bf16[128,512]{1,0:T(8,128)(2,1)S(1)}, bf16[128,512]{1,0:T(8,128)(2,1)S(1)}) custom-call(s32[1]{0:T(128)} %bitcast.2.core, s32[1]{0:T(128)} %bitcast.1.grp, bf16[512,512]{1,0:T(8,128)(2,1)S(1)} %copy-done.9, bf16[512,512]{1,0:T(8,128)(2,1)} %collective-permute-done.8.theirs_ref, ...), custom_call_target="tpu_custom_call" | custom-call | tf_op jit(solution)/shard_map/forward_partial/pallas_call | solution.py:265
  54.4 2.7 %collective-permute-done.9.refs_1_ = bf16[128,512]{1,0:T(8,128)(2,1)S(1)} collective-permute-done((bf16[128,512]{1,0:T(8,128)(2,1)S(1)}, bf16[128,512]{1,0:T(8,128)(2,1)S(1)}, u32[]{:S(2)}, u32[]{:S(2)}) %collective-permute-start.9) | collective-permute-done | bytes 131104 | tf_op jit(solution)/shard_map/ppermute | solution.py:655
  57.1 2.0 %collective-permute-done.10.refs_2_ = bf16[128,512]{1,0:T(8,128)(2,1)S(1)} collective-permute-done((bf16[128,512]{1,0:T(8,128)(2,1)S(1)}, bf16[128,512]{1,0:T(8,128)(2,1)S(1)}, u32[]{:S(2)}, u32[]{:S(2)}) %collective-permute-start.10) | collective-permute-done | bytes 131104 | tf_op jit(solution)/shard_map/ppermute | solution.py:655
  64.5 1.8 %collective-permute-start.23 = (bf16[128,512]{1,0:T(8,128)(2,1)S(1)}, bf16[128,512]{1,0:T(8,128)(2,1)S(1)}, u32[]{:S(2)}, u32[]{:S(2)}) collective-permute-start(bf16[128,512]{1,0:T(8,128)(2,1)S(1)} %join_group.2.refs_0_), channel_id=1, source_target_pairs={{0,6},{1,7},{2,0},{3,1},{4,2},{5,3},{6,4},{7,5},{8,14},{9,15},{10,... | collective-permute-start | bytes 393224 | tf_op jit(solution)/shard_map/ppermute | solution.py:647
  66.4 3.0 %collective-permute-done.15.refs_4_ = bf16[128,512]{1,0:T(8,128)(2,1)S(1)} collective-permute-done((bf16[128,512]{1,0:T(8,128)(2,1)S(1)}, bf16[128,512]{1,0:T(8,128)(2,1)S(1)}, u32[]{:S(2)}, u32[]{:S(2)}) %collective-permute-start.15) | collective-permute-done | bytes 131104 | tf_op jit(solution)/shard_map/ppermute | solution.py:647
  69.3 4.0 %collective-permute-start.16 = (bf16[128,512]{1,0:T(8,128)(2,1)S(1)}, bf16[128,512]{1,0:T(8,128)(2,1)S(1)}, u32[]{:S(2)}, u32[]{:S(2)}) collective-permute-start(bf16[128,512]{1,0:T(8,128)(2,1)S(1)} %collective-permute-done.15.refs_4_), channel_id=1, source_target_pairs={{0,8},{8,0},{16,24},{24,16},{1,9},{9,1},{17,25},{25,17},{2,10},{10... | collective-permute-start | bytes 393224 | tf_op jit(solution)/shard_map/ppermute | solution.py:655
  73.5 2.0 %collective-permute-start.14 = (bf16[128,512]{1,0:T(8,128)(2,1)S(1)}, bf16[128,512]{1,0:T(8,128)(2,1)S(1)}, u32[]{:S(2)}, u32[]{:S(2)}) collective-permute-start(bf16[128,512]{1,0:T(8,128)(2,1)S(1)} %collective-permute-done.13.refs_2_), channel_id=1, source_target_pairs={{0,8},{8,0},{16,24},{24,16},{1,9},{9,1},{17,25},{25,17},{2,10},{10... | collective-permute-start | bytes 393224 | tf_op jit(solution)/shard_map/ppermute | solution.py:655
  75.5 1.9 %collective-permute-start.24 = (bf16[128,512]{1,0:T(8,128)(2,1)S(1)}, bf16[128,512]{1,0:T(8,128)(2,1)S(1)}, u32[]{:S(2)}, u32[]{:S(2)}) collective-permute-start(bf16[128,512]{1,0:T(8,128)(2,1)S(1)} %collective-permute-done.23.refs_12_), channel_id=1, source_target_pairs={{0,8},{8,0},{16,24},{24,16},{1,9},{9,1},{17,25},{25,17},{2,10},{10... | collective-permute-start | bytes 393224 | tf_op jit(solution)/shard_map/ppermute | solution.py:655
  77.5 2.1 %collective-permute-done.14.refs_3_ = bf16[128,512]{1,0:T(8,128)(2,1)S(1)} collective-permute-done((bf16[128,512]{1,0:T(8,128)(2,1)S(1)}, bf16[128,512]{1,0:T(8,128)(2,1)S(1)}, u32[]{:S(2)}, u32[]{:S(2)}) %collective-permute-start.14) | collective-permute-done | bytes 131104 | tf_op jit(solution)/shard_map/ppermute | solution.py:655
  79.5 2.3 %collective-permute-start.20 = (bf16[128,512]{1,0:T(8,128)(2,1)S(1)}, bf16[128,512]{1,0:T(8,128)(2,1)S(1)}, u32[]{:S(2)}, u32[]{:S(2)}) collective-permute-start(bf16[128,512]{1,0:T(8,128)(2,1)S(1)} %collective-permute-done.19.refs_8_), channel_id=1, source_target_pairs={{0,8},{8,0},{16,24},{24,16},{1,9},{9,1},{17,25},{25,17},{2,10},{10... | collective-permute-start | bytes 393224 | tf_op jit(solution)/shard_map/ppermute | solution.py:655
  81.9 2.0 %collective-permute-start.18 = (bf16[128,512]{1,0:T(8,128)(2,1)S(1)}, bf16[128,512]{1,0:T(8,128)(2,1)S(1)}, u32[]{:S(2)}, u32[]{:S(2)}) collective-permute-start(bf16[128,512]{1,0:T(8,128)(2,1)S(1)} %collective-permute-done.16.refs_5_), channel_id=1, source_target_pairs={{0,16},{8,24},{16,0},{24,8},{1,17},{9,25},{17,1},{25,9},{2,18},{10... | collective-permute-start | bytes 393224 | tf_op jit(solution)/shard_map/ppermute | solution.py:655
  84.0 1.9 %collective-permute-start.26 = (bf16[128,512]{1,0:T(8,128)(2,1)S(1)}, bf16[128,512]{1,0:T(8,128)(2,1)}, u32[]{:S(2)}, u32[]{:S(2)}) collective-permute-start(bf16[128,512]{1,0:T(8,128)(2,1)S(1)} %collective-permute-done.24.refs_13_), channel_id=1, source_target_pairs={{0,16},{8,24},{16,0},{24,8},{1,17},{9,25},{17,1},{25,9},{2,18},{10... | collective-permute-start | bytes 393224 | tf_op jit(solution)/shard_map/ppermute | solution.py:655
  89.8 6.9 %activate.1 = (bf16[2048,512]{1,0:T(8,128)(2,1)}, bf16[2048,512]{1,0:T(8,128)(2,1)}, bf16[2048,512]{1,0:T(8,128)(2,1)}, bf16[2048,512]{1,0:T(8,128)(2,1)}) custom-call(s32[1]{0:T(128)} %bitcast.plane, s32[1]{0:T(128)} %bitcast.1.grp, bf16[512,512]{1,0:T(8,128)(2,1)} %refs_0_.1, bf16[512,512]{1,0:T(8,128)(2,1)} %refs_1_.1, bf16[128,512]{1,0:T(8,128)(2,1)} %copy-done.10, ...), custom_call_target="tpu_custom_call" | custom-call | tf_op jit(solution)/shard_map/activate/pallas_call | solution.py:326
  98.2 3.2 %collective-permute-start.29 = (bf16[320,512]{1,0:T(8,128)(2,1)S(1)}, bf16[320,512]{1,0:T(8,128)(2,1)S(1)}, u32[]{:S(2)}, u32[]{:S(2)}) collective-permute-start(bf16[320,512]{1,0:T(8,128)(2,1)S(1)} %get-tuple-element.136), channel_id=1, source_target_pairs={{0,2},{1,3},{2,4},{3,5},{4,6},{5,7},{6,0},{7,1},{8,10},{9,11},{10,... | collective-permute-start | bytes 983048 | tf_op jit(solution)/shard_map/ppermute | solution.py:647
  103.0 1.6 constant_dynamic-slice_fusion
  104.6 21.5 %score.1 = (bf16[4096,512]{1,0:T(8,128)(2,1)S(1)}, bf16[512,512]{1,0:T(8,128)(2,1)S(1)}, bf16[512,512]{1,0:T(8,128)(2,1)S(1)}, f32[1,512]{1,0:T(1,128)}, bf16[2048,512]{1,0:T(8,128)(2,1)S(1)}) custom-call(bf16[2048,512]{1,0:T(8,128)(2,1)S(1)} %copy-done.5, bf16[2048,512]{1,0:T(8,128)(2,1)} %collective-permute-done.27.other_ref, ...), custom_call_target="tpu_custom_call" | custom-call | flops 60000002048 | bytes 60000000 | tf_op jit(solution)/shard_map/score/pallas_call | solution.py:447
  126.1 4.0 %collective-permute-done.30.refs_4_.refs_1_ = bf16[320,512]{1,0:T(8,128)(2,1)S(1)} collective-permute-done((bf16[320,512]{1,0:T(8,128)(2,1)S(1)}, bf16[320,512]{1,0:T(8,128)(2,1)S(1)}, u32[]{:S(2)}, u32[]{:S(2)}) %collective-permute-start.30) | collective-permute-done | bytes 327712 | tf_op jit(solution)/shard_map/ppermute | solution.py:647
  130.2 3.5 %rows_own.1.own_ref = bf16[2048,512]{1,0:T(8,128)(2,1)S(1)} custom-call(bf16[4096,512]{1,0:T(8,128)(2,1)S(1)} %get-tuple-element.106.gs_ref, bf16[512,512]{1,0:T(8,128)(2,1)S(1)} %get-tuple-element.107.qb_ref, bf16[512,512]{1,0:T(8,128)(2,1)S(1)} %get-tuple-element.108.qg_ref, s32[16,512]{1,0:T(8,128)S(1)} %pad_add_fusion.meta_ref, ...), custom_call_target="tpu_custom_call" | custom-call | tf_op jit(solution)/shard_map/rows_own/pallas_call | solution.py:489
  134.3 4.8 %backward_rows.1 = (bf16[2048,512]{1,0:T(8,128)(2,1)S(1)}, bf16[2048,512]{1,0:T(8,128)(2,1)S(1)}, f32[512,512]{1,0:T(8,128)S(1)}, bf16[512,512]{1,0:T(8,128)(2,1)S(1)}, f32[128,512]{1,0:T(8,128)S(1)}) custom-call(s32[1]{0:T(128)} %bitcast.plane, s32[1]{0:T(128)} %bitcast.1.grp, bf16[2048,512]{1,0:T(8,128)(2,1)S(1)} %rows_own.1.own_ref, ...), custom_call_target="tpu_custom_call" | custom-call | flops 6000000000 | bytes 6000000 | tf_op jit(solution)/shard_map/backward_rows/pallas_call | solution.py:553
  139.1 6.3 %sums_of_half.1.a_ref = bf16[1280,512]{1,0:T(8,128)(2,1)S(1)} custom-call(s32[1]{0:T(128)} %bitcast.plane, bf16[2048,512]{1,0:T(8,128)(2,1)S(1)} %get-tuple-element.117.pre_ref, bf16[2048,512]{1,0:T(8,128)(2,1)S(1)} %copy-done.16, bf16[2048,512]{1,0:T(8,128)(2,1)S(1)} %copy-done.17, bf16[2048,512]{1,0:T(8,128)(2,1)S(1)} %get-tuple-element.120.agg_grad_ref, ...), custom_call_target="tpu_custom_call" | custom-call | flops 20000000000 | bytes 20000000 | tf_op jit(solution)/shard_map/sums_of_half/pallas_call | solution.py:625
  146.0 3.3 %collective-permute-done.33.theirs_ref = bf16[512,512]{1,0:T(8,128)(2,1)S(1)} collective-permute-done((bf16[512,512]{1,0:T(8,128)(2,1)S(1)}, bf16[512,512]{1,0:T(8,128)(2,1)S(1)}, u32[]{:S(2)}, u32[]{:S(2)}) %collective-permute-start.33) | collective-permute-done | bytes 524320 | tf_op jit(solution)/shard_map/ppermute | solution.py:651
  157.2 2.9 %total_sums.1 = (f32[512,512]{1,0:T(8,128)}, f32[512,512]{1,0:T(8,128)}, f32[225,512]{1,0:T(8,128)}) custom-call(bf16[1280,512]{1,0:T(8,128)(2,1)S(1)} %sums_of_half.1.a_ref, bf16[1280,512]{1,0:T(8,128)(2,1)} %collective-permute-done.34.b_ref), custom_call_target="tpu_custom_call" | custom-call | tf_op jit(solution)/shard_map/total_sums/pallas_call | solution.py:669
  160.5 1.7 %join_group.3 = f32[128,512]{1,0:T(8,128)} custom-call(f32[128,512]{1,0:T(8,128)S(1)} %copy-done.15, f32[128,512]{1,0:T(8,128)S(1)} %get-tuple-element.125.refs_1_, bf16[128,512]{1,0:T(8,128)(2,1)S(1)} %collective-permute-done.35.refs_2_, bf16[128,512]{1,0:T(8,128)(2,1)} %collective-permute-done.36.refs_3_, bf16[128,512]{1,0:T(8,128)(2,1)} %collective-permute-done.37.refs_4_), custom_call_target="tpu_custom_call" | custom-call | tf_op jit(solution)/shard_map/join_group/pallas_call | solution.py:250
  (152 shorter events, 39.4 us)
Async XLA Ops:
  1.7 16.0 %collective-permute-start.3 = (bf16[128,512]{1,0:T(8,128)(2,1)S(1)}, bf16[128,512]{1,0:T(8,128)(2,1)S(1)}, u32[]{:S(2)}, u32[]{:S(2)}) collective-permute-start(bf16[128,512]{1,0:T(8,128)(2,1)S(1)} %dynamic-slice_bitcast_fusion.3), channel_id=1, source_target_pairs={{0,6},{1,7},{2,0},{3,1},{4,2},{5,3},{6,4},{7,5},{8,14},{9,15},{10,... | collective-permute-start | bytes 393224 | tf_op jit(solution)/shard_map/ppermute | solution.py:647
  1.8 15.9 %collective-permute-start.2 = (bf16[128,512]{1,0:T(8,128)(2,1)S(1)}, bf16[128,512]{1,0:T(8,128)(2,1)S(1)}, u32[]{:S(2)}, u32[]{:S(2)}) collective-permute-start(bf16[128,512]{1,0:T(8,128)(2,1)S(1)} %dynamic-slice_bitcast_fusion.3), channel_id=1, source_target_pairs={{0,4},{1,5},{2,6},{3,7},{4,0},{5,1},{6,2},{7,3},{8,12},{9,13},{10,... | collective-permute-start | bytes 393224 | tf_op jit(solution)/shard_map/ppermute | solution.py:647
  4.8 12.9 %collective-permute-start.1 = (bf16[128,512]{1,0:T(8,128)(2,1)S(1)}, bf16[128,512]{1,0:T(8,128)(2,1)S(1)}, u32[]{:S(2)}, u32[]{:S(2)}) collective-permute-start(bf16[128,512]{1,0:T(8,128)(2,1)S(1)} %dynamic-slice_bitcast_fusion.3), channel_id=1, source_target_pairs={{0,2},{1,3},{2,4},{3,5},{4,6},{5,7},{6,0},{7,1},{8,10},{9,11},{10,... | collective-permute-start | bytes 393224 | tf_op jit(solution)/shard_map/ppermute | solution.py:647
  17.7 10.1 %collective-permute-start.5 = (bf16[384,512]{1,0:T(8,128)(2,1)S(1)}, bf16[384,512]{1,0:T(8,128)(2,1)S(1)}, u32[]{:S(2)}, u32[]{:S(2)}) collective-permute-start(bf16[384,512]{1,0:T(8,128)(2,1)S(1)} %pad_maximum_fusion.refs_1_.refs_17_), channel_id=1, source_target_pairs={{0,16},{8,24},{16,0},{24,8},{1,17},{9,25},{17,1},{25,9},{2,18},{10... | collective-permute-start | bytes 1179656 | tf_op jit(solution)/shard_map/ppermute | solution.py:655
  19.3 10.7 %collective-permute-start.4 = (bf16[384,512]{1,0:T(8,128)(2,1)S(1)}, bf16[384,512]{1,0:T(8,128)(2,1)S(1)}, u32[]{:S(2)}, u32[]{:S(2)}) collective-permute-start(bf16[384,512]{1,0:T(8,128)(2,1)S(1)} %pad_maximum_fusion.refs_1_.refs_17_), channel_id=1, source_target_pairs={{0,8},{8,0},{16,24},{24,16},{1,9},{9,1},{17,25},{25,17},{2,10},{10... | collective-permute-start | bytes 1179656 | tf_op jit(solution)/shard_map/ppermute | solution.py:655
  28.6 7.5 %collective-permute-start.7 = (bf16[256,512]{1,0:T(8,128)(2,1)}, bf16[256,512]{1,0:T(8,128)(2,1)}, u32[]{:S(2)}, u32[]{:S(2)}) collective-permute-start(bf16[256,512]{1,0:T(8,128)(2,1)} %slice.11), channel_id=1, source_target_pairs={{0,8},{8,0},{16,24},{24,16},{1,9},{9,1},{17,25},{25,17},{2,10},{10... | collective-permute-start | bytes 786440 | tf_op jit(solution)/shard_map/ppermute | solution.py:655
  30.8 5.3 %collective-permute-start.6 = (bf16[128,512]{1,0:T(8,128)(2,1)}, bf16[128,512]{1,0:T(8,128)(2,1)}, u32[]{:S(2)}, u32[]{:S(2)}) collective-permute-start(bf16[128,512]{1,0:T(8,128)(2,1)} %slice.10), channel_id=1, source_target_pairs={{0,16},{8,24},{16,0},{24,8},{1,17},{9,25},{17,1},{25,9},{2,18},{10... | collective-permute-start | bytes 393224 | tf_op jit(solution)/shard_map/ppermute | solution.py:655
  50.7 6.4 %collective-permute-start.9 = (bf16[128,512]{1,0:T(8,128)(2,1)S(1)}, bf16[128,512]{1,0:T(8,128)(2,1)S(1)}, u32[]{:S(2)}, u32[]{:S(2)}) collective-permute-start(bf16[128,512]{1,0:T(8,128)(2,1)S(1)} %get-tuple-element.76), channel_id=1, source_target_pairs={{0,8},{8,0},{16,24},{24,16},{1,9},{9,1},{17,25},{25,17},{2,10},{10... | collective-permute-start | bytes 393224 | tf_op jit(solution)/shard_map/ppermute | solution.py:655
  51.6 7.5 %collective-permute-start.10 = (bf16[128,512]{1,0:T(8,128)(2,1)S(1)}, bf16[128,512]{1,0:T(8,128)(2,1)S(1)}, u32[]{:S(2)}, u32[]{:S(2)}) collective-permute-start(bf16[128,512]{1,0:T(8,128)(2,1)S(1)} %get-tuple-element.77), channel_id=1, source_target_pairs={{0,16},{8,24},{16,0},{24,8},{1,17},{9,25},{17,1},{25,9},{2,18},{10... | collective-permute-start | bytes 393224 | tf_op jit(solution)/shard_map/ppermute | solution.py:655
  53.1 7.3 %collective-permute-start.11 = (bf16[128,512]{1,0:T(8,128)(2,1)S(1)}, bf16[128,512]{1,0:T(8,128)(2,1)S(1)}, u32[]{:S(2)}, u32[]{:S(2)}) collective-permute-start(bf16[128,512]{1,0:T(8,128)(2,1)S(1)} %get-tuple-element.78), channel_id=1, source_target_pairs={{0,24},{8,16},{16,8},{24,0},{1,25},{9,17},{17,9},{25,1},{2,26},{10... | collective-permute-start | bytes 393224 | tf_op jit(solution)/shard_map/ppermute | solution.py:655
  60.5 12.9 %collective-permute-start.12 = (bf16[128,512]{1,0:T(8,128)(2,1)S(1)}, bf16[128,512]{1,0:T(8,128)(2,1)S(1)}, u32[]{:S(2)}, u32[]{:S(2)}) collective-permute-start(bf16[128,512]{1,0:T(8,128)(2,1)S(1)} %join_group.2.refs_0_), channel_id=1, source_target_pairs={{0,8},{8,0},{16,24},{24,16},{1,9},{9,1},{17,25},{25,17},{2,10},{10... | collective-permute-start | bytes 393224 | tf_op jit(solution)/shard_map/ppermute | solution.py:655
  61.4 12.1 %collective-permute-start.13 = (bf16[128,512]{1,0:T(8,128)(2,1)S(1)}, bf16[128,512]{1,0:T(8,128)(2,1)S(1)}, u32[]{:S(2)}, u32[]{:S(2)}) collective-permute-start(bf16[128,512]{1,0:T(8,128)(2,1)S(1)} %join_group.2.refs_0_), channel_id=1, source_target_pairs={{0,16},{8,24},{16,0},{24,8},{1,17},{9,25},{17,1},{25,9},{2,18},{10... | collective-permute-start | bytes 393224 | tf_op jit(solution)/shard_map/ppermute | solution.py:655
  62.9 6.4 %collective-permute-start.15 = (bf16[128,512]{1,0:T(8,128)(2,1)S(1)}, bf16[128,512]{1,0:T(8,128)(2,1)S(1)}, u32[]{:S(2)}, u32[]{:S(2)}) collective-permute-start(bf16[128,512]{1,0:T(8,128)(2,1)S(1)} %join_group.2.refs_0_), channel_id=1, source_target_pairs={{0,2},{1,3},{2,4},{3,5},{4,6},{5,7},{6,0},{7,1},{8,10},{9,11},{10,... | collective-permute-start | bytes 393224 | tf_op jit(solution)/shard_map/ppermute | solution.py:647
  63.2 12.3 %collective-permute-start.19 = (bf16[128,512]{1,0:T(8,128)(2,1)S(1)}, bf16[128,512]{1,0:T(8,128)(2,1)S(1)}, u32[]{:S(2)}, u32[]{:S(2)}) collective-permute-start(bf16[128,512]{1,0:T(8,128)(2,1)S(1)} %join_group.2.refs_0_), channel_id=1, source_target_pairs={{0,4},{1,5},{2,6},{3,7},{4,0},{5,1},{6,2},{7,3},{8,12},{9,13},{10,... | collective-permute-start | bytes 393224 | tf_op jit(solution)/shard_map/ppermute | solution.py:647
  64.5 11.1 %collective-permute-start.23 = (bf16[128,512]{1,0:T(8,128)(2,1)S(1)}, bf16[128,512]{1,0:T(8,128)(2,1)S(1)}, u32[]{:S(2)}, u32[]{:S(2)}) collective-permute-start(bf16[128,512]{1,0:T(8,128)(2,1)S(1)} %join_group.2.refs_0_), channel_id=1, source_target_pairs={{0,6},{1,7},{2,0},{3,1},{4,2},{5,3},{6,4},{7,5},{8,14},{9,15},{10,... | collective-permute-start | bytes 393224 | tf_op jit(solution)/shard_map/ppermute | solution.py:647
  69.3 12.5 %collective-permute-start.16 = (bf16[128,512]{1,0:T(8,128)(2,1)S(1)}, bf16[128,512]{1,0:T(8,128)(2,1)S(1)}, u32[]{:S(2)}, u32[]{:S(2)}) collective-permute-start(bf16[128,512]{1,0:T(8,128)(2,1)S(1)} %collective-permute-done.15.refs_4_), channel_id=1, source_target_pairs={{0,8},{8,0},{16,24},{24,16},{1,9},{9,1},{17,25},{25,17},{2,10},{10... | collective-permute-start | bytes 393224 | tf_op jit(solution)/shard_map/ppermute | solution.py:655
  73.4 8.5 %collective-permute-start.17 = (bf16[128,512]{1,0:T(8,128)(2,1)S(1)}, bf16[128,512]{1,0:T(8,128)(2,1)S(1)}, u32[]{:S(2)}, u32[]{:S(2)}) collective-permute-start(bf16[128,512]{1,0:T(8,128)(2,1)S(1)} %collective-permute-done.15.refs_4_), channel_id=1, source_target_pairs={{0,16},{8,24},{16,0},{24,8},{1,17},{9,25},{17,1},{25,9},{2,18},{10... | collective-permute-start | bytes 393224 | tf_op jit(solution)/shard_map/ppermute | solution.py:655
  73.5 6.0 %collective-permute-start.14 = (bf16[128,512]{1,0:T(8,128)(2,1)S(1)}, bf16[128,512]{1,0:T(8,128)(2,1)S(1)}, u32[]{:S(2)}, u32[]{:S(2)}) collective-permute-start(bf16[128,512]{1,0:T(8,128)(2,1)S(1)} %collective-permute-done.13.refs_2_), channel_id=1, source_target_pairs={{0,8},{8,0},{16,24},{24,16},{1,9},{9,1},{17,25},{25,17},{2,10},{10... | collective-permute-start | bytes 393224 | tf_op jit(solution)/shard_map/ppermute | solution.py:655
  75.5 8.4 %collective-permute-start.21 = (bf16[128,512]{1,0:T(8,128)(2,1)S(1)}, bf16[128,512]{1,0:T(8,128)(2,1)S(1)}, u32[]{:S(2)}, u32[]{:S(2)}) collective-permute-start(bf16[128,512]{1,0:T(8,128)(2,1)S(1)} %collective-permute-done.19.refs_8_), channel_id=1, source_target_pairs={{0,16},{8,24},{16,0},{24,8},{1,17},{9,25},{17,1},{25,9},{2,18},{10... | collective-permute-start | bytes 393224 | tf_op jit(solution)/shard_map/ppermute | solution.py:655
  75.5 8.4 %collective-permute-start.24 = (bf16[128,512]{1,0:T(8,128)(2,1)S(1)}, bf16[128,512]{1,0:T(8,128)(2,1)S(1)}, u32[]{:S(2)}, u32[]{:S(2)}) collective-permute-start(bf16[128,512]{1,0:T(8,128)(2,1)S(1)} %collective-permute-done.23.refs_12_), channel_id=1, source_target_pairs={{0,8},{8,0},{16,24},{24,16},{1,9},{9,1},{17,25},{25,17},{2,10},{10... | collective-permute-start | bytes 393224 | tf_op jit(solution)/shard_map/ppermute | solution.py:655
  79.5 6.4 %collective-permute-start.20 = (bf16[128,512]{1,0:T(8,128)(2,1)S(1)}, bf16[128,512]{1,0:T(8,128)(2,1)S(1)}, u32[]{:S(2)}, u32[]{:S(2)}) collective-permute-start(bf16[128,512]{1,0:T(8,128)(2,1)S(1)} %collective-permute-done.19.refs_8_), channel_id=1, source_target_pairs={{0,8},{8,0},{16,24},{24,16},{1,9},{9,1},{17,25},{25,17},{2,10},{10... | collective-permute-start | bytes 393224 | tf_op jit(solution)/shard_map/ppermute | solution.py:655
  81.9 6.3 %collective-permute-start.18 = (bf16[128,512]{1,0:T(8,128)(2,1)S(1)}, bf16[128,512]{1,0:T(8,128)(2,1)S(1)}, u32[]{:S(2)}, u32[]{:S(2)}) collective-permute-start(bf16[128,512]{1,0:T(8,128)(2,1)S(1)} %collective-permute-done.16.refs_5_), channel_id=1, source_target_pairs={{0,16},{8,24},{16,0},{24,8},{1,17},{9,25},{17,1},{25,9},{2,18},{10... | collective-permute-start | bytes 393224 | tf_op jit(solution)/shard_map/ppermute | solution.py:655
  83.9 5.0 %collective-permute-start.22 = (bf16[128,512]{1,0:T(8,128)(2,1)S(1)}, bf16[128,512]{1,0:T(8,128)(2,1)S(1)}, u32[]{:S(2)}, u32[]{:S(2)}) collective-permute-start(bf16[128,512]{1,0:T(8,128)(2,1)S(1)} %collective-permute-done.21.refs_10_), channel_id=1, source_target_pairs={{0,8},{8,0},{16,24},{24,16},{1,9},{9,1},{17,25},{25,17},{2,10},{10... | collective-permute-start | bytes 393224 | tf_op jit(solution)/shard_map/ppermute | solution.py:655
  84.0 5.8 %collective-permute-start.26 = (bf16[128,512]{1,0:T(8,128)(2,1)S(1)}, bf16[128,512]{1,0:T(8,128)(2,1)}, u32[]{:S(2)}, u32[]{:S(2)}) collective-permute-start(bf16[128,512]{1,0:T(8,128)(2,1)S(1)} %collective-permute-done.24.refs_13_), channel_id=1, source_target_pairs={{0,16},{8,24},{16,0},{24,8},{1,17},{9,25},{17,1},{25,9},{2,18},{10... | collective-permute-start | bytes 393224 | tf_op jit(solution)/shard_map/ppermute | solution.py:655
  96.7 7.9 %collective-permute-start.27 = (bf16[2048,512]{1,0:T(8,128)(2,1)}, bf16[2048,512]{1,0:T(8,128)(2,1)}, u32[]{:S(2)}, u32[]{:S(2)}) collective-permute-start(bf16[2048,512]{1,0:T(8,128)(2,1)} %get-tuple-element.95.own_ref.h_ref), channel_id=1, source_target_pairs={{0,1},{1,0},{2,3},{3,2},{4,5},{5,4},{6,7},{7,6},{8,9},{9,8},{10,11... | collective-permute-start | bytes 6291464 | tf_op jit(solution)/shard_map/ppermute | solution.py:651
  98.2 27.9 %collective-permute-start.29 = (bf16[320,512]{1,0:T(8,128)(2,1)S(1)}, bf16[320,512]{1,0:T(8,128)(2,1)S(1)}, u32[]{:S(2)}, u32[]{:S(2)}) collective-permute-start(bf16[320,512]{1,0:T(8,128)(2,1)S(1)} %get-tuple-element.136), channel_id=1, source_target_pairs={{0,2},{1,3},{2,4},{3,5},{4,6},{5,7},{6,0},{7,1},{8,10},{9,11},{10,... | collective-permute-start | bytes 983048 | tf_op jit(solution)/shard_map/ppermute | solution.py:647
  101.5 28.6 %collective-permute-start.30 = (bf16[320,512]{1,0:T(8,128)(2,1)S(1)}, bf16[320,512]{1,0:T(8,128)(2,1)S(1)}, u32[]{:S(2)}, u32[]{:S(2)}) collective-permute-start(bf16[320,512]{1,0:T(8,128)(2,1)S(1)} %get-tuple-element.135), channel_id=1, source_target_pairs={{0,4},{1,5},{2,6},{3,7},{4,0},{5,1},{6,2},{7,3},{8,12},{9,13},{10,... | collective-permute-start | bytes 983048 | tf_op jit(solution)/shard_map/ppermute | solution.py:647
  101.5 28.6 %collective-permute-start.31 = (bf16[320,512]{1,0:T(8,128)(2,1)S(1)}, bf16[320,512]{1,0:T(8,128)(2,1)S(1)}, u32[]{:S(2)}, u32[]{:S(2)}) collective-permute-start(bf16[320,512]{1,0:T(8,128)(2,1)S(1)} %get-tuple-element.134), channel_id=1, source_target_pairs={{0,6},{1,7},{2,0},{3,1},{4,2},{5,3},{6,4},{7,5},{8,14},{9,15},{10,... | collective-permute-start | bytes 983048 | tf_op jit(solution)/shard_map/ppermute | solution.py:647
  145.4 11.8 %collective-permute-start.34 = (bf16[1280,512]{1,0:T(8,128)(2,1)S(1)}, bf16[1280,512]{1,0:T(8,128)(2,1)}, u32[]{:S(2)}, u32[]{:S(2)}) collective-permute-start(bf16[1280,512]{1,0:T(8,128)(2,1)S(1)} %sums_of_half.1.a_ref), channel_id=1, source_target_pairs={{0,1},{1,0},{2,3},{3,2},{4,5},{5,4},{6,7},{7,6},{8,9},{9,8},{10,11... | collective-permute-start | bytes 3932168 | tf_op jit(solution)/shard_map/ppermute | solution.py:651
  150.9 9.2 %collective-permute-start.35 = (bf16[128,512]{1,0:T(8,128)(2,1)}, bf16[128,512]{1,0:T(8,128)(2,1)S(1)}, u32[]{:S(2)}, u32[]{:S(2)}) collective-permute-start(bf16[128,512]{1,0:T(8,128)(2,1)} %get-tuple-element.126), channel_id=1, source_target_pairs={{0,8},{8,0},{16,24},{24,16},{1,9},{9,1},{17,25},{25,17},{2,10},{10... | collective-permute-start | bytes 393224 | tf_op jit(solution)/shard_map/ppermute | solution.py:655
  152.1 8.4 %collective-permute-start.36 = (bf16[128,512]{1,0:T(8,128)(2,1)}, bf16[128,512]{1,0:T(8,128)(2,1)}, u32[]{:S(2)}, u32[]{:S(2)}) collective-permute-start(bf16[128,512]{1,0:T(8,128)(2,1)} %get-tuple-element.127), channel_id=1, source_target_pairs={{0,16},{8,24},{16,0},{24,8},{1,17},{9,25},{17,1},{25,9},{2,18},{10... | collective-permute-start | bytes 393224 | tf_op jit(solution)/shard_map/ppermute | solution.py:655
  152.9 7.6 %collective-permute-start.37 = (bf16[128,512]{1,0:T(8,128)(2,1)}, bf16[128,512]{1,0:T(8,128)(2,1)}, u32[]{:S(2)}, u32[]{:S(2)}) collective-permute-start(bf16[128,512]{1,0:T(8,128)(2,1)} %get-tuple-element.128), channel_id=1, source_target_pairs={{0,24},{8,16},{16,8},{24,0},{1,25},{9,17},{17,9},{25,1},{2,26},{10... | collective-permute-start | bytes 393224 | tf_op jit(solution)/shard_map/ppermute | solution.py:655
  (44 other events, 444.6 us)

commit v4 on v3

--- a/solution.py
+++ b/solution.py
@@ -216,29 +216,6 @@
     return [((rows // flips, width), BF if flip else F32) for flip in range(flips)]
 
 
-def merge_kernel(grp, mine_ref, theirs_ref, *refs):
-    *share_refs, total = refs
-    total[...] = mine_ref[...] + theirs_ref[...].astype(F32)
-    put_shares(total, grp[0], share_refs)
-
-
-def merge(grp, mine, theirs, flips):
-    outs = share_shapes(*mine.shape, flips)
-    return pl.pallas_call(
-        merge_kernel,
-        grid_spec=pltpu.PrefetchScalarGridSpec(
-            num_scalar_prefetch=1,
-            grid=(1,),
-            in_specs=[fixed(mine.shape), fixed(theirs.shape)],
-            out_specs=[fixed(x) for x, _ in outs],
-            scratch_shapes=[pltpu.VMEM(mine.shape, F32)],
-        ),
-        out_shape=shaped(*outs),
-        compiler_params=params(True, 8),
-        name="merge_cores",
-    )(grp, mine, theirs)
-
-
 def join_kernel(*refs):
     total = refs[0][...]
     for ref in refs[1:-1]:
@@ -281,7 +258,7 @@
     agg_pieces = refs[: planes * flips]
     sources = refs[planes * flips : planes * flips + 6]
     outs = refs[planes * flips + 6 : planes * flips + 10]
-    *held, sems = refs[planes * flips + 10 :]
+    own_ref, *held, sems = refs[planes * flips + 10 :]
     agg_ref, node_ref, h_ref, d_ref = held
     rows = sources[0].shape[0]
     block = rows // flips
@@ -312,6 +289,7 @@
         return carry
 
     lax.fori_loop(0, planes, embed, 0)
+    own_ref[...] = h_ref[rows_at(plane[0] * flips + grp[0], block), :]
     lax.fori_loop(0, planes, finish, 0)
 
 
@@ -329,10 +307,10 @@
             num_scalar_prefetch=2,
             grid=(1,),
             in_specs=[fixed(x.shape) for x in args],
-            out_specs=[pl.BlockSpec(memory_space=pl.ANY)] * 4,
+            out_specs=[pl.BlockSpec(memory_space=pl.ANY)] * 4 + [fixed((block, width))],
             scratch_shapes=[pltpu.VMEM(*out)] * 4 + [pltpu.SemaphoreType.DMA((4, planes))],
         ),
-        out_shape=shaped(*[out] * 4),
+        out_shape=shaped(*[out] * 4, ((block, width), BF)),
         compiler_params=params(planes <= 4, 60),
         name="activate",
     )(plane, grp, *args)
@@ -369,7 +347,7 @@
             picked = jnp.where(column == head - (base + b * step), 1.0, 0.0).astype(BF)
             return q + dot(picked, ref[rows_at(b, step), :])
 
-        q = lax.fori_loop(0, half // step, pick, q)
+        q = lax.fori_loop(0, half // step, pick, q, unroll=4)
     qb_ref[...] = q.astype(BF)
     flipped = q.T
     hi, lo = split(flipped * (2.0 * scale))
@@ -383,7 +361,7 @@
             cross = dot(hb, hi) + dot(hb, lo)
             x = hb.astype(F32)
             hsq = scale * jnp.sum(x * x, axis=1, keepdims=True)
-            ht_ref[:, pl.ds(pl.multiple_of(base + b * step, step), step)] = x.T.astype(BF)
+            ht_ref[:, pl.ds(pl.multiple_of(base + b * step, step), step)] = hb.T
             for u in range(blocks):
                 at = slice(u * block, (u + 1) * block)
                 bias = bias_ref[pl.ds(base // block + b * blocks + u, 1), :] - qsq
@@ -433,7 +411,7 @@
             grad_ref[rows_at(b, step), :] = grad.astype(BF)
             return carry
 
-        lax.fori_loop(0, half // step, push, 0)
+        lax.fori_loop(0, half // step, push, 0, unroll=2)
 
 
 def score(own, other, rel, bias, meta, block, total_q):
@@ -576,15 +554,23 @@
     )(plane, grp, own, other, d, w_in, w_self, send, *got)
 
 
-def sums_kernel(skip, planes, plane, pre_ref, agg_ref, node_ref, agg_grad_ref, send_ref, *refs):
-    got = refs[: planes - 1]
-    out_ref, gw, grel, box, sems = refs[planes - 1 :]
+def sums_kernel(skip, planes, plane, grp, core, pre_ref, agg_ref, node_ref, agg_grad_ref, *refs):
+    mine_ref, theirs_ref, loss_ref, other_loss_ref, send_ref = refs[:5]
+    got = refs[5 : planes + 4]
+    out_ref, all_loss_ref, *share_refs = refs[planes + 4 : -5]
+    total, gw, grel, box, sems = refs[-5:]
     j = pl.program_id(0)
     node_rows, width = pre_ref.shape
     used = box.shape[1]
 
     @pl.when(j == 0)
     def _():
+        total[...] = mine_ref[...] + theirs_ref[...].astype(F32)
+        put_shares(total, grp[0], share_refs)
+        own, other = loss_ref[...], other_loss_ref[...]
+        here = jnp.zeros(own.shape, I32) + core[0]
+        all_loss_ref[0:1, :] = jnp.where(here == 0, own, other)
+        all_loss_ref[1:2, :] = jnp.where(here == 0, other, own)
         gw[...] = jnp.zeros_like(gw)
         grel[...] = jnp.zeros_like(grel)
         for s in range(planes):
@@ -616,31 +602,39 @@
         out_ref[2 * width :, :] = grel[...].astype(BF)
 
 
-def sums_of_half(plane, pre, agg, nodes, agg_grad, send, got, skip, rel_rows):
+def sums_of_half(
+    places, pre, agg, nodes, agg_grad, mine, theirs, loss, other_loss, send, got, skip, rel_rows, flips
+):
     width = pre.shape[1]
+    small = (mine, theirs, loss, other_loss)
     planes, send_rows, node_rows = send.shape
-    tall = pl.BlockSpec((node_rows, width), lambda i, plane: (i, 0))
+    tall = pl.BlockSpec((node_rows, width), lambda i, *a: (i, 0))
     anywhere = pl.BlockSpec(memory_space=pl.ANY)
-    out = ((2 * width + rel_rows, width), BF)
+    outs = [
+        ((2 * width + rel_rows, width), BF),
+        ((2, loss.shape[1]), F32),
+        *share_shapes(*mine.shape, flips),
+    ]
     return pl.pallas_call(
         functools.partial(sums_kernel, skip, planes),
         grid_spec=pltpu.PrefetchScalarGridSpec(
-            num_scalar_prefetch=1,
+            num_scalar_prefetch=3,
             grid=(planes,),
-            in_specs=[tall] * 4 + [anywhere] * planes,
-            out_specs=fixed(out[0]),
+            in_specs=[tall] * 4 + [fixed(x.shape) for x in small] + [anywhere] * planes,
+            out_specs=[fixed(x) for x, _ in outs],
             scratch_shapes=[
+                pltpu.VMEM(mine.shape, F32),
                 pltpu.VMEM((2, width, width), F32),
                 pltpu.VMEM((rel_rows, width), F32),
                 pltpu.VMEM((planes, send_rows - skip, node_rows), BF),
                 pltpu.SemaphoreType.DMA((planes,)),
             ],
         ),
-        out_shape=shaped(out)[0],
-        compiler_params=params(planes <= 4, 16),
+        out_shape=shaped(*outs),
+        compiler_params=params(planes <= 4, 20),
         cost_estimate=cost(20),
         name="sums_of_half",
-    )(plane, pre, agg, nodes, agg_grad, send, *got)
+    )(*places, pre, agg, nodes, agg_grad, *small, send, *got)
 
 
 def shift_planes(x, by, cand_count):
@@ -763,17 +757,6 @@
     stack, cat, send = lax.optimization_barrier((stack, cat, send))
     nodes_at = [nodes, *gather_stacks(stack, share_rows, grp_count)]
 
-    mine, theirs = pick(
-        plane[None], grp_index[None], core[None], want, their_want, nodes_at, block
-    )
-    theirs = swap_core(theirs, cand_count)
-    own, *parts = forward(
-        core[None], grp_index[None], mine, theirs, cat, rel_emb, block, grp_count
-    )
-    own_agg = join([own, *swap_shares(parts, grp_count)], BF)
-    agg_planes = gather_planes(own_agg, cand_count)
-    agg_pieces = gather_pieces(agg_planes, 0, cand_count, grp_count)
-
     def own_half(x):
         return lax.dynamic_slice_in_dim(x, core * half_q, half_q, 0)
 
@@ -792,8 +775,20 @@
             jnp.broadcast_to(order(own_half(query_head))[None], (8, half_q)),
         ]
     )
+    *nodes_at, rel_q, bias, meta = lax.optimization_barrier((*nodes_at, rel_q, bias, meta))
+    mine, theirs = pick(
+        plane[None], grp_index[None], core[None], want, their_want, nodes_at, block
+    )
+    theirs = swap_core(theirs, cand_count)
+    own, *parts = forward(
+        core[None], grp_index[None], mine, theirs, cat, rel_emb, block, grp_count
+    )
+    own_agg = join([own, *swap_shares(parts, grp_count)], BF)
+    agg_planes = gather_planes(own_agg, cand_count)
+    agg_pieces = gather_pieces(agg_planes, 0, cand_count, grp_count)
+
     agg_pieces, rel_q, bias, meta = lax.optimization_barrier((agg_pieces, rel_q, bias, meta))
-    half_agg, half_nodes, half_h, half_d = activate(
+    half_agg, half_nodes, half_h, half_d, h_own = activate(
         plane[None], grp_index[None], agg_pieces, nodes_at, w_in, w_self
     )
 
@@ -805,18 +800,10 @@
 
     send_after = lax.optimization_barrier((send, half_h))[0]
     got = [send_to_plane(send_after, by) for by in range(1, plane_count)]
-    first_row = plane * node_rows + grp_index * share_rows
-    h_own = lax.dynamic_slice_in_dim(half_h, first_row, share_rows, 0)
-    other_h, h_own = lax.optimization_barrier((other_h, h_own))
     gs, qg, qb, loss, *out_grad = score(half_h, other_h, rel_q, bias, meta, block, total_q)
     gs, *more = lax.optimization_barrier((gs, *out_grad, *got))
     out_grad, got = more[: len(out_grad)], more[len(out_grad) :]
     other_loss = swap_core(loss, cand_count)
-    loss = jnp.where(
-        core == 0,
-        jnp.concatenate([loss[0], other_loss[0]]),
-        jnp.concatenate([other_loss[0], loss[0]]),
-    )
     out_grad = out_grad[0] if out_grad else rows(half, gs, qb, qg, meta, other_h, "rows_other")
     in_grad = swap_core(out_grad, cand_count)
     own_grad = rows(0, gs, qb, qg, meta, half_h, "rows_own")
@@ -833,24 +820,28 @@
         tiles,
         block,
     )
-    sums = sums_of_half(
-        plane[None],
+    sums, loss, own, *parts = sums_of_half(
+        (plane[None], grp_index[None], core[None]),
         pre,
         half_agg,
         half_nodes,
         agg_grad,
+        mine,
+        swap_core(theirs, cand_count),
+        loss,
+        other_loss,
         send,
         got,
         2 * block,
         rel_rows,
+        grp_count,
     )
     gwin, gwself, grel = total_sums(sums, swap_core(sums, cand_count), rel_emb.shape[0])
-    own, *parts = merge(grp_index[None], mine, swap_core(theirs, cand_count), grp_count)
     own, gwin, gwself, grel = lax.optimization_barrier((own, gwin, gwself, grel))
     node_grad = join([own, self_grad, *swap_shares(parts, grp_count)], F32)
     return (
         h_own[None],
-        loss,
+        loss.reshape(total_q),
         node_grad[None],
         grel,
         gwin,

time: 164 us -> 158 us (0.963)
  waiting for transfers between devices: 34.8 us -> 43.3 us
  starting transfers between devices: 44.2 us -> 36.8 us
  Pallas kernels: 63.3 us -> 56.5 us
    ppermute x9, waiting for transfers between devices: 6.98 us -> 14.3 us  [shift_planes(): lax.ppermute(x, 'cand', [(i, (i + 2 * by) % cand_count) for i in range(ca...]
    ppermute x22, starting transfers between devices: 29.8 us -> 24.1 us  [swap_grp(): return lax.ppermute(x, 'grp', [(i, i ^ flip) for i in range(grp_count)])]
    ppermute x22, waiting for transfers between devices: 21.1 us -> 25 us  [swap_grp(): return lax.ppermute(x, 'grp', [(i, i ^ flip) for i in range(grp_count)])]
    pallas_call x1, Pallas kernels: 21.5 us -> 18.7 us  [score(): pl.pallas_call(functools.partial(score_kernel, block, min(512, half), tot...]
    ppermute x7, waiting for transfers between devices: 6.67 us -> 3.96 us  [swap_core(): return lax.ppermute(x, 'cand', [(i, i ^ 1) for i in range(cand_count)])]
    select_n x1, other arithmetic: 0.14 us -> 2.33 us  [body(): rel_q = jnp.take(rel_score, own_half(query_rel), axis=0)]
    ppermute x9, starting transfers between devices: 13.7 us -> 11.8 us  [shift_planes(): lax.ppermute(x, 'cand', [(i, (i + 2 * by) % cand_count) for i in range(ca...]
    unnamed x76 -> x75, local copies, waits for them, and re-layouts: 5.13 us -> 5.67 us
  transfers between devices with their start and end apart: 38 -> 38, of which waited for: 17 -> 21; matrix products, arithmetic and copies ran while one was open for 7% -> 8% of each run, Pallas kernels for 23% -> 20%
where the time goes in v4:
time: 158 us; the launch traced here: 157 us
  Pallas kernels  56.5 us (36%)
  waiting for transfers between devices  43.3 us (27%)
  starting transfers between devices  36.8 us (23%)
  local copies, waits for them, and re-layouts  13.8 us (9%)
  other arithmetic  5.19 us (3%)
  between operations  1.78 us (1%)
    ppermute x22, waiting for transfers between devices, swap_grp(): return lax.ppermute(x, 'grp', [(i, i ^ flip) for i in range(grp_count)])  25 us
    ppermute x22, starting transfers between devices, swap_grp(): return lax.ppermute(x, 'grp', [(i, i ^ flip) for i in range(grp_count)])  24.1 us
    pallas_call x1, Pallas kernels, score(): pl.pallas_call(functools.partial(score_kernel, block, min(512, half), tot...  18.7 us
    ppermute x9, waiting for transfers between devices, shift_planes(): lax.ppermute(x, 'cand', [(i, (i + 2 * by) % cand_count) for i in range(ca...  14.3 us
    ppermute x9, starting transfers between devices, shift_planes(): lax.ppermute(x, 'cand', [(i, (i + 2 * by) % cand_count) for i in range(ca...  11.8 us
    pallas_call x1, Pallas kernels, fold(): pl.pallas_call(functools.partial(fold_kernel, tiles, per), grid_spec=pltp...  8.41 us
    pallas_call x1, Pallas kernels, activate(): pl.pallas_call(functools.partial(activate_kernel, planes, flips, cut), gr...  7.59 us
    pallas_call x1, Pallas kernels, sums_of_half(): pl.pallas_call(functools.partial(sums_kernel, skip, planes), grid_spec=pl...  6.56 us
  transfers between devices with their start and end apart: 38, of which 21 were waited for; matrix products, arithmetic and copies ran while one was open for 8% of the time, Pallas kernels for 20%

profile of v4, /device:TPU:8, one launch (start us, length us, event | category | flops | bytes accessed | tf_op | source)
XLA Modules:
  0.0 157.4 jit_solution(15510729467647275086)
XLA Ops:
  1.7 1.6 %collective-permute-start.1 = (bf16[128,512]{1,0:T(8,128)(2,1)S(1)}, bf16[128,512]{1,0:T(8,128)(2,1)S(1)}, u32[]{:S(2)}, u32[]{:S(2)}) collective-permute-start(bf16[128,512]{1,0:T(8,128)(2,1)S(1)} %dynamic-slice_bitcast_fusion.3), channel_id=1, source_target_pairs={{0,2},{1,3},{2,4},{3,5},{4,6},{5,7},{6,0},{7,1},{8,10},{9,11},{10,... | collective-permute-start | bytes 393224 | tf_op jit(solution)/shard_map/ppermute | solution.py:641
  4.4 1.9 %collective-permute-start.3 = (bf16[128,512]{1,0:T(8,128)(2,1)S(1)}, bf16[128,512]{1,0:T(8,128)(2,1)S(1)}, u32[]{:S(2)}, u32[]{:S(2)}) collective-permute-start(bf16[128,512]{1,0:T(8,128)(2,1)S(1)} %dynamic-slice_bitcast_fusion.3), channel_id=1, source_target_pairs={{0,6},{1,7},{2,0},{3,1},{4,2},{5,3},{6,4},{7,5},{8,14},{9,15},{10,... | collective-permute-start | bytes 393224 | tf_op jit(solution)/shard_map/ppermute | solution.py:641
  8.4 8.4 %fold_adjacency.1 = (bf16[512,2816]{1,0:T(8,128)(2,1)}, bf16[4,320,512]{2,1,0:T(8,128)(2,1)}) custom-call(s32[192]{0:T(256)} %bitcast.41, s32[192]{0:T(256)} %bitcast.36, s32[192]{0:T(256)} %bitcast.38, s32[1]{0:T(128)} %bitcast.26.live, s32[8]{0:T(128)} %bitcast.31, s32[1]{0:T(128)} %bitcast.2.core, bf16[192,128,128]{2,1,0:T(8,128)(2,1)} %bitcast.39, ...), custom_call_target="tpu_custom_call" | custom-call | flops 8000000000 | bytes 8000000 | tf_op jit(solution)/shard_map/fold_adjacency/pallas_call | solution.py:112
  16.9 2.3 %gather_fusion = f32[512,512]{1,0:T(8,128)} fusion(f32[900,512]{1,0:T(8,128)S(1)} %copy-done, s32[1024]{0:T(1024)S(1)} %pad_clamp_fusion), kind=kCustom, calls=%fused_computation | custom fusion | bytes 2099200 | tf_op jit(solution)/shard_map/jit(_take)/gather | solution.py:767
  19.3 1.6 %collective-permute-start.5 = (bf16[384,512]{1,0:T(8,128)(2,1)S(1)}, bf16[384,512]{1,0:T(8,128)(2,1)S(1)}, u32[]{:S(2)}, u32[]{:S(2)}) collective-permute-start(bf16[384,512]{1,0:T(8,128)(2,1)S(1)} %pad_maximum_fusion.refs_1_.refs_17_), channel_id=1, source_target_pairs={{0,16},{8,24},{16,0},{24,8},{1,17},{9,25},{17,1},{25,9},{2,18},{10... | collective-permute-start | bytes 1179656 | tf_op jit(solution)/shard_map/ppermute | solution.py:649
  20.9 2.3 %broadcast_select_fusion.rel_ref = f32[512,512]{1,0:T(8,128)} fusion(f32[512,512]{1,0:T(8,128)} %gather_fusion, pred[512]{0:T(512)(128)(4,1)S(1)} %get-tuple-element.152), kind=kLoop, calls=%fused_computation.2 | loop fusion | flops 262144 | bytes 2097664 | tf_op jit(solution)/shard_map/jit(_take)/select_n | solution.py:767
  24.8 6.0 %collective-permute-done.5.refs_3_.refs_19_ = bf16[384,512]{1,0:T(8,128)(2,1)S(1)} collective-permute-done((bf16[384,512]{1,0:T(8,128)(2,1)S(1)}, bf16[384,512]{1,0:T(8,128)(2,1)S(1)}, u32[]{:S(2)}, u32[]{:S(2)}) %collective-permute-start.5) | collective-permute-done | bytes 393248 | tf_op jit(solution)/shard_map/ppermute | solution.py:649
  31.7 1.5 collective-permute-start.7
  38.7 1.9 %collective-permute-done.6.refs_4_.refs_20_ = bf16[128,512]{1,0:T(8,128)(2,1)} collective-permute-done((bf16[128,512]{1,0:T(8,128)(2,1)}, bf16[128,512]{1,0:T(8,128)(2,1)}, u32[]{:S(2)}, u32[]{:S(2)}) %collective-permute-start.6) | collective-permute-done | bytes 131104 | tf_op jit(solution)/shard_map/ppermute | solution.py:649
  41.3 2.7 %pick_mirrors.1 = (bf16[512,512]{1,0:T(8,128)(2,1)S(1)}, bf16[512,512]{1,0:T(8,128)(2,1)S(1)}) custom-call(s32[1]{0:T(128)} %bitcast.plane, s32[1]{0:T(128)} %bitcast.1.grp, s32[1]{0:T(128)} %bitcast.2.core, s32[8]{0:T(128)S(1)} %bitcast.32, s32[8]{0:T(128)} %collective-permute-done.theirs, bf16[512,512]{1,0:T(8,128)(2,1)S(1)} %bitcast.28, ...), custom_call_target="tpu_custom_call" | custom-call | tf_op jit(solution)/shard_map/pick_mirrors/pallas_call | solution.py:175
  44.1 1.9 %collective-permute-done.8.theirs_ref = bf16[512,512]{1,0:T(8,128)(2,1)S(1)} collective-permute-done((bf16[512,512]{1,0:T(8,128)(2,1)S(1)}, bf16[512,512]{1,0:T(8,128)(2,1)S(1)}, u32[]{:S(2)}, u32[]{:S(2)}) %collective-permute-start.8) | collective-permute-done | bytes 524320 | tf_op jit(solution)/shard_map/ppermute | solution.py:645
  46.0 1.8 %copy-done.2 = bf16[512,2816]{1,0:T(8,128)(2,1)S(1)} copy-done((bf16[512,2816]{1,0:T(8,128)(2,1)S(1)}, bf16[512,2816]{1,0:T(8,128)(2,1)}, u32[]{:S(2)}) %copy-start.2) | copy-done | bytes 2883608
  47.8 1.9 %forward_partial.1 = (f32[128,512]{1,0:T(8,128)S(1)}, bf16[128,512]{1,0:T(8,128)(2,1)S(1)}, bf16[128,512]{1,0:T(8,128)(2,1)S(1)}, bf16[128,512]{1,0:T(8,128)(2,1)S(1)}) custom-call(s32[1]{0:T(128)} %bitcast.2.core, s32[1]{0:T(128)} %bitcast.1.grp, bf16[512,512]{1,0:T(8,128)(2,1)S(1)} %get-tuple-element.88.mine_ref, ...), custom_call_target="tpu_custom_call" | custom-call | tf_op jit(solution)/shard_map/forward_partial/pallas_call | solution.py:242
  50.0 2.2 %collective-permute-start.11 = (bf16[128,512]{1,0:T(8,128)(2,1)S(1)}, bf16[128,512]{1,0:T(8,128)(2,1)S(1)}, u32[]{:S(2)}, u32[]{:S(2)}) collective-permute-start(bf16[128,512]{1,0:T(8,128)(2,1)S(1)} %get-tuple-element.94), channel_id=1, source_target_pairs={{0,24},{8,16},{16,8},{24,0},{1,25},{9,17},{17,9},{25,1},{2,26},{10... | collective-permute-start | bytes 393224 | tf_op jit(solution)/shard_map/ppermute | solution.py:649
  53.3 4.9 %collective-permute-done.10.refs_2_ = bf16[128,512]{1,0:T(8,128)(2,1)S(1)} collective-permute-done((bf16[128,512]{1,0:T(8,128)(2,1)S(1)}, bf16[128,512]{1,0:T(8,128)(2,1)S(1)}, u32[]{:S(2)}, u32[]{:S(2)}) %collective-permute-start.10) | collective-permute-done | bytes 131104 | tf_op jit(solution)/shard_map/ppermute | solution.py:649
  59.9 3.0 %collective-permute-start.19 = (bf16[128,512]{1,0:T(8,128)(2,1)S(1)}, bf16[128,512]{1,0:T(8,128)(2,1)S(1)}, u32[]{:S(2)}, u32[]{:S(2)}) collective-permute-start(bf16[128,512]{1,0:T(8,128)(2,1)S(1)} %join_group.2.refs_0_), channel_id=1, source_target_pairs={{0,4},{1,5},{2,6},{3,7},{4,0},{5,1},{6,2},{7,3},{8,12},{9,13},{10,... | collective-permute-start | bytes 393224 | tf_op jit(solution)/shard_map/ppermute | solution.py:641
  66.9 3.9 %collective-permute-done.19.refs_8_ = bf16[128,512]{1,0:T(8,128)(2,1)S(1)} collective-permute-done((bf16[128,512]{1,0:T(8,128)(2,1)S(1)}, bf16[128,512]{1,0:T(8,128)(2,1)S(1)}, u32[]{:S(2)}, u32[]{:S(2)}) %collective-permute-start.19) | collective-permute-done | bytes 131104 | tf_op jit(solution)/shard_map/ppermute | solution.py:641
  71.8 1.8 %collective-permute-done.23.refs_12_ = bf16[128,512]{1,0:T(8,128)(2,1)S(1)} collective-permute-done((bf16[128,512]{1,0:T(8,128)(2,1)S(1)}, bf16[128,512]{1,0:T(8,128)(2,1)S(1)}, u32[]{:S(2)}, u32[]{:S(2)}) %collective-permute-start.23) | collective-permute-done | bytes 131104 | tf_op jit(solution)/shard_map/ppermute | solution.py:641
  80.5 2.3 %collective-permute-done.14.refs_3_ = bf16[128,512]{1,0:T(8,128)(2,1)S(1)} collective-permute-done((bf16[128,512]{1,0:T(8,128)(2,1)S(1)}, bf16[128,512]{1,0:T(8,128)(2,1)S(1)}, u32[]{:S(2)}, u32[]{:S(2)}) %collective-permute-start.14) | collective-permute-done | bytes 131104 | tf_op jit(solution)/shard_map/ppermute | solution.py:649
  85.6 1.8 %collective-permute-done.18.refs_7_ = bf16[128,512]{1,0:T(8,128)(2,1)S(1)} collective-permute-done((bf16[128,512]{1,0:T(8,128)(2,1)S(1)}, bf16[128,512]{1,0:T(8,128)(2,1)S(1)}, u32[]{:S(2)}, u32[]{:S(2)}) %collective-permute-start.18) | collective-permute-done | bytes 131104 | tf_op jit(solution)/shard_map/ppermute | solution.py:649
  88.9 7.6 %activate.1 = (bf16[2048,512]{1,0:T(8,128)(2,1)}, bf16[2048,512]{1,0:T(8,128)(2,1)}, bf16[2048,512]{1,0:T(8,128)(2,1)}, bf16[2048,512]{1,0:T(8,128)(2,1)}, bf16[128,512]{1,0:T(8,128)(2,1)}) custom-call(s32[1]{0:T(128)} %bitcast.plane, s32[1]{0:T(128)} %bitcast.1.grp, bf16[512,512]{1,0:T(8,128)(2,1)} %refs_0_.1, bf16[512,512]{1,0:T(8,128)(2,1)} %refs_1_.1, ...), custom_call_target="tpu_custom_call" | custom-call | tf_op jit(solution)/shard_map/activate/pallas_call | solution.py:304
  98.0 2.6 %collective-permute-start.29 = (bf16[320,512]{1,0:T(8,128)(2,1)S(1)}, bf16[320,512]{1,0:T(8,128)(2,1)S(1)}, u32[]{:S(2)}, u32[]{:S(2)}) collective-permute-start(bf16[320,512]{1,0:T(8,128)(2,1)S(1)} %get-tuple-element.155), channel_id=1, source_target_pairs={{0,4},{1,5},{2,6},{3,7},{4,0},{5,1},{6,2},{7,3},{8,12},{9,13},{10,... | collective-permute-start | bytes 983048 | tf_op jit(solution)/shard_map/ppermute | solution.py:641
  101.7 1.6 %copy-done.6 = bf16[2048,512]{1,0:T(8,128)(2,1)S(1)} copy-done((bf16[2048,512]{1,0:T(8,128)(2,1)S(1)}, bf16[2048,512]{1,0:T(8,128)(2,1)}, u32[]{:S(2)}) %copy-start.6) | copy-done | bytes 2097176
  103.2 18.7 %score.1 = (bf16[4096,512]{1,0:T(8,128)(2,1)S(1)}, bf16[512,512]{1,0:T(8,128)(2,1)S(1)}, bf16[512,512]{1,0:T(8,128)(2,1)S(1)}, f32[1,512]{1,0:T(1,128)S(1)}, bf16[2048,512]{1,0:T(8,128)(2,1)S(1)}) custom-call(bf16[2048,512]{1,0:T(8,128)(2,1)S(1)} %copy-done.6, bf16[2048,512]{1,0:T(8,128)(2,1)} %collective-permute-done.27.other_ref, ...), custom_call_target="tpu_custom_call" | custom-call | flops 60000002048 | bytes 60000000 | tf_op jit(solution)/shard_map/score/pallas_call | solution.py:425
  122.0 4.9 %collective-permute-done.29.refs_4_.refs_6_ = bf16[320,512]{1,0:T(8,128)(2,1)S(1)} collective-permute-done((bf16[320,512]{1,0:T(8,128)(2,1)S(1)}, bf16[320,512]{1,0:T(8,128)(2,1)S(1)}, u32[]{:S(2)}, u32[]{:S(2)}) %collective-permute-start.29) | collective-permute-done | bytes 327712 | tf_op jit(solution)/shard_map/ppermute | solution.py:641
  126.9 2.8 %collective-permute-done.30.refs_5_.refs_7_ = bf16[320,512]{1,0:T(8,128)(2,1)S(1)} collective-permute-done((bf16[320,512]{1,0:T(8,128)(2,1)S(1)}, bf16[320,512]{1,0:T(8,128)(2,1)S(1)}, u32[]{:S(2)}, u32[]{:S(2)}) %collective-permute-start.30) | collective-permute-done | bytes 327712 | tf_op jit(solution)/shard_map/ppermute | solution.py:641
  129.8 3.5 %rows_own.1.own_ref = bf16[2048,512]{1,0:T(8,128)(2,1)S(1)} custom-call(bf16[4096,512]{1,0:T(8,128)(2,1)S(1)} %get-tuple-element.123.gs_ref, bf16[512,512]{1,0:T(8,128)(2,1)S(1)} %get-tuple-element.124.qb_ref, bf16[512,512]{1,0:T(8,128)(2,1)S(1)} %get-tuple-element.125.qg_ref, s32[16,512]{1,0:T(8,128)S(1)} %copy-done.13, bf16[2048,512]{1,0:T(8,128)(2,1)S(1)} %copy-done.6), custom_call_target="tpu_custom_call" | custom-call | tf_op jit(solution)/shard_map/rows_own/pallas_call | solution.py:467
  133.9 4.8 %backward_rows.1 = (bf16[2048,512]{1,0:T(8,128)(2,1)S(1)}, bf16[2048,512]{1,0:T(8,128)(2,1)S(1)}, f32[512,512]{1,0:T(8,128)S(1)}, bf16[512,512]{1,0:T(8,128)(2,1)S(1)}, f32[128,512]{1,0:T(8,128)S(1)}) custom-call(s32[1]{0:T(128)} %bitcast.plane, s32[1]{0:T(128)} %bitcast.1.grp, bf16[2048,512]{1,0:T(8,128)(2,1)S(1)} %rows_own.1.own_ref, ...), custom_call_target="tpu_custom_call" | custom-call | flops 6000000000 | bytes 6000000 | tf_op jit(solution)/shard_map/backward_rows/pallas_call | solution.py:531
  140.8 6.6 %sums_of_half.1 = (bf16[1280,512]{1,0:T(8,128)(2,1)S(1)}, f32[2,512]{1,0:T(2,128)S(1)}, f32[128,512]{1,0:T(8,128)S(1)}, bf16[128,512]{1,0:T(8,128)(2,1)S(1)}, bf...) custom-call(s32[1]{0:T(128)} %bitcast.plane, s32[1]{0:T(128)} %bitcast.1.grp, s32[1]{0:T(128)} %bitcast.2.core, ...), custom_call_target="tpu_custom_call" | custom-call | flops 20000000000 | bytes 20000000 | tf_op jit(solution)/shard_map/sums_of_half/pallas_call | solution.py:618
  149.5 1.6 %collective-permute-start.37 = (bf16[128,512]{1,0:T(8,128)(2,1)S(1)}, bf16[128,512]{1,0:T(8,128)(2,1)S(1)}, u32[]{:S(2)}, u32[]{:S(2)}) collective-permute-start(bf16[128,512]{1,0:T(8,128)(2,1)S(1)} %get-tuple-element.148), channel_id=1, source_target_pairs={{0,24},{8,16},{16,8},{24,0},{1,25},{9,17},{17,9},{25,1},{2,26},{10... | collective-permute-start | bytes 393224 | tf_op jit(solution)/shard_map/ppermute | solution.py:649
  151.7 1.6 %total_sums.1 = (f32[512,512]{1,0:T(8,128)}, f32[512,512]{1,0:T(8,128)}, f32[225,512]{1,0:T(8,128)}) custom-call(bf16[1280,512]{1,0:T(8,128)(2,1)S(1)} %get-tuple-element.140.a_ref, bf16[1280,512]{1,0:T(8,128)(2,1)S(1)} %collective-permute-done.34.b_ref), custom_call_target="tpu_custom_call" | custom-call | tf_op jit(solution)/shard_map/total_sums/pallas_call | solution.py:663
  153.9 2.7 %collective-permute-done.36.refs_3_ = bf16[128,512]{1,0:T(8,128)(2,1)S(1)} collective-permute-done((bf16[128,512]{1,0:T(8,128)(2,1)S(1)}, bf16[128,512]{1,0:T(8,128)(2,1)S(1)}, u32[]{:S(2)}, u32[]{:S(2)}) %collective-permute-start.36) | collective-permute-done | bytes 131104 | tf_op jit(solution)/shard_map/ppermute | solution.py:649
  (148 shorter events, 40.8 us)
Async XLA Ops:
  1.7 17.5 %collective-permute-start.1 = (bf16[128,512]{1,0:T(8,128)(2,1)S(1)}, bf16[128,512]{1,0:T(8,128)(2,1)S(1)}, u32[]{:S(2)}, u32[]{:S(2)}) collective-permute-start(bf16[128,512]{1,0:T(8,128)(2,1)S(1)} %dynamic-slice_bitcast_fusion.3), channel_id=1, source_target_pairs={{0,2},{1,3},{2,4},{3,5},{4,6},{5,7},{6,0},{7,1},{8,10},{9,11},{10,... | collective-permute-start | bytes 393224 | tf_op jit(solution)/shard_map/ppermute | solution.py:641
  3.3 15.9 %collective-permute-start.2 = (bf16[128,512]{1,0:T(8,128)(2,1)S(1)}, bf16[128,512]{1,0:T(8,128)(2,1)S(1)}, u32[]{:S(2)}, u32[]{:S(2)}) collective-permute-start(bf16[128,512]{1,0:T(8,128)(2,1)S(1)} %dynamic-slice_bitcast_fusion.3), channel_id=1, source_target_pairs={{0,4},{1,5},{2,6},{3,7},{4,0},{5,1},{6,2},{7,3},{8,12},{9,13},{10,... | collective-permute-start | bytes 393224 | tf_op jit(solution)/shard_map/ppermute | solution.py:641
  4.4 14.8 %collective-permute-start.3 = (bf16[128,512]{1,0:T(8,128)(2,1)S(1)}, bf16[128,512]{1,0:T(8,128)(2,1)S(1)}, u32[]{:S(2)}, u32[]{:S(2)}) collective-permute-start(bf16[128,512]{1,0:T(8,128)(2,1)S(1)} %dynamic-slice_bitcast_fusion.3), channel_id=1, source_target_pairs={{0,6},{1,7},{2,0},{3,1},{4,2},{5,3},{6,4},{7,5},{8,14},{9,15},{10,... | collective-permute-start | bytes 393224 | tf_op jit(solution)/shard_map/ppermute | solution.py:641
  6.4 34.3 %collective-permute-start = (s32[8]{0:T(128)}, s32[8]{0:T(128)}, u32[]{:S(2)}, u32[]{:S(2)}) collective-permute-start(s32[8]{0:T(128)} %bitcast.30), channel_id=1, source_target_pairs={{0,1},{1,0},{2,3},{3,2},{4,5},{5,4},{6,7},{7,6},{8,9},{9,8},{10,11... | collective-permute-start | bytes 104 | tf_op jit(solution)/shard_map/ppermute | solution.py:645
  19.3 11.6 %collective-permute-start.5 = (bf16[384,512]{1,0:T(8,128)(2,1)S(1)}, bf16[384,512]{1,0:T(8,128)(2,1)S(1)}, u32[]{:S(2)}, u32[]{:S(2)}) collective-permute-start(bf16[384,512]{1,0:T(8,128)(2,1)S(1)} %pad_maximum_fusion.refs_1_.refs_17_), channel_id=1, source_target_pairs={{0,16},{8,24},{16,0},{24,8},{1,17},{9,25},{17,1},{25,9},{2,18},{10... | collective-permute-start | bytes 1179656 | tf_op jit(solution)/shard_map/ppermute | solution.py:649
  23.2 11.5 %collective-permute-start.4 = (bf16[384,512]{1,0:T(8,128)(2,1)S(1)}, bf16[384,512]{1,0:T(8,128)(2,1)S(1)}, u32[]{:S(2)}, u32[]{:S(2)}) collective-permute-start(bf16[384,512]{1,0:T(8,128)(2,1)S(1)} %pad_maximum_fusion.refs_1_.refs_17_), channel_id=1, source_target_pairs={{0,8},{8,0},{16,24},{24,16},{1,9},{9,1},{17,25},{25,17},{2,10},{10... | collective-permute-start | bytes 1179656 | tf_op jit(solution)/shard_map/ppermute | solution.py:649
  31.7 9.0 %collective-permute-start.7 = (bf16[256,512]{1,0:T(8,128)(2,1)}, bf16[256,512]{1,0:T(8,128)(2,1)}, u32[]{:S(2)}, u32[]{:S(2)}) collective-permute-start(bf16[256,512]{1,0:T(8,128)(2,1)} %slice.11), channel_id=1, source_target_pairs={{0,8},{8,0},{16,24},{24,16},{1,9},{9,1},{17,25},{25,17},{2,10},{10... | collective-permute-start | bytes 786440 | tf_op jit(solution)/shard_map/ppermute | solution.py:649
  35.4 5.3 %collective-permute-start.6 = (bf16[128,512]{1,0:T(8,128)(2,1)}, bf16[128,512]{1,0:T(8,128)(2,1)}, u32[]{:S(2)}, u32[]{:S(2)}) collective-permute-start(bf16[128,512]{1,0:T(8,128)(2,1)} %slice.10), channel_id=1, source_target_pairs={{0,16},{8,24},{16,0},{24,8},{1,17},{9,25},{17,1},{25,9},{2,18},{10... | collective-permute-start | bytes 393224 | tf_op jit(solution)/shard_map/ppermute | solution.py:649
  49.7 8.4 %collective-permute-start.10 = (bf16[128,512]{1,0:T(8,128)(2,1)S(1)}, bf16[128,512]{1,0:T(8,128)(2,1)S(1)}, u32[]{:S(2)}, u32[]{:S(2)}) collective-permute-start(bf16[128,512]{1,0:T(8,128)(2,1)S(1)} %get-tuple-element.93), channel_id=1, source_target_pairs={{0,16},{8,24},{16,0},{24,8},{1,17},{9,25},{17,1},{25,9},{2,18},{10... | collective-permute-start | bytes 393224 | tf_op jit(solution)/shard_map/ppermute | solution.py:649
  50.0 8.1 %collective-permute-start.11 = (bf16[128,512]{1,0:T(8,128)(2,1)S(1)}, bf16[128,512]{1,0:T(8,128)(2,1)S(1)}, u32[]{:S(2)}, u32[]{:S(2)}) collective-permute-start(bf16[128,512]{1,0:T(8,128)(2,1)S(1)} %get-tuple-element.94), channel_id=1, source_target_pairs={{0,24},{8,16},{16,8},{24,0},{1,25},{9,17},{17,9},{25,1},{2,26},{10... | collective-permute-start | bytes 393224 | tf_op jit(solution)/shard_map/ppermute | solution.py:649
  52.2 7.1 %collective-permute-start.9 = (bf16[128,512]{1,0:T(8,128)(2,1)S(1)}, bf16[128,512]{1,0:T(8,128)(2,1)S(1)}, u32[]{:S(2)}, u32[]{:S(2)}) collective-permute-start(bf16[128,512]{1,0:T(8,128)(2,1)S(1)} %get-tuple-element.92), channel_id=1, source_target_pairs={{0,8},{8,0},{16,24},{24,16},{1,9},{9,1},{17,25},{25,17},{2,10},{10... | collective-permute-start | bytes 393224 | tf_op jit(solution)/shard_map/ppermute | solution.py:649
  59.4 6.5 %collective-permute-start.15 = (bf16[128,512]{1,0:T(8,128)(2,1)S(1)}, bf16[128,512]{1,0:T(8,128)(2,1)S(1)}, u32[]{:S(2)}, u32[]{:S(2)}) collective-permute-start(bf16[128,512]{1,0:T(8,128)(2,1)S(1)} %join_group.2.refs_0_), channel_id=1, source_target_pairs={{0,2},{1,3},{2,4},{3,5},{4,6},{5,7},{6,0},{7,1},{8,10},{9,11},{10,... | collective-permute-start | bytes 393224 | tf_op jit(solution)/shard_map/ppermute | solution.py:641
  59.9 10.9 %collective-permute-start.19 = (bf16[128,512]{1,0:T(8,128)(2,1)S(1)}, bf16[128,512]{1,0:T(8,128)(2,1)S(1)}, u32[]{:S(2)}, u32[]{:S(2)}) collective-permute-start(bf16[128,512]{1,0:T(8,128)(2,1)S(1)} %join_group.2.refs_0_), channel_id=1, source_target_pairs={{0,4},{1,5},{2,6},{3,7},{4,0},{5,1},{6,2},{7,3},{8,12},{9,13},{10,... | collective-permute-start | bytes 393224 | tf_op jit(solution)/shard_map/ppermute | solution.py:641
  62.9 10.7 %collective-permute-start.23 = (bf16[128,512]{1,0:T(8,128)(2,1)S(1)}, bf16[128,512]{1,0:T(8,128)(2,1)S(1)}, u32[]{:S(2)}, u32[]{:S(2)}) collective-permute-start(bf16[128,512]{1,0:T(8,128)(2,1)S(1)} %join_group.2.refs_0_), channel_id=1, source_target_pairs={{0,6},{1,7},{2,0},{3,1},{4,2},{5,3},{6,4},{7,5},{8,14},{9,15},{10,... | collective-permute-start | bytes 393224 | tf_op jit(solution)/shard_map/ppermute | solution.py:641
  62.9 11.9 %collective-permute-start.13 = (bf16[128,512]{1,0:T(8,128)(2,1)S(1)}, bf16[128,512]{1,0:T(8,128)(2,1)S(1)}, u32[]{:S(2)}, u32[]{:S(2)}) collective-permute-start(bf16[128,512]{1,0:T(8,128)(2,1)S(1)} %join_group.2.refs_0_), channel_id=1, source_target_pairs={{0,16},{8,24},{16,0},{24,8},{1,17},{9,25},{17,1},{25,9},{2,18},{10... | collective-permute-start | bytes 393224 | tf_op jit(solution)/shard_map/ppermute | solution.py:649
  63.8 11.8 %collective-permute-start.12 = (bf16[128,512]{1,0:T(8,128)(2,1)S(1)}, bf16[128,512]{1,0:T(8,128)(2,1)S(1)}, u32[]{:S(2)}, u32[]{:S(2)}) collective-permute-start(bf16[128,512]{1,0:T(8,128)(2,1)S(1)} %join_group.2.refs_0_), channel_id=1, source_target_pairs={{0,8},{8,0},{16,24},{24,16},{1,9},{9,1},{17,25},{25,17},{2,10},{10... | collective-permute-start | bytes 393224 | tf_op jit(solution)/shard_map/ppermute | solution.py:649
  65.9 10.2 %collective-permute-start.16 = (bf16[128,512]{1,0:T(8,128)(2,1)S(1)}, bf16[128,512]{1,0:T(8,128)(2,1)S(1)}, u32[]{:S(2)}, u32[]{:S(2)}) collective-permute-start(bf16[128,512]{1,0:T(8,128)(2,1)S(1)} %collective-permute-done.15.refs_4_), channel_id=1, source_target_pairs={{0,8},{8,0},{16,24},{24,16},{1,9},{9,1},{17,25},{25,17},{2,10},{10... | collective-permute-start | bytes 393224 | tf_op jit(solution)/shard_map/ppermute | solution.py:649
  70.8 6.7 %collective-permute-start.21 = (bf16[128,512]{1,0:T(8,128)(2,1)S(1)}, bf16[128,512]{1,0:T(8,128)(2,1)S(1)}, u32[]{:S(2)}, u32[]{:S(2)}) collective-permute-start(bf16[128,512]{1,0:T(8,128)(2,1)S(1)} %collective-permute-done.19.refs_8_), channel_id=1, source_target_pairs={{0,16},{8,24},{16,0},{24,8},{1,17},{9,25},{17,1},{25,9},{2,18},{10... | collective-permute-start | bytes 393224 | tf_op jit(solution)/shard_map/ppermute | solution.py:649
  73.6 6.4 %collective-permute-start.24 = (bf16[128,512]{1,0:T(8,128)(2,1)S(1)}, bf16[128,512]{1,0:T(8,128)(2,1)S(1)}, u32[]{:S(2)}, u32[]{:S(2)}) collective-permute-start(bf16[128,512]{1,0:T(8,128)(2,1)S(1)} %collective-permute-done.23.refs_12_), channel_id=1, source_target_pairs={{0,8},{8,0},{16,24},{24,16},{1,9},{9,1},{17,25},{25,17},{2,10},{10... | collective-permute-start | bytes 393224 | tf_op jit(solution)/shard_map/ppermute | solution.py:649
  74.8 8.0 %collective-permute-start.14 = (bf16[128,512]{1,0:T(8,128)(2,1)S(1)}, bf16[128,512]{1,0:T(8,128)(2,1)S(1)}, u32[]{:S(2)}, u32[]{:S(2)}) collective-permute-start(bf16[128,512]{1,0:T(8,128)(2,1)S(1)} %collective-permute-done.13.refs_2_), channel_id=1, source_target_pairs={{0,8},{8,0},{16,24},{24,16},{1,9},{9,1},{17,25},{25,17},{2,10},{10... | collective-permute-start | bytes 393224 | tf_op jit(solution)/shard_map/ppermute | solution.py:649
  75.6 7.9 %collective-permute-start.17 = (bf16[128,512]{1,0:T(8,128)(2,1)S(1)}, bf16[128,512]{1,0:T(8,128)(2,1)S(1)}, u32[]{:S(2)}, u32[]{:S(2)}) collective-permute-start(bf16[128,512]{1,0:T(8,128)(2,1)S(1)} %collective-permute-done.15.refs_4_), channel_id=1, source_target_pairs={{0,16},{8,24},{16,0},{24,8},{1,17},{9,25},{17,1},{25,9},{2,18},{10... | collective-permute-start | bytes 393224 | tf_op jit(solution)/shard_map/ppermute | solution.py:649
  76.1 9.5 %collective-permute-start.20 = (bf16[128,512]{1,0:T(8,128)(2,1)S(1)}, bf16[128,512]{1,0:T(8,128)(2,1)S(1)}, u32[]{:S(2)}, u32[]{:S(2)}) collective-permute-start(bf16[128,512]{1,0:T(8,128)(2,1)S(1)} %collective-permute-done.19.refs_8_), channel_id=1, source_target_pairs={{0,8},{8,0},{16,24},{24,16},{1,9},{9,1},{17,25},{25,17},{2,10},{10... | collective-permute-start | bytes 393224 | tf_op jit(solution)/shard_map/ppermute | solution.py:649
  77.5 8.1 %collective-permute-start.25 = (bf16[128,512]{1,0:T(8,128)(2,1)S(1)}, bf16[128,512]{1,0:T(8,128)(2,1)S(1)}, u32[]{:S(2)}, u32[]{:S(2)}) collective-permute-start(bf16[128,512]{1,0:T(8,128)(2,1)S(1)} %collective-permute-done.23.refs_12_), channel_id=1, source_target_pairs={{0,16},{8,24},{16,0},{24,8},{1,17},{9,25},{17,1},{25,9},{2,18},{10... | collective-permute-start | bytes 393224 | tf_op jit(solution)/shard_map/ppermute | solution.py:649
  80.0 7.4 %collective-permute-start.18 = (bf16[128,512]{1,0:T(8,128)(2,1)S(1)}, bf16[128,512]{1,0:T(8,128)(2,1)S(1)}, u32[]{:S(2)}, u32[]{:S(2)}) collective-permute-start(bf16[128,512]{1,0:T(8,128)(2,1)S(1)} %collective-permute-done.16.refs_5_), channel_id=1, source_target_pairs={{0,16},{8,24},{16,0},{24,8},{1,17},{9,25},{17,1},{25,9},{2,18},{10... | collective-permute-start | bytes 393224 | tf_op jit(solution)/shard_map/ppermute | solution.py:649
  83.5 5.3 %collective-permute-start.26 = (bf16[128,512]{1,0:T(8,128)(2,1)S(1)}, bf16[128,512]{1,0:T(8,128)(2,1)}, u32[]{:S(2)}, u32[]{:S(2)}) collective-permute-start(bf16[128,512]{1,0:T(8,128)(2,1)S(1)} %collective-permute-done.24.refs_13_), channel_id=1, source_target_pairs={{0,16},{8,24},{16,0},{24,8},{1,17},{9,25},{17,1},{25,9},{2,18},{10... | collective-permute-start | bytes 393224 | tf_op jit(solution)/shard_map/ppermute | solution.py:649
  96.5 5.1 %collective-permute-start.27 = (bf16[2048,512]{1,0:T(8,128)(2,1)}, bf16[2048,512]{1,0:T(8,128)(2,1)}, u32[]{:S(2)}, u32[]{:S(2)}) collective-permute-start(bf16[2048,512]{1,0:T(8,128)(2,1)} %get-tuple-element.115.own_ref.h_ref), channel_id=1, source_target_pairs={{0,1},{1,0},{2,3},{3,2},{4,5},{5,4},{6,7},{7,6},{8,9},{9,8},{10,11... | collective-permute-start | bytes 6291464 | tf_op jit(solution)/shard_map/ppermute | solution.py:645
  97.9 24.0 %collective-permute-start.28 = (bf16[320,512]{1,0:T(8,128)(2,1)S(1)}, bf16[320,512]{1,0:T(8,128)(2,1)S(1)}, u32[]{:S(2)}, u32[]{:S(2)}) collective-permute-start(bf16[320,512]{1,0:T(8,128)(2,1)S(1)} %get-tuple-element.156), channel_id=1, source_target_pairs={{0,2},{1,3},{2,4},{3,5},{4,6},{5,7},{6,0},{7,1},{8,10},{9,11},{10,... | collective-permute-start | bytes 983048 | tf_op jit(solution)/shard_map/ppermute | solution.py:641
  98.0 28.9 %collective-permute-start.29 = (bf16[320,512]{1,0:T(8,128)(2,1)S(1)}, bf16[320,512]{1,0:T(8,128)(2,1)S(1)}, u32[]{:S(2)}, u32[]{:S(2)}) collective-permute-start(bf16[320,512]{1,0:T(8,128)(2,1)S(1)} %get-tuple-element.155), channel_id=1, source_target_pairs={{0,4},{1,5},{2,6},{3,7},{4,0},{5,1},{6,2},{7,3},{8,12},{9,13},{10,... | collective-permute-start | bytes 983048 | tf_op jit(solution)/shard_map/ppermute | solution.py:641
  100.6 29.1 %collective-permute-start.30 = (bf16[320,512]{1,0:T(8,128)(2,1)S(1)}, bf16[320,512]{1,0:T(8,128)(2,1)S(1)}, u32[]{:S(2)}, u32[]{:S(2)}) collective-permute-start(bf16[320,512]{1,0:T(8,128)(2,1)S(1)} %get-tuple-element.154), channel_id=1, source_target_pairs={{0,6},{1,7},{2,0},{3,1},{4,2},{5,3},{6,4},{7,5},{8,14},{9,15},{10,... | collective-permute-start | bytes 983048 | tf_op jit(solution)/shard_map/ppermute | solution.py:641
  147.6 6.3 %collective-permute-start.35 = (bf16[128,512]{1,0:T(8,128)(2,1)S(1)}, bf16[128,512]{1,0:T(8,128)(2,1)S(1)}, u32[]{:S(2)}, u32[]{:S(2)}) collective-permute-start(bf16[128,512]{1,0:T(8,128)(2,1)S(1)} %get-tuple-element.146), channel_id=1, source_target_pairs={{0,8},{8,0},{16,24},{24,16},{1,9},{9,1},{17,25},{25,17},{2,10},{10... | collective-permute-start | bytes 393224 | tf_op jit(solution)/shard_map/ppermute | solution.py:649
  148.3 8.3 %collective-permute-start.36 = (bf16[128,512]{1,0:T(8,128)(2,1)S(1)}, bf16[128,512]{1,0:T(8,128)(2,1)S(1)}, u32[]{:S(2)}, u32[]{:S(2)}) collective-permute-start(bf16[128,512]{1,0:T(8,128)(2,1)S(1)} %get-tuple-element.147), channel_id=1, source_target_pairs={{0,16},{8,24},{16,0},{24,8},{1,17},{9,25},{17,1},{25,9},{2,18},{10... | collective-permute-start | bytes 393224 | tf_op jit(solution)/shard_map/ppermute | solution.py:649
  149.5 7.1 %collective-permute-start.37 = (bf16[128,512]{1,0:T(8,128)(2,1)S(1)}, bf16[128,512]{1,0:T(8,128)(2,1)S(1)}, u32[]{:S(2)}, u32[]{:S(2)}) collective-permute-start(bf16[128,512]{1,0:T(8,128)(2,1)S(1)} %get-tuple-element.148), channel_id=1, source_target_pairs={{0,24},{8,16},{16,8},{24,0},{1,25},{9,17},{17,9},{25,1},{2,26},{10... | collective-permute-start | bytes 393224 | tf_op jit(solution)/shard_map/ppermute | solution.py:649
  (43 other events, 493.2 us)

commit v5 on v4

--- a/solution.py
+++ b/solution.py
@@ -102,7 +102,7 @@
 def fold(adj, src, tgt, rel, live, want, core, tiles, rel_rows):
     count, block, _ = adj.shape
     slots = want.shape[0]
-    per = next(p for p in (48, 16, 8, 4, 2, 1) if count % p == 0)
+    per = next(p for p in (96, 48, 16, 8, 4, 2, 1) if count % p == 0)
     rows = tiles * block
     info = jnp.pad(jnp.stack([rel, tgt]).astype(F32), ((0, INFO_ROWS - 2), (0, rows - count)))
     outs = [
@@ -447,7 +447,7 @@
             *[(other.shape, BF)] * whole,
         ),
         scratch_shapes=[pltpu.VMEM((total, qt), F32), pltpu.VMEM((width, total), BF)],
-        compiler_params=params(whole, 28),
+        compiler_params=params(whole, 36),
         cost_estimate=cost(60),
         name="score",
     )(own, other, rel, bias, meta)
@@ -631,7 +631,7 @@
             ],
         ),
         out_shape=shaped(*outs),
-        compiler_params=params(planes <= 4, 20),
+        compiler_params=params(planes <= 4, 14),
         cost_estimate=cost(20),
         name="sums_of_half",
     )(*places, pre, agg, nodes, agg_grad, *small, send, *got)

time: 158 us -> 158 us (level)
  transfers between devices with their start and end apart: 38 -> 38, of which waited for: 21 -> 24; matrix products, arithmetic and copies ran while one was open for 8% -> 8% of each run, Pallas kernels for 20% -> 20%
where the time goes in v5:
time: 158 us
  Pallas kernels  55.7 us (35%)
  waiting for transfers between devices  44 us (28%)
  starting transfers between devices  37.1 us (23%)
  local copies, waits for them, and re-layouts  13.8 us (9%)
  other arithmetic  5.19 us (3%)
  between operations  1.77 us (1%)
    ppermute x22, waiting for transfers between devices, swap_grp(): return lax.ppermute(x, 'grp', [(i, i ^ flip) for i in range(grp_count)])  24.8 us
    ppermute x22, starting transfers between devices, swap_grp(): return lax.ppermute(x, 'grp', [(i, i ^ flip) for i in range(grp_count)])  24.7 us
    pallas_call x1, Pallas kernels, score(): pl.pallas_call(functools.partial(score_kernel, block, min(512, half), tot...  18.7 us
    ppermute x9, waiting for transfers between devices, shift_planes(): lax.ppermute(x, 'cand', [(i, (i + 2 * by) % cand_count) for i in range(ca...  15.2 us
    ppermute x9, starting transfers between devices, shift_planes(): lax.ppermute(x, 'cand', [(i, (i + 2 * by) % cand_count) for i in range(ca...  11.4 us
    pallas_call x1, Pallas kernels, fold(): pl.pallas_call(functools.partial(fold_kernel, tiles, per), grid_spec=pltp...  7.75 us
    pallas_call x1, Pallas kernels, activate(): pl.pallas_call(functools.partial(activate_kernel, planes, flips, cut), gr...  7.59 us
    pallas_call x1, Pallas kernels, sums_of_half(): pl.pallas_call(functools.partial(sums_kernel, skip, planes), grid_spec=pl...  6.5 us
  transfers between devices with their start and end apart: 38, of which 24 were waited for; matrix products, arithmetic and copies ran while one was open for 8% of the time, Pallas kernels for 20%

profile of v5, /device:TPU:8, one launch (start us, length us, event | category | flops | bytes accessed | tf_op | source)
XLA Modules:
  0.0 157.6 jit_solution(5603779144066004078)
XLA Ops:
  1.7 1.6 %collective-permute-start.1 = (bf16[128,512]{1,0:T(8,128)(2,1)S(1)}, bf16[128,512]{1,0:T(8,128)(2,1)S(1)}, u32[]{:S(2)}, u32[]{:S(2)}) collective-permute-start(bf16[128,512]{1,0:T(8,128)(2,1)S(1)} %dynamic-slice_bitcast_fusion.3), channel_id=1, source_target_pairs={{0,2},{1,3},{2,4},{3,5},{4,6},{5,7},{6,0},{7,1},{8,10},{9,11},{10,... | collective-permute-start | bytes 393224 | tf_op jit(solution)/shard_map/ppermute | solution.py:641
  4.4 1.9 %collective-permute-start.3 = (bf16[128,512]{1,0:T(8,128)(2,1)S(1)}, bf16[128,512]{1,0:T(8,128)(2,1)S(1)}, u32[]{:S(2)}, u32[]{:S(2)}) collective-permute-start(bf16[128,512]{1,0:T(8,128)(2,1)S(1)} %dynamic-slice_bitcast_fusion.3), channel_id=1, source_target_pairs={{0,6},{1,7},{2,0},{3,1},{4,2},{5,3},{6,4},{7,5},{8,14},{9,15},{10,... | collective-permute-start | bytes 393224 | tf_op jit(solution)/shard_map/ppermute | solution.py:641
  8.4 7.8 %fold_adjacency.1 = (bf16[512,2816]{1,0:T(8,128)(2,1)}, bf16[4,320,512]{2,1,0:T(8,128)(2,1)}) custom-call(s32[192]{0:T(256)} %bitcast.41, s32[192]{0:T(256)} %bitcast.36, s32[192]{0:T(256)} %bitcast.38, s32[1]{0:T(128)} %bitcast.26.live, s32[8]{0:T(128)} %bitcast.31, s32[1]{0:T(128)} %bitcast.2.core, bf16[192,128,128]{2,1,0:T(8,128)(2,1)} %bitcast.39, ...), custom_call_target="tpu_custom_call" | custom-call | flops 8000000000 | bytes 8000000 | tf_op jit(solution)/shard_map/fold_adjacency/pallas_call | solution.py:112
  16.2 2.3 %gather_fusion = f32[512,512]{1,0:T(8,128)} fusion(f32[900,512]{1,0:T(8,128)S(1)} %copy-done, s32[1024]{0:T(1024)S(1)} %pad_clamp_fusion), kind=kCustom, calls=%fused_computation | custom fusion | bytes 2099200 | tf_op jit(solution)/shard_map/jit(_take)/gather | solution.py:767
  20.2 2.3 %broadcast_select_fusion.rel_ref = f32[512,512]{1,0:T(8,128)} fusion(f32[512,512]{1,0:T(8,128)} %gather_fusion, pred[512]{0:T(512)(128)(4,1)S(1)} %get-tuple-element.152), kind=kLoop, calls=%fused_computation.2 | loop fusion | flops 262144 | bytes 2097664 | tf_op jit(solution)/shard_map/jit(_take)/select_n | solution.py:767
  24.2 6.0 %collective-permute-done.5.refs_3_.refs_19_ = bf16[384,512]{1,0:T(8,128)(2,1)S(1)} collective-permute-done((bf16[384,512]{1,0:T(8,128)(2,1)S(1)}, bf16[384,512]{1,0:T(8,128)(2,1)S(1)}, u32[]{:S(2)}, u32[]{:S(2)}) %collective-permute-start.5) | collective-permute-done | bytes 393248 | tf_op jit(solution)/shard_map/ppermute | solution.py:649
  38.0 2.1 %collective-permute-done.6.refs_4_.refs_20_ = bf16[128,512]{1,0:T(8,128)(2,1)} collective-permute-done((bf16[128,512]{1,0:T(8,128)(2,1)}, bf16[128,512]{1,0:T(8,128)(2,1)}, u32[]{:S(2)}, u32[]{:S(2)}) %collective-permute-start.6) | collective-permute-done | bytes 131104 | tf_op jit(solution)/shard_map/ppermute | solution.py:649
  40.8 2.7 %pick_mirrors.1 = (bf16[512,512]{1,0:T(8,128)(2,1)S(1)}, bf16[512,512]{1,0:T(8,128)(2,1)S(1)}) custom-call(s32[1]{0:T(128)} %bitcast.plane, s32[1]{0:T(128)} %bitcast.1.grp, s32[1]{0:T(128)} %bitcast.2.core, s32[8]{0:T(128)S(1)} %bitcast.32, s32[8]{0:T(128)} %collective-permute-done.theirs, bf16[512,512]{1,0:T(8,128)(2,1)S(1)} %bitcast.28, ...), custom_call_target="tpu_custom_call" | custom-call | tf_op jit(solution)/shard_map/pick_mirrors/pallas_call | solution.py:175
  43.5 1.9 %collective-permute-done.8.theirs_ref = bf16[512,512]{1,0:T(8,128)(2,1)S(1)} collective-permute-done((bf16[512,512]{1,0:T(8,128)(2,1)S(1)}, bf16[512,512]{1,0:T(8,128)(2,1)S(1)}, u32[]{:S(2)}, u32[]{:S(2)}) %collective-permute-start.8) | collective-permute-done | bytes 524320 | tf_op jit(solution)/shard_map/ppermute | solution.py:645
  45.4 1.8 %copy-done.2 = bf16[512,2816]{1,0:T(8,128)(2,1)S(1)} copy-done((bf16[512,2816]{1,0:T(8,128)(2,1)S(1)}, bf16[512,2816]{1,0:T(8,128)(2,1)}, u32[]{:S(2)}) %copy-start.2) | copy-done | bytes 2883608
  47.2 1.9 %forward_partial.1 = (f32[128,512]{1,0:T(8,128)S(1)}, bf16[128,512]{1,0:T(8,128)(2,1)S(1)}, bf16[128,512]{1,0:T(8,128)(2,1)S(1)}, bf16[128,512]{1,0:T(8,128)(2,1)S(1)}) custom-call(s32[1]{0:T(128)} %bitcast.2.core, s32[1]{0:T(128)} %bitcast.1.grp, bf16[512,512]{1,0:T(8,128)(2,1)S(1)} %get-tuple-element.88.mine_ref, ...), custom_call_target="tpu_custom_call" | custom-call | tf_op jit(solution)/shard_map/forward_partial/pallas_call | solution.py:242
  50.3 2.1 %collective-permute-start.11 = (bf16[128,512]{1,0:T(8,128)(2,1)S(1)}, bf16[128,512]{1,0:T(8,128)(2,1)S(1)}, u32[]{:S(2)}, u32[]{:S(2)}) collective-permute-start(bf16[128,512]{1,0:T(8,128)(2,1)S(1)} %get-tuple-element.94), channel_id=1, source_target_pairs={{0,24},{8,16},{16,8},{24,0},{1,25},{9,17},{17,9},{25,1},{2,26},{10... | collective-permute-start | bytes 393224 | tf_op jit(solution)/shard_map/ppermute | solution.py:649
  52.7 4.8 %collective-permute-done.10.refs_2_ = bf16[128,512]{1,0:T(8,128)(2,1)S(1)} collective-permute-done((bf16[128,512]{1,0:T(8,128)(2,1)S(1)}, bf16[128,512]{1,0:T(8,128)(2,1)S(1)}, u32[]{:S(2)}, u32[]{:S(2)}) %collective-permute-start.10) | collective-permute-done | bytes 131104 | tf_op jit(solution)/shard_map/ppermute | solution.py:649
  59.5 3.1 %collective-permute-start.19 = (bf16[128,512]{1,0:T(8,128)(2,1)S(1)}, bf16[128,512]{1,0:T(8,128)(2,1)S(1)}, u32[]{:S(2)}, u32[]{:S(2)}) collective-permute-start(bf16[128,512]{1,0:T(8,128)(2,1)S(1)} %join_group.2.refs_0_), channel_id=1, source_target_pairs={{0,4},{1,5},{2,6},{3,7},{4,0},{5,1},{6,2},{7,3},{8,12},{9,13},{10,... | collective-permute-start | bytes 393224 | tf_op jit(solution)/shard_map/ppermute | solution.py:641
  63.3 1.8 %collective-permute-start.12 = (bf16[128,512]{1,0:T(8,128)(2,1)S(1)}, bf16[128,512]{1,0:T(8,128)(2,1)S(1)}, u32[]{:S(2)}, u32[]{:S(2)}) collective-permute-start(bf16[128,512]{1,0:T(8,128)(2,1)S(1)} %join_group.2.refs_0_), channel_id=1, source_target_pairs={{0,8},{8,0},{16,24},{24,16},{1,9},{9,1},{17,25},{25,17},{2,10},{10... | collective-permute-start | bytes 393224 | tf_op jit(solution)/shard_map/ppermute | solution.py:649
  65.1 3.3 %collective-permute-done.15.refs_4_ = bf16[128,512]{1,0:T(8,128)(2,1)S(1)} collective-permute-done((bf16[128,512]{1,0:T(8,128)(2,1)S(1)}, bf16[128,512]{1,0:T(8,128)(2,1)S(1)}, u32[]{:S(2)}, u32[]{:S(2)}) %collective-permute-start.15) | collective-permute-done | bytes 131104 | tf_op jit(solution)/shard_map/ppermute | solution.py:641
  68.4 2.0 %collective-permute-done.19.refs_8_ = bf16[128,512]{1,0:T(8,128)(2,1)S(1)} collective-permute-done((bf16[128,512]{1,0:T(8,128)(2,1)S(1)}, bf16[128,512]{1,0:T(8,128)(2,1)S(1)}, u32[]{:S(2)}, u32[]{:S(2)}) %collective-permute-start.19) | collective-permute-done | bytes 131104 | tf_op jit(solution)/shard_map/ppermute | solution.py:641
  71.0 2.0 %collective-permute-done.23.refs_12_ = bf16[128,512]{1,0:T(8,128)(2,1)S(1)} collective-permute-done((bf16[128,512]{1,0:T(8,128)(2,1)S(1)}, bf16[128,512]{1,0:T(8,128)(2,1)S(1)}, u32[]{:S(2)}, u32[]{:S(2)}) %collective-permute-start.23) | collective-permute-done | bytes 131104 | tf_op jit(solution)/shard_map/ppermute | solution.py:641
  73.0 1.8 %collective-permute-start.24 = (bf16[128,512]{1,0:T(8,128)(2,1)S(1)}, bf16[128,512]{1,0:T(8,128)(2,1)S(1)}, u32[]{:S(2)}, u32[]{:S(2)}) collective-permute-start(bf16[128,512]{1,0:T(8,128)(2,1)S(1)} %collective-permute-done.23.refs_12_), channel_id=1, source_target_pairs={{0,8},{8,0},{16,24},{24,16},{1,9},{9,1},{17,25},{25,17},{2,10},{10... | collective-permute-start | bytes 393224 | tf_op jit(solution)/shard_map/ppermute | solution.py:649
  80.5 1.7 %collective-permute-done.14.refs_3_ = bf16[128,512]{1,0:T(8,128)(2,1)S(1)} collective-permute-done((bf16[128,512]{1,0:T(8,128)(2,1)S(1)}, bf16[128,512]{1,0:T(8,128)(2,1)S(1)}, u32[]{:S(2)}, u32[]{:S(2)}) %collective-permute-start.14) | collective-permute-done | bytes 131104 | tf_op jit(solution)/shard_map/ppermute | solution.py:649
  82.2 1.9 %collective-permute-start.22 = (bf16[128,512]{1,0:T(8,128)(2,1)S(1)}, bf16[128,512]{1,0:T(8,128)(2,1)S(1)}, u32[]{:S(2)}, u32[]{:S(2)}) collective-permute-start(bf16[128,512]{1,0:T(8,128)(2,1)S(1)} %collective-permute-done.21.refs_10_), channel_id=1, source_target_pairs={{0,8},{8,0},{16,24},{24,16},{1,9},{9,1},{17,25},{25,17},{2,10},{10... | collective-permute-start | bytes 393224 | tf_op jit(solution)/shard_map/ppermute | solution.py:649
  84.9 1.9 %collective-permute-done.18.refs_7_ = bf16[128,512]{1,0:T(8,128)(2,1)S(1)} collective-permute-done((bf16[128,512]{1,0:T(8,128)(2,1)S(1)}, bf16[128,512]{1,0:T(8,128)(2,1)S(1)}, u32[]{:S(2)}, u32[]{:S(2)}) %collective-permute-start.18) | collective-permute-done | bytes 131104 | tf_op jit(solution)/shard_map/ppermute | solution.py:649
  89.2 7.6 %activate.1 = (bf16[2048,512]{1,0:T(8,128)(2,1)}, bf16[2048,512]{1,0:T(8,128)(2,1)}, bf16[2048,512]{1,0:T(8,128)(2,1)}, bf16[2048,512]{1,0:T(8,128)(2,1)}, bf16[128,512]{1,0:T(8,128)(2,1)}) custom-call(s32[1]{0:T(128)} %bitcast.plane, s32[1]{0:T(128)} %bitcast.1.grp, bf16[512,512]{1,0:T(8,128)(2,1)} %refs_0_.1, bf16[512,512]{1,0:T(8,128)(2,1)} %refs_1_.1, ...), custom_call_target="tpu_custom_call" | custom-call | tf_op jit(solution)/shard_map/activate/pallas_call | solution.py:304
  98.2 2.1 %collective-permute-start.29 = (bf16[320,512]{1,0:T(8,128)(2,1)S(1)}, bf16[320,512]{1,0:T(8,128)(2,1)S(1)}, u32[]{:S(2)}, u32[]{:S(2)}) collective-permute-start(bf16[320,512]{1,0:T(8,128)(2,1)S(1)} %get-tuple-element.155), channel_id=1, source_target_pairs={{0,4},{1,5},{2,6},{3,7},{4,0},{5,1},{6,2},{7,3},{8,12},{9,13},{10,... | collective-permute-start | bytes 983048 | tf_op jit(solution)/shard_map/ppermute | solution.py:641
  103.0 18.7 %score.1 = (bf16[4096,512]{1,0:T(8,128)(2,1)S(1)}, bf16[512,512]{1,0:T(8,128)(2,1)S(1)}, bf16[512,512]{1,0:T(8,128)(2,1)S(1)}, f32[1,512]{1,0:T(1,128)S(1)}, bf16[2048,512]{1,0:T(8,128)(2,1)S(1)}) custom-call(bf16[2048,512]{1,0:T(8,128)(2,1)S(1)} %copy-done.6, bf16[2048,512]{1,0:T(8,128)(2,1)} %collective-permute-done.27.other_ref, ...), custom_call_target="tpu_custom_call" | custom-call | flops 60000002048 | bytes 60000000 | tf_op jit(solution)/shard_map/score/pallas_call | solution.py:425
  121.7 5.5 %collective-permute-done.29.refs_4_.refs_6_ = bf16[320,512]{1,0:T(8,128)(2,1)S(1)} collective-permute-done((bf16[320,512]{1,0:T(8,128)(2,1)S(1)}, bf16[320,512]{1,0:T(8,128)(2,1)S(1)}, u32[]{:S(2)}, u32[]{:S(2)}) %collective-permute-start.29) | collective-permute-done | bytes 327712 | tf_op jit(solution)/shard_map/ppermute | solution.py:641
  127.1 2.4 %collective-permute-done.30.refs_5_.refs_7_ = bf16[320,512]{1,0:T(8,128)(2,1)S(1)} collective-permute-done((bf16[320,512]{1,0:T(8,128)(2,1)S(1)}, bf16[320,512]{1,0:T(8,128)(2,1)S(1)}, u32[]{:S(2)}, u32[]{:S(2)}) %collective-permute-start.30) | collective-permute-done | bytes 327712 | tf_op jit(solution)/shard_map/ppermute | solution.py:641
  129.6 3.5 %rows_own.1.own_ref = bf16[2048,512]{1,0:T(8,128)(2,1)S(1)} custom-call(bf16[4096,512]{1,0:T(8,128)(2,1)S(1)} %get-tuple-element.123.gs_ref, bf16[512,512]{1,0:T(8,128)(2,1)S(1)} %get-tuple-element.124.qb_ref, bf16[512,512]{1,0:T(8,128)(2,1)S(1)} %get-tuple-element.125.qg_ref, s32[16,512]{1,0:T(8,128)S(1)} %copy-done.13, bf16[2048,512]{1,0:T(8,128)(2,1)S(1)} %copy-done.6), custom_call_target="tpu_custom_call" | custom-call | tf_op jit(solution)/shard_map/rows_own/pallas_call | solution.py:467
  133.7 4.8 %backward_rows.1 = (bf16[2048,512]{1,0:T(8,128)(2,1)S(1)}, bf16[2048,512]{1,0:T(8,128)(2,1)S(1)}, f32[512,512]{1,0:T(8,128)S(1)}, bf16[512,512]{1,0:T(8,128)(2,1)S(1)}, f32[128,512]{1,0:T(8,128)S(1)}) custom-call(s32[1]{0:T(128)} %bitcast.plane, s32[1]{0:T(128)} %bitcast.1.grp, bf16[2048,512]{1,0:T(8,128)(2,1)S(1)} %rows_own.1.own_ref, ...), custom_call_target="tpu_custom_call" | custom-call | flops 6000000000 | bytes 6000000 | tf_op jit(solution)/shard_map/backward_rows/pallas_call | solution.py:531
  140.5 6.5 %sums_of_half.1 = (bf16[1280,512]{1,0:T(8,128)(2,1)S(1)}, f32[2,512]{1,0:T(2,128)S(1)}, f32[128,512]{1,0:T(8,128)S(1)}, bf16[128,512]{1,0:T(8,128)(2,1)S(1)}, bf...) custom-call(s32[1]{0:T(128)} %bitcast.plane, s32[1]{0:T(128)} %bitcast.1.grp, s32[1]{0:T(128)} %bitcast.2.core, ...), custom_call_target="tpu_custom_call" | custom-call | flops 20000000000 | bytes 20000000 | tf_op jit(solution)/shard_map/sums_of_half/pallas_call | solution.py:618
  151.3 1.6 %total_sums.1 = (f32[512,512]{1,0:T(8,128)}, f32[512,512]{1,0:T(8,128)}, f32[225,512]{1,0:T(8,128)}) custom-call(bf16[1280,512]{1,0:T(8,128)(2,1)S(1)} %get-tuple-element.140.a_ref, bf16[1280,512]{1,0:T(8,128)(2,1)S(1)} %collective-permute-done.34.b_ref), custom_call_target="tpu_custom_call" | custom-call | tf_op jit(solution)/shard_map/total_sums/pallas_call | solution.py:663
  153.5 1.8 %collective-permute-done.36.refs_3_ = bf16[128,512]{1,0:T(8,128)(2,1)S(1)} collective-permute-done((bf16[128,512]{1,0:T(8,128)(2,1)S(1)}, bf16[128,512]{1,0:T(8,128)(2,1)S(1)}, u32[]{:S(2)}, u32[]{:S(2)}) %collective-permute-start.36) | collective-permute-done | bytes 131104 | tf_op jit(solution)/shard_map/ppermute | solution.py:649
  (148 shorter events, 42.8 us)
Async XLA Ops:
  1.7 16.9 %collective-permute-start.1 = (bf16[128,512]{1,0:T(8,128)(2,1)S(1)}, bf16[128,512]{1,0:T(8,128)(2,1)S(1)}, u32[]{:S(2)}, u32[]{:S(2)}) collective-permute-start(bf16[128,512]{1,0:T(8,128)(2,1)S(1)} %dynamic-slice_bitcast_fusion.3), channel_id=1, source_target_pairs={{0,2},{1,3},{2,4},{3,5},{4,6},{5,7},{6,0},{7,1},{8,10},{9,11},{10,... | collective-permute-start | bytes 393224 | tf_op jit(solution)/shard_map/ppermute | solution.py:641
  3.3 15.2 %collective-permute-start.2 = (bf16[128,512]{1,0:T(8,128)(2,1)S(1)}, bf16[128,512]{1,0:T(8,128)(2,1)S(1)}, u32[]{:S(2)}, u32[]{:S(2)}) collective-permute-start(bf16[128,512]{1,0:T(8,128)(2,1)S(1)} %dynamic-slice_bitcast_fusion.3), channel_id=1, source_target_pairs={{0,4},{1,5},{2,6},{3,7},{4,0},{5,1},{6,2},{7,3},{8,12},{9,13},{10,... | collective-permute-start | bytes 393224 | tf_op jit(solution)/shard_map/ppermute | solution.py:641
  4.4 14.2 %collective-permute-start.3 = (bf16[128,512]{1,0:T(8,128)(2,1)S(1)}, bf16[128,512]{1,0:T(8,128)(2,1)S(1)}, u32[]{:S(2)}, u32[]{:S(2)}) collective-permute-start(bf16[128,512]{1,0:T(8,128)(2,1)S(1)} %dynamic-slice_bitcast_fusion.3), channel_id=1, source_target_pairs={{0,6},{1,7},{2,0},{3,1},{4,2},{5,3},{6,4},{7,5},{8,14},{9,15},{10,... | collective-permute-start | bytes 393224 | tf_op jit(solution)/shard_map/ppermute | solution.py:641
  6.4 33.7 %collective-permute-start = (s32[8]{0:T(128)}, s32[8]{0:T(128)}, u32[]{:S(2)}, u32[]{:S(2)}) collective-permute-start(s32[8]{0:T(128)} %bitcast.30), channel_id=1, source_target_pairs={{0,1},{1,0},{2,3},{3,2},{4,5},{5,4},{6,7},{7,6},{8,9},{9,8},{10,11... | collective-permute-start | bytes 104 | tf_op jit(solution)/shard_map/ppermute | solution.py:645
  18.6 11.6 %collective-permute-start.5 = (bf16[384,512]{1,0:T(8,128)(2,1)S(1)}, bf16[384,512]{1,0:T(8,128)(2,1)S(1)}, u32[]{:S(2)}, u32[]{:S(2)}) collective-permute-start(bf16[384,512]{1,0:T(8,128)(2,1)S(1)} %pad_maximum_fusion.refs_1_.refs_17_), channel_id=1, source_target_pairs={{0,16},{8,24},{16,0},{24,8},{1,17},{9,25},{17,1},{25,9},{2,18},{10... | collective-permute-start | bytes 1179656 | tf_op jit(solution)/shard_map/ppermute | solution.py:649
  22.5 11.6 %collective-permute-start.4 = (bf16[384,512]{1,0:T(8,128)(2,1)S(1)}, bf16[384,512]{1,0:T(8,128)(2,1)S(1)}, u32[]{:S(2)}, u32[]{:S(2)}) collective-permute-start(bf16[384,512]{1,0:T(8,128)(2,1)S(1)} %pad_maximum_fusion.refs_1_.refs_17_), channel_id=1, source_target_pairs={{0,8},{8,0},{16,24},{24,16},{1,9},{9,1},{17,25},{25,17},{2,10},{10... | collective-permute-start | bytes 1179656 | tf_op jit(solution)/shard_map/ppermute | solution.py:649
  31.0 9.1 %collective-permute-start.7 = (bf16[256,512]{1,0:T(8,128)(2,1)}, bf16[256,512]{1,0:T(8,128)(2,1)}, u32[]{:S(2)}, u32[]{:S(2)}) collective-permute-start(bf16[256,512]{1,0:T(8,128)(2,1)} %slice.11), channel_id=1, source_target_pairs={{0,8},{8,0},{16,24},{24,16},{1,9},{9,1},{17,25},{25,17},{2,10},{10... | collective-permute-start | bytes 786440 | tf_op jit(solution)/shard_map/ppermute | solution.py:649
  34.8 5.3 %collective-permute-start.6 = (bf16[128,512]{1,0:T(8,128)(2,1)}, bf16[128,512]{1,0:T(8,128)(2,1)}, u32[]{:S(2)}, u32[]{:S(2)}) collective-permute-start(bf16[128,512]{1,0:T(8,128)(2,1)} %slice.10), channel_id=1, source_target_pairs={{0,16},{8,24},{16,0},{24,8},{1,17},{9,25},{17,1},{25,9},{2,18},{10... | collective-permute-start | bytes 393224 | tf_op jit(solution)/shard_map/ppermute | solution.py:649
  49.1 8.3 %collective-permute-start.10 = (bf16[128,512]{1,0:T(8,128)(2,1)S(1)}, bf16[128,512]{1,0:T(8,128)(2,1)S(1)}, u32[]{:S(2)}, u32[]{:S(2)}) collective-permute-start(bf16[128,512]{1,0:T(8,128)(2,1)S(1)} %get-tuple-element.93), channel_id=1, source_target_pairs={{0,16},{8,24},{16,0},{24,8},{1,17},{9,25},{17,1},{25,9},{2,18},{10... | collective-permute-start | bytes 393224 | tf_op jit(solution)/shard_map/ppermute | solution.py:649
  50.3 7.3 %collective-permute-start.11 = (bf16[128,512]{1,0:T(8,128)(2,1)S(1)}, bf16[128,512]{1,0:T(8,128)(2,1)S(1)}, u32[]{:S(2)}, u32[]{:S(2)}) collective-permute-start(bf16[128,512]{1,0:T(8,128)(2,1)S(1)} %get-tuple-element.94), channel_id=1, source_target_pairs={{0,24},{8,16},{16,8},{24,0},{1,25},{9,17},{17,9},{25,1},{2,26},{10... | collective-permute-start | bytes 393224 | tf_op jit(solution)/shard_map/ppermute | solution.py:649
  52.4 6.3 %collective-permute-start.9 = (bf16[128,512]{1,0:T(8,128)(2,1)S(1)}, bf16[128,512]{1,0:T(8,128)(2,1)S(1)}, u32[]{:S(2)}, u32[]{:S(2)}) collective-permute-start(bf16[128,512]{1,0:T(8,128)(2,1)S(1)} %get-tuple-element.92), channel_id=1, source_target_pairs={{0,8},{8,0},{16,24},{24,16},{1,9},{9,1},{17,25},{25,17},{2,10},{10... | collective-permute-start | bytes 393224 | tf_op jit(solution)/shard_map/ppermute | solution.py:649
  58.8 9.5 %collective-permute-start.15 = (bf16[128,512]{1,0:T(8,128)(2,1)S(1)}, bf16[128,512]{1,0:T(8,128)(2,1)S(1)}, u32[]{:S(2)}, u32[]{:S(2)}) collective-permute-start(bf16[128,512]{1,0:T(8,128)(2,1)S(1)} %join_group.2.refs_0_), channel_id=1, source_target_pairs={{0,2},{1,3},{2,4},{3,5},{4,6},{5,7},{6,0},{7,1},{8,10},{9,11},{10,... | collective-permute-start | bytes 393224 | tf_op jit(solution)/shard_map/ppermute | solution.py:641
  59.5 10.9 %collective-permute-start.19 = (bf16[128,512]{1,0:T(8,128)(2,1)S(1)}, bf16[128,512]{1,0:T(8,128)(2,1)S(1)}, u32[]{:S(2)}, u32[]{:S(2)}) collective-permute-start(bf16[128,512]{1,0:T(8,128)(2,1)S(1)} %join_group.2.refs_0_), channel_id=1, source_target_pairs={{0,4},{1,5},{2,6},{3,7},{4,0},{5,1},{6,2},{7,3},{8,12},{9,13},{10,... | collective-permute-start | bytes 393224 | tf_op jit(solution)/shard_map/ppermute | solution.py:641
  62.6 10.4 %collective-permute-start.23 = (bf16[128,512]{1,0:T(8,128)(2,1)S(1)}, bf16[128,512]{1,0:T(8,128)(2,1)S(1)}, u32[]{:S(2)}, u32[]{:S(2)}) collective-permute-start(bf16[128,512]{1,0:T(8,128)(2,1)S(1)} %join_group.2.refs_0_), channel_id=1, source_target_pairs={{0,6},{1,7},{2,0},{3,1},{4,2},{5,3},{6,4},{7,5},{8,14},{9,15},{10,... | collective-permute-start | bytes 393224 | tf_op jit(solution)/shard_map/ppermute | solution.py:641
  62.6 12.2 %collective-permute-start.13 = (bf16[128,512]{1,0:T(8,128)(2,1)S(1)}, bf16[128,512]{1,0:T(8,128)(2,1)S(1)}, u32[]{:S(2)}, u32[]{:S(2)}) collective-permute-start(bf16[128,512]{1,0:T(8,128)(2,1)S(1)} %join_group.2.refs_0_), channel_id=1, source_target_pairs={{0,16},{8,24},{16,0},{24,8},{1,17},{9,25},{17,1},{25,9},{2,18},{10... | collective-permute-start | bytes 393224 | tf_op jit(solution)/shard_map/ppermute | solution.py:649
  63.3 11.7 %collective-permute-start.12 = (bf16[128,512]{1,0:T(8,128)(2,1)S(1)}, bf16[128,512]{1,0:T(8,128)(2,1)S(1)}, u32[]{:S(2)}, u32[]{:S(2)}) collective-permute-start(bf16[128,512]{1,0:T(8,128)(2,1)S(1)} %join_group.2.refs_0_), channel_id=1, source_target_pairs={{0,8},{8,0},{16,24},{24,16},{1,9},{9,1},{17,25},{25,17},{2,10},{10... | collective-permute-start | bytes 393224 | tf_op jit(solution)/shard_map/ppermute | solution.py:649
  68.4 7.8 %collective-permute-start.16 = (bf16[128,512]{1,0:T(8,128)(2,1)S(1)}, bf16[128,512]{1,0:T(8,128)(2,1)S(1)}, u32[]{:S(2)}, u32[]{:S(2)}) collective-permute-start(bf16[128,512]{1,0:T(8,128)(2,1)S(1)} %collective-permute-done.15.refs_4_), channel_id=1, source_target_pairs={{0,8},{8,0},{16,24},{24,16},{1,9},{9,1},{17,25},{25,17},{2,10},{10... | collective-permute-start | bytes 393224 | tf_op jit(solution)/shard_map/ppermute | solution.py:649
  70.4 7.1 %collective-permute-start.21 = (bf16[128,512]{1,0:T(8,128)(2,1)S(1)}, bf16[128,512]{1,0:T(8,128)(2,1)S(1)}, u32[]{:S(2)}, u32[]{:S(2)}) collective-permute-start(bf16[128,512]{1,0:T(8,128)(2,1)S(1)} %collective-permute-done.19.refs_8_), channel_id=1, source_target_pairs={{0,16},{8,24},{16,0},{24,8},{1,17},{9,25},{17,1},{25,9},{2,18},{10... | collective-permute-start | bytes 393224 | tf_op jit(solution)/shard_map/ppermute | solution.py:649
  73.0 6.4 %collective-permute-start.24 = (bf16[128,512]{1,0:T(8,128)(2,1)S(1)}, bf16[128,512]{1,0:T(8,128)(2,1)S(1)}, u32[]{:S(2)}, u32[]{:S(2)}) collective-permute-start(bf16[128,512]{1,0:T(8,128)(2,1)S(1)} %collective-permute-done.23.refs_12_), channel_id=1, source_target_pairs={{0,8},{8,0},{16,24},{24,16},{1,9},{9,1},{17,25},{25,17},{2,10},{10... | collective-permute-start | bytes 393224 | tf_op jit(solution)/shard_map/ppermute | solution.py:649
  74.8 7.4 %collective-permute-start.14 = (bf16[128,512]{1,0:T(8,128)(2,1)S(1)}, bf16[128,512]{1,0:T(8,128)(2,1)S(1)}, u32[]{:S(2)}, u32[]{:S(2)}) collective-permute-start(bf16[128,512]{1,0:T(8,128)(2,1)S(1)} %collective-permute-done.13.refs_2_), channel_id=1, source_target_pairs={{0,8},{8,0},{16,24},{24,16},{1,9},{9,1},{17,25},{25,17},{2,10},{10... | collective-permute-start | bytes 393224 | tf_op jit(solution)/shard_map/ppermute | solution.py:649
  75.0 9.0 %collective-permute-start.17 = (bf16[128,512]{1,0:T(8,128)(2,1)S(1)}, bf16[128,512]{1,0:T(8,128)(2,1)S(1)}, u32[]{:S(2)}, u32[]{:S(2)}) collective-permute-start(bf16[128,512]{1,0:T(8,128)(2,1)S(1)} %collective-permute-done.15.refs_4_), channel_id=1, source_target_pairs={{0,16},{8,24},{16,0},{24,8},{1,17},{9,25},{17,1},{25,9},{2,18},{10... | collective-permute-start | bytes 393224 | tf_op jit(solution)/shard_map/ppermute | solution.py:649
  76.1 8.8 %collective-permute-start.20 = (bf16[128,512]{1,0:T(8,128)(2,1)S(1)}, bf16[128,512]{1,0:T(8,128)(2,1)S(1)}, u32[]{:S(2)}, u32[]{:S(2)}) collective-permute-start(bf16[128,512]{1,0:T(8,128)(2,1)S(1)} %collective-permute-done.19.refs_8_), channel_id=1, source_target_pairs={{0,8},{8,0},{16,24},{24,16},{1,9},{9,1},{17,25},{25,17},{2,10},{10... | collective-permute-start | bytes 393224 | tf_op jit(solution)/shard_map/ppermute | solution.py:649
  77.5 7.4 %collective-permute-start.25 = (bf16[128,512]{1,0:T(8,128)(2,1)S(1)}, bf16[128,512]{1,0:T(8,128)(2,1)S(1)}, u32[]{:S(2)}, u32[]{:S(2)}) collective-permute-start(bf16[128,512]{1,0:T(8,128)(2,1)S(1)} %collective-permute-done.23.refs_12_), channel_id=1, source_target_pairs={{0,16},{8,24},{16,0},{24,8},{1,17},{9,25},{17,1},{25,9},{2,18},{10... | collective-permute-start | bytes 393224 | tf_op jit(solution)/shard_map/ppermute | solution.py:649
  79.4 7.4 %collective-permute-start.18 = (bf16[128,512]{1,0:T(8,128)(2,1)S(1)}, bf16[128,512]{1,0:T(8,128)(2,1)S(1)}, u32[]{:S(2)}, u32[]{:S(2)}) collective-permute-start(bf16[128,512]{1,0:T(8,128)(2,1)S(1)} %collective-permute-done.16.refs_5_), channel_id=1, source_target_pairs={{0,16},{8,24},{16,0},{24,8},{1,17},{9,25},{17,1},{25,9},{2,18},{10... | collective-permute-start | bytes 393224 | tf_op jit(solution)/shard_map/ppermute | solution.py:649
  82.2 5.0 %collective-permute-start.22 = (bf16[128,512]{1,0:T(8,128)(2,1)S(1)}, bf16[128,512]{1,0:T(8,128)(2,1)S(1)}, u32[]{:S(2)}, u32[]{:S(2)}) collective-permute-start(bf16[128,512]{1,0:T(8,128)(2,1)S(1)} %collective-permute-done.21.refs_10_), channel_id=1, source_target_pairs={{0,8},{8,0},{16,24},{24,16},{1,9},{9,1},{17,25},{25,17},{2,10},{10... | collective-permute-start | bytes 393224 | tf_op jit(solution)/shard_map/ppermute | solution.py:649
  84.0 5.1 %collective-permute-start.26 = (bf16[128,512]{1,0:T(8,128)(2,1)S(1)}, bf16[128,512]{1,0:T(8,128)(2,1)}, u32[]{:S(2)}, u32[]{:S(2)}) collective-permute-start(bf16[128,512]{1,0:T(8,128)(2,1)S(1)} %collective-permute-done.24.refs_13_), channel_id=1, source_target_pairs={{0,16},{8,24},{16,0},{24,8},{1,17},{9,25},{17,1},{25,9},{2,18},{10... | collective-permute-start | bytes 393224 | tf_op jit(solution)/shard_map/ppermute | solution.py:649
  98.2 23.5 %collective-permute-start.28 = (bf16[320,512]{1,0:T(8,128)(2,1)S(1)}, bf16[320,512]{1,0:T(8,128)(2,1)S(1)}, u32[]{:S(2)}, u32[]{:S(2)}) collective-permute-start(bf16[320,512]{1,0:T(8,128)(2,1)S(1)} %get-tuple-element.156), channel_id=1, source_target_pairs={{0,2},{1,3},{2,4},{3,5},{4,6},{5,7},{6,0},{7,1},{8,10},{9,11},{10,... | collective-permute-start | bytes 983048 | tf_op jit(solution)/shard_map/ppermute | solution.py:641
  98.2 28.9 %collective-permute-start.29 = (bf16[320,512]{1,0:T(8,128)(2,1)S(1)}, bf16[320,512]{1,0:T(8,128)(2,1)S(1)}, u32[]{:S(2)}, u32[]{:S(2)}) collective-permute-start(bf16[320,512]{1,0:T(8,128)(2,1)S(1)} %get-tuple-element.155), channel_id=1, source_target_pairs={{0,4},{1,5},{2,6},{3,7},{4,0},{5,1},{6,2},{7,3},{8,12},{9,13},{10,... | collective-permute-start | bytes 983048 | tf_op jit(solution)/shard_map/ppermute | solution.py:641
  100.4 29.1 %collective-permute-start.30 = (bf16[320,512]{1,0:T(8,128)(2,1)S(1)}, bf16[320,512]{1,0:T(8,128)(2,1)S(1)}, u32[]{:S(2)}, u32[]{:S(2)}) collective-permute-start(bf16[320,512]{1,0:T(8,128)(2,1)S(1)} %get-tuple-element.154), channel_id=1, source_target_pairs={{0,6},{1,7},{2,0},{3,1},{4,2},{5,3},{6,4},{7,5},{8,14},{9,15},{10,... | collective-permute-start | bytes 983048 | tf_op jit(solution)/shard_map/ppermute | solution.py:641
  147.2 6.3 %collective-permute-start.35 = (bf16[128,512]{1,0:T(8,128)(2,1)S(1)}, bf16[128,512]{1,0:T(8,128)(2,1)S(1)}, u32[]{:S(2)}, u32[]{:S(2)}) collective-permute-start(bf16[128,512]{1,0:T(8,128)(2,1)S(1)} %get-tuple-element.146), channel_id=1, source_target_pairs={{0,8},{8,0},{16,24},{24,16},{1,9},{9,1},{17,25},{25,17},{2,10},{10... | collective-permute-start | bytes 393224 | tf_op jit(solution)/shard_map/ppermute | solution.py:649
  148.3 7.0 %collective-permute-start.36 = (bf16[128,512]{1,0:T(8,128)(2,1)S(1)}, bf16[128,512]{1,0:T(8,128)(2,1)S(1)}, u32[]{:S(2)}, u32[]{:S(2)}) collective-permute-start(bf16[128,512]{1,0:T(8,128)(2,1)S(1)} %get-tuple-element.147), channel_id=1, source_target_pairs={{0,16},{8,24},{16,0},{24,8},{1,17},{9,25},{17,1},{25,9},{2,18},{10... | collective-permute-start | bytes 393224 | tf_op jit(solution)/shard_map/ppermute | solution.py:649
  149.4 7.4 %collective-permute-start.37 = (bf16[128,512]{1,0:T(8,128)(2,1)S(1)}, bf16[128,512]{1,0:T(8,128)(2,1)S(1)}, u32[]{:S(2)}, u32[]{:S(2)}) collective-permute-start(bf16[128,512]{1,0:T(8,128)(2,1)S(1)} %get-tuple-element.148), channel_id=1, source_target_pairs={{0,24},{8,16},{16,8},{24,0},{1,25},{9,17},{17,9},{25,1},{2,26},{10... | collective-permute-start | bytes 393224 | tf_op jit(solution)/shard_map/ppermute | solution.py:649
  (43 other events, 493.3 us)
